TPU v7x, 128 devices: a whole 4x4x4 slice. The times are simulated.
128 devices in a mesh: row: 16 (over x_lo, z, core), col: 8 (over x_hi, y).
Axes of the slice: x: 4 (x_hi: 2, x_lo: 2; x = x_hi * 2 + x_lo), y: 4, z: 4, core: 2. Of those that a mesh axis runs over, the one named last changes fastest.
Arguments:
- hidden: bfloat16 [2048, 2560], P('row'), may hold values from -4 to 4
- rel_bins: int32 [2048, 2048], P('row', 'col'), may hold values from 0 to 64, as said below
- attn_gain: float32 [2560], replicated, may hold values from 0.25 to 1.75
- w_query: bfloat16 [2560, 2560], P(None, 'col'), may hold values from -0.25 to 0.25
- w_key: bfloat16 [2560, 2560], P(None, 'col'), may hold values from -0.25 to 0.25
- w_value: bfloat16 [2560, 2560], P(None, 'col'), may hold values from -0.125 to 0.125
- w_out: bfloat16 [2560, 2560], P('col'), may hold values from -0.125 to 0.125
- final_gain: float32 [2560], P('col'), may hold values from 0.25 to 1.75
- w_single: bfloat16 [2560, 1024], P('col'), may hold values from -0.125 to 0.125
- w_second: bfloat16 [1024, 1024], replicated, may hold values from -0.1875 to 0.1875
- w_left: bfloat16 [1024, 128], replicated, may hold values from -0.1875 to 0.1875
- w_right: bfloat16 [1024, 128], replicated, may hold values from -0.1875 to 0.1875
- rel_table: bfloat16 [65, 128], replicated, may hold values from -6 to 6
- pair_gain: float32 [128], replicated, may hold values from 0.25 to 1.75
- w_expand: bfloat16 [128, 512], replicated, may hold values from -0.5 to 0.5
- w_contract: bfloat16 [512, 128], replicated, may hold values from -0.25 to 0.25
Outputs:
- pair_rep: bfloat16 [2048, 2048, 128], P('row', 'col')
Inputs may be any that keep to these rules, and one draw needn't show every extreme that they name: rel_bins[i, j] is the difference of the residue numbers of j and i, clipped to plus or minus (64) // 2 and shifted by (64) // 2.
All inputs are finite; a program needn't handle non-finite values.
Results may differ from a plain program's by a relative error of at most 0.013.
Values may be sent and summed in bfloat16 or wider, within the bound.
No kernel may reach another device: no remote copies, remote signals or barrier semaphores. Data moves between devices by JAX's collectives and lax.ppermute only.
A program may use at most 128 MiB of HBM per device.

v0:
```python
import math

import jax
import jax.numpy as jnp
from jax import lax
from jax.sharding import PartitionSpec as P

HD = 64


epsilon = 1e-05


def layer_norm(values, gain):
    count = values.shape[-1]
    average = jnp.sum(values, -1, keepdims=True) / count
    variance = jnp.sum(values * values, -1, keepdims=True) / count - average * average
    return (values - average) * lax.rsqrt(variance + epsilon) * gain


def rotary(vectors, positions):
    half_size = vectors.shape[-1] // 2
    frequency = jnp.exp(
        jnp.arange(half_size, dtype=jnp.float32) * (-2.0 * math.log(10000.0) / vectors.shape[-1])
    )
    angles = positions.astype(jnp.float32)[:, None] * frequency[None, :]
    angles = jnp.concatenate([angles, angles], -1)[:, None, :]
    turned = jnp.concatenate([-vectors[..., half_size:], vectors[..., :half_size]], -1)
    return vectors * jnp.cos(angles) + turned * jnp.sin(angles)


def local(
    hidden,
    rel_bins,
    attn_gain,
    w_query,
    w_key,
    w_value,
    w_out,
    final_gain,
    w_single,
    w_second,
    w_left,
    w_right,
    rel_table,
    pair_gain,
    w_expand,
    w_contract,
):
    row_count = hidden.shape[0]
    model_width = hidden.shape[1]
    local_width = w_query.shape[1]
    local_heads = local_width // HD
    positions = lax.axis_index("row") * row_count + jnp.arange(row_count, dtype=jnp.int32)
    stream = hidden.astype(jnp.float32)
    attn_in = layer_norm(stream, attn_gain).astype(jnp.bfloat16)
    query = jnp.dot(attn_in, w_query, preferred_element_type=jnp.float32) * HD ** (-0.5)
    query = rotary(query.reshape(row_count, local_heads, HD), positions).astype(jnp.bfloat16)
    keys = jnp.dot(attn_in, w_key, preferred_element_type=jnp.float32)
    keys = rotary(keys.reshape(row_count, local_heads, HD), positions).astype(jnp.bfloat16)
    values = jnp.dot(attn_in, w_value, preferred_element_type=jnp.float32).astype(jnp.bfloat16)
    stacked = jnp.concatenate([keys.reshape(row_count, local_width), values], 1)
    incoming = lax.all_gather(stacked, "row", axis=0, tiled=True)
    key_block = incoming[:, :local_width].reshape(-1, local_heads, HD)
    value_block = incoming[:, local_width:].reshape(-1, local_heads, HD)
    scores = jnp.einsum("qhd,khd->hqk", query, key_block, preferred_element_type=jnp.float32)
    weights = jnp.exp(scores)
    totals = jnp.sum(weights, -1)
    numerator = jnp.einsum(
        "hqk,khd->hqd",
        weights.astype(jnp.bfloat16),
        value_block,
        preferred_element_type=jnp.float32,
    )
    numerator, totals = (numerator, totals)
    context = (numerator / totals[..., None]).astype(jnp.bfloat16)
    context = jnp.transpose(context, (1, 0, 2)).reshape(row_count, local_width)
    attn_part = jnp.dot(context, w_out, preferred_element_type=jnp.float32)
    shared = lax.psum_scatter(attn_part, "col", scatter_dimension=1, tiled=True)
    col_index = lax.axis_index("col")
    feature_count = w_single.shape[0]
    own_stream = lax.dynamic_slice_in_dim(stream, col_index * feature_count, feature_count, 1)
    resid = own_stream + shared
    sum_first, sum_second = lax.psum((jnp.sum(resid, -1), jnp.sum(resid * resid, -1)), "col")
    average = sum_first / model_width
    variance = sum_second / model_width - average * average
    final = (
        (resid - average[:, None]) * lax.rsqrt(variance[:, None] + epsilon) * final_gain
    ).astype(jnp.bfloat16)
    part_single = jnp.dot(final, w_single, preferred_element_type=jnp.float32)
    summed = lax.psum(part_single, "col")
    lifted = jnp.maximum(summed, 0.0).astype(jnp.bfloat16)
    single = jnp.dot(lifted, w_second, preferred_element_type=jnp.float32).astype(jnp.bfloat16)
    left = jnp.dot(single, w_left, preferred_element_type=jnp.float32).astype(jnp.bfloat16)
    right = jnp.dot(single, w_right, preferred_element_type=jnp.float32).astype(jnp.bfloat16)
    owner_count = lax.axis_size("row") // lax.axis_size("col")
    every_right = lax.all_gather(right, "row", axis=0, tiled=True)
    column_right = lax.dynamic_slice_in_dim(
        every_right, col_index * owner_count * row_count, owner_count * row_count, 0
    )
    col_count = column_right.shape[0]
    channels = column_right.shape[1]
    right_wide = column_right.astype(jnp.float32)
    left_wide = left.astype(jnp.float32)
    block_rows = math.gcd(row_count, 32)
    bin_codes = jnp.arange(rel_table.shape[0], dtype=jnp.int32)

    def pair_tile(entries):
        bin_block, left_block = entries
        one_hot = (bin_block[..., None] == bin_codes).astype(jnp.bfloat16)
        table_part = jnp.einsum(
            "ijb,bc->ijc", one_hot, rel_table, preferred_element_type=jnp.float32
        )
        pair_in = left_block[:, None, :] + right_wide[None, :, :] + table_part
        normed = layer_norm(pair_in, pair_gain).astype(jnp.bfloat16)
        flat = normed.reshape(-1, channels)
        expanded = jnp.maximum(
            jnp.dot(flat, w_expand, preferred_element_type=jnp.float32), 0.0
        ).astype(jnp.bfloat16)
        update = jnp.dot(expanded, w_contract, preferred_element_type=jnp.float32).reshape(
            pair_in.shape
        )
        return (pair_in + update).astype(jnp.bfloat16)

    pair_rep = lax.map(
        pair_tile,
        (
            rel_bins.reshape(row_count // block_rows, block_rows, col_count),
            left_wide.reshape(row_count // block_rows, block_rows, channels),
        ),
    )
    return pair_rep.reshape(row_count, col_count, channels)


def solution(mesh):
    in_specs = (
        P("row", None),
        P("row", "col"),
        P(),
        P(None, "col"),
        P(None, "col"),
        P(None, "col"),
        P("col", None),
        P("col"),
        P("col", None),
        P(),
        P(),
        P(),
        P(),
        P(),
        P(),
        P(),
    )
    out_specs = P("row", "col", None)
    return jax.shard_map(local, mesh=mesh, in_specs=in_specs, out_specs=out_specs, check_vma=False)
```

profile of v0, /device:TPU:1, one launch (start us, length us, event | category | flops | bytes accessed | tf_op | source)
XLA Modules:
  0.0 320.3 jit_solution(5461199882438731854)
XLA Ops:
  8.5 2.1 fusion.30
  13.8 2.1 convolution_multiply_fusion
  16.0 40.8 %all-gather.2.cloned.1.call-done = bf16[2048,640]{0,1:T(8,128)(2,1)} async-done(((bf16[128,640]{0,1:T(8,128)(2,1)}), bf16[2048,640]{0,1:T(8,128)(2,1)}) %all-gather.2.cloned.1.call-update) | async-done | bytes 2621456 | tf_op jit(solution)/shard_map/all_gather | solution.py:63
  64.3 70.5 %reduce-scatter.2.cloned.1.call-done = f32[128,320]{0,1:T(8,128)} async-done(((f32[128,2560]{0,1:T(8,128)}), f32[128,320]{0,1:T(8,128)}) %reduce-scatter.2.cloned.1.call-update) | async-done | bytes 163856 | tf_op jit(solution)/shard_map/reduce_scatter | solution.py:79
  135.9 18.1 %all-reduce = (f32[128]{0:T(128)S(1)}, f32[128]{0:T(128)S(1)}) all-reduce(f32[128]{0:T(128)S(1)} %get-tuple-element.83, f32[128]{0:T(128)S(1)} %get-tuple-element.82), channel_id=1, replica_groups=mesh['row'=16,'col'=8] {'col'}, use_global_device_ids=true, to_apply=%region_7.0 | all-reduce | flops 256 | bytes 2048 | tf_op jit(solution)/shard_map/psum | solution.py:84
  154.5 36.8 %all-reduce.2 = bf16[128,1024]{1,0:T(8,128)(2,1)S(1)} all-reduce(f32[128,1024]{1,0:T(8,128)S(1)} %fusion.18), channel_id=1, replica_groups=mesh['row'=16,'col'=8] {'col'}, use_global_device_ids=true, to_apply=%region_8.0 | all-reduce | flops 131072 | bytes 786432 | tf_op jit(solution)/shard_map/psum | solution.py:91
  192.0 33.5 %all_gather.7 = bf16[2048,128]{1,0:T(8,128)(2,1)S(1)} all-gather(bf16[128,128]{1,0:T(8,128)(2,1)S(1)} %convolution_convert_fusion.2), channel_id=1, replica_groups=mesh['row'=16,'col'=8] {'row'}, dimensions={0}, use_global_device_ids=true | all-gather | bytes 557056 | tf_op jit(solution)/shard_map/all_gather | solution.py:97
  225.8 87.6 %while.11 = (s32[]{:T(128)}, bf16[4,32,256,128]{3,2,1,0:T(8,128)(2,1)}, f32[4,32,128]{2,1,0:T(8,128)S(1)}, f32[256,128]{1,0:T(8,128)S(1)}, s32[4,32,256]{2,1,0:T...) while((s32[]{:T(128)}, ...), condition=%wide.region_12.13_spmd.clone, body=%wide.region_9.12_spmd.clone.sunk | while | flops 2308472832 | bytes 45155720 | solution.py:125
  226.6 3.4 %fusion.59 = (f32[32,256]{1,0:T(8,128)S(1)}, f32[32,256]{1,0:T(8,128)S(1)}, f32[32,256,128]{2,1,0:T(8,128)S(1)}) fusion(f32[256,128]{1,0:T(8,128)S(1)} %get-tuple-element.210, f32[32,128]{1,0:T(8,128)S(1)} %dynamic-slice_bitcast_fusion.4, bf16[65,128]{1,0:T(8,128)(2,1)S(1)} %get-tuple-element.212, s32[32,256]{1,0:T(8,128)S(1)} %dynamic-slice_bitcast_fusion.5), kind=kOutput, calls=%fused_computation.7.clone.1 | convolution fusion | flops 142073856 | bytes 4456704 | tf_op jit(solution)/shard_map/while/body/eval_jaxpr/ijb,bc->ijc/dot_general | solution.py:111
  230.0 3.9 %multiply_convert_fusion.8 = bf16[32,256,128]{2,1,0:T(8,128)(2,1)} fusion(f32[32,256,128]{2,1,0:T(8,128)S(1)} %get-tuple-element.182, f32[128]{0:T(128)S(1)} %get-tuple-element.213, f32[32,256]{1,0:T(8,128)S(1)} %get-tuple-element.185, f32[32,256]{1,0:T(8,128)S(1)} %get-tuple-element.186, f32[256,128]{1,0:T(8,128)S(1)} %get-tuple-element.210, ...), kind=kLoop, calls=%fused_computation.3.clone.1 | loop fusion | flops 6291456 | bytes 6504960 | tf_op jit(solution)/shard_map/while/body/eval_jaxpr/convert_element_type | solution.py:115
  233.9 8.1 %fusion.60 = f32[8192,128]{1,0:T(8,128)} fusion(bf16[512,128]{1,0:T(8,128)(2,1)S(1)} %get-tuple-element.215, bf16[8192,128]{1,0:T(8,128)(2,1)} %bitcast.74, bf16[128,512]{1,0:T(8,128)(2,1)S(1)} %get-tuple-element.214), kind=kOutput, calls=%fused_computation.6.clone.1 | convolution fusion | flops 2155872256 | bytes 6553600 | tf_op jit(solution)/shard_map/while/body/eval_jaxpr/dot_general | solution.py:120
  242.0 5.7 %fusion.61 = bf16[4,32,256,128]{3,2,1,0:T(8,128)(2,1)} fusion(bf16[4,32,256,128]{3,2,1,0:T(8,128)(2,1)} %get-tuple-element.198, s32[]{:T(128)} %get-tuple-element.197, f32[32,256,128]{2,1,0:T(8,128)} %bitcast.73, f32[32,256,128]{2,1,0:T(8,128)} %copy-done.1, f32[256,128]{1,0:T(8,128)S(1)} %get-tuple-element.210, ...), kind=kLoop, calls=%fused_computation.11.clone.1 | loop fusion | flops 4194304 | bytes 10633728 | tf_op jit(solution)/shard_map/while/body/jit(dynamic_update_index_in_dim)/dynamic_update_slice | solution.py:125
  248.5 3.4 %fusion.59 = (f32[32,256]{1,0:T(8,128)S(1)}, f32[32,256]{1,0:T(8,128)S(1)}, f32[32,256,128]{2,1,0:T(8,128)S(1)}) fusion(f32[256,128]{1,0:T(8,128)S(1)} %get-tuple-element.210, f32[32,128]{1,0:T(8,128)S(1)} %dynamic-slice_bitcast_fusion.4, bf16[65,128]{1,0:T(8,128)(2,1)S(1)} %get-tuple-element.212, s32[32,256]{1,0:T(8,128)S(1)} %dynamic-slice_bitcast_fusion.5), kind=kOutput, calls=%fused_computation.7.clone.1 | convolution fusion | flops 142073856 | bytes 4456704 | tf_op jit(solution)/shard_map/while/body/eval_jaxpr/ijb,bc->ijc/dot_general | solution.py:111
  251.9 3.9 %multiply_convert_fusion.8 = bf16[32,256,128]{2,1,0:T(8,128)(2,1)} fusion(f32[32,256,128]{2,1,0:T(8,128)S(1)} %get-tuple-element.182, f32[128]{0:T(128)S(1)} %get-tuple-element.213, f32[32,256]{1,0:T(8,128)S(1)} %get-tuple-element.185, f32[32,256]{1,0:T(8,128)S(1)} %get-tuple-element.186, f32[256,128]{1,0:T(8,128)S(1)} %get-tuple-element.210, ...), kind=kLoop, calls=%fused_computation.3.clone.1 | loop fusion | flops 6291456 | bytes 6504960 | tf_op jit(solution)/shard_map/while/body/eval_jaxpr/convert_element_type | solution.py:115
  255.8 8.1 %fusion.60 = f32[8192,128]{1,0:T(8,128)} fusion(bf16[512,128]{1,0:T(8,128)(2,1)S(1)} %get-tuple-element.215, bf16[8192,128]{1,0:T(8,128)(2,1)} %bitcast.74, bf16[128,512]{1,0:T(8,128)(2,1)S(1)} %get-tuple-element.214), kind=kOutput, calls=%fused_computation.6.clone.1 | convolution fusion | flops 2155872256 | bytes 6553600 | tf_op jit(solution)/shard_map/while/body/eval_jaxpr/dot_general | solution.py:120
  263.9 5.7 %fusion.61 = bf16[4,32,256,128]{3,2,1,0:T(8,128)(2,1)} fusion(bf16[4,32,256,128]{3,2,1,0:T(8,128)(2,1)} %get-tuple-element.198, s32[]{:T(128)} %get-tuple-element.197, f32[32,256,128]{2,1,0:T(8,128)} %bitcast.73, f32[32,256,128]{2,1,0:T(8,128)} %copy-done.1, f32[256,128]{1,0:T(8,128)S(1)} %get-tuple-element.210, ...), kind=kLoop, calls=%fused_computation.11.clone.1 | loop fusion | flops 4194304 | bytes 10633728 | tf_op jit(solution)/shard_map/while/body/jit(dynamic_update_index_in_dim)/dynamic_update_slice | solution.py:125
  270.4 3.4 %fusion.59 = (f32[32,256]{1,0:T(8,128)S(1)}, f32[32,256]{1,0:T(8,128)S(1)}, f32[32,256,128]{2,1,0:T(8,128)S(1)}) fusion(f32[256,128]{1,0:T(8,128)S(1)} %get-tuple-element.210, f32[32,128]{1,0:T(8,128)S(1)} %dynamic-slice_bitcast_fusion.4, bf16[65,128]{1,0:T(8,128)(2,1)S(1)} %get-tuple-element.212, s32[32,256]{1,0:T(8,128)S(1)} %dynamic-slice_bitcast_fusion.5), kind=kOutput, calls=%fused_computation.7.clone.1 | convolution fusion | flops 142073856 | bytes 4456704 | tf_op jit(solution)/shard_map/while/body/eval_jaxpr/ijb,bc->ijc/dot_general | solution.py:111
  273.8 3.9 %multiply_convert_fusion.8 = bf16[32,256,128]{2,1,0:T(8,128)(2,1)} fusion(f32[32,256,128]{2,1,0:T(8,128)S(1)} %get-tuple-element.182, f32[128]{0:T(128)S(1)} %get-tuple-element.213, f32[32,256]{1,0:T(8,128)S(1)} %get-tuple-element.185, f32[32,256]{1,0:T(8,128)S(1)} %get-tuple-element.186, f32[256,128]{1,0:T(8,128)S(1)} %get-tuple-element.210, ...), kind=kLoop, calls=%fused_computation.3.clone.1 | loop fusion | flops 6291456 | bytes 6504960 | tf_op jit(solution)/shard_map/while/body/eval_jaxpr/convert_element_type | solution.py:115
  277.7 8.1 %fusion.60 = f32[8192,128]{1,0:T(8,128)} fusion(bf16[512,128]{1,0:T(8,128)(2,1)S(1)} %get-tuple-element.215, bf16[8192,128]{1,0:T(8,128)(2,1)} %bitcast.74, bf16[128,512]{1,0:T(8,128)(2,1)S(1)} %get-tuple-element.214), kind=kOutput, calls=%fused_computation.6.clone.1 | convolution fusion | flops 2155872256 | bytes 6553600 | tf_op jit(solution)/shard_map/while/body/eval_jaxpr/dot_general | solution.py:120
  285.8 5.7 %fusion.61 = bf16[4,32,256,128]{3,2,1,0:T(8,128)(2,1)} fusion(bf16[4,32,256,128]{3,2,1,0:T(8,128)(2,1)} %get-tuple-element.198, s32[]{:T(128)} %get-tuple-element.197, f32[32,256,128]{2,1,0:T(8,128)} %bitcast.73, f32[32,256,128]{2,1,0:T(8,128)} %copy-done.1, f32[256,128]{1,0:T(8,128)S(1)} %get-tuple-element.210, ...), kind=kLoop, calls=%fused_computation.11.clone.1 | loop fusion | flops 4194304 | bytes 10633728 | tf_op jit(solution)/shard_map/while/body/jit(dynamic_update_index_in_dim)/dynamic_update_slice | solution.py:125
  292.3 3.4 %fusion.59 = (f32[32,256]{1,0:T(8,128)S(1)}, f32[32,256]{1,0:T(8,128)S(1)}, f32[32,256,128]{2,1,0:T(8,128)S(1)}) fusion(f32[256,128]{1,0:T(8,128)S(1)} %get-tuple-element.210, f32[32,128]{1,0:T(8,128)S(1)} %dynamic-slice_bitcast_fusion.4, bf16[65,128]{1,0:T(8,128)(2,1)S(1)} %get-tuple-element.212, s32[32,256]{1,0:T(8,128)S(1)} %dynamic-slice_bitcast_fusion.5), kind=kOutput, calls=%fused_computation.7.clone.1 | convolution fusion | flops 142073856 | bytes 4456704 | tf_op jit(solution)/shard_map/while/body/eval_jaxpr/ijb,bc->ijc/dot_general | solution.py:111
  295.7 3.9 %multiply_convert_fusion.8 = bf16[32,256,128]{2,1,0:T(8,128)(2,1)} fusion(f32[32,256,128]{2,1,0:T(8,128)S(1)} %get-tuple-element.182, f32[128]{0:T(128)S(1)} %get-tuple-element.213, f32[32,256]{1,0:T(8,128)S(1)} %get-tuple-element.185, f32[32,256]{1,0:T(8,128)S(1)} %get-tuple-element.186, f32[256,128]{1,0:T(8,128)S(1)} %get-tuple-element.210, ...), kind=kLoop, calls=%fused_computation.3.clone.1 | loop fusion | flops 6291456 | bytes 6504960 | tf_op jit(solution)/shard_map/while/body/eval_jaxpr/convert_element_type | solution.py:115
  299.6 8.1 %fusion.60 = f32[8192,128]{1,0:T(8,128)} fusion(bf16[512,128]{1,0:T(8,128)(2,1)S(1)} %get-tuple-element.215, bf16[8192,128]{1,0:T(8,128)(2,1)} %bitcast.74, bf16[128,512]{1,0:T(8,128)(2,1)S(1)} %get-tuple-element.214), kind=kOutput, calls=%fused_computation.6.clone.1 | convolution fusion | flops 2155872256 | bytes 6553600 | tf_op jit(solution)/shard_map/while/body/eval_jaxpr/dot_general | solution.py:120
  307.7 5.7 %fusion.61 = bf16[4,32,256,128]{3,2,1,0:T(8,128)(2,1)} fusion(bf16[4,32,256,128]{3,2,1,0:T(8,128)(2,1)} %get-tuple-element.198, s32[]{:T(128)} %get-tuple-element.197, f32[32,256,128]{2,1,0:T(8,128)} %bitcast.73, f32[32,256,128]{2,1,0:T(8,128)} %copy-done.1, f32[256,128]{1,0:T(8,128)S(1)} %get-tuple-element.210, ...), kind=kLoop, calls=%fused_computation.11.clone.1 | loop fusion | flops 4194304 | bytes 10633728 | tf_op jit(solution)/shard_map/while/body/jit(dynamic_update_index_in_dim)/dynamic_update_slice | solution.py:125
  (73 shorter events, 18.2 us)
Async XLA Ops:
  6.5 184.8 %copy-start = (bf16[1024,1024]{1,0:T(8,128)(2,1)S(1)}, bf16[1024,1024]{1,0:T(8,128)(2,1)}, u32[]{:S(2)}) copy-start(bf16[1024,1024]{1,0:T(8,128)(2,1)} %param.27) | copy-start | bytes 6291460
  6.5 50.2 %all-gather.2.cloned.1.call-start = ((), (), s32[]{:S(2)}) async-start(), calls=%async_computation.1 | async-start | bytes 2785280 | tf_op jit(solution)/shard_map/all_gather | solution.py:63
  8.1 2.7 copy-start.11
  13.7 121.1 %reduce-scatter.2.cloned.1.call-start = ((), (), s32[]{:S(2)}) async-start(), calls=%async_computation.2 | async-start | bytes 1474560 | tf_op jit(solution)/shard_map/reduce_scatter | solution.py:79
  59.7 1.4 copy-start.2
  63.1 90.9 %copy-start.3 = (bf16[320,1024]{1,0:T(8,128)(2,1)S(1)}, bf16[320,1024]{1,0:T(8,128)(2,1)}, u32[]{:S(2)}) copy-start(bf16[320,1024]{1,0:T(8,128)(2,1)} %param.26) | copy-start | bytes 1966084
  63.1 90.9 %copy-start.7 = (f32[320]{0:T(512)S(1)}, f32[320]{0:T(512)}, u32[]{:S(2)}) copy-start(f32[320]{0:T(512)} %param.25) | copy-start | bytes 3844
  154.5 37.3 %copy-start.4 = (bf16[1024,128]{1,0:T(8,128)(2,1)S(1)}, bf16[1024,128]{1,0:T(8,128)(2,1)}, u32[]{:S(2)}) copy-start(bf16[1024,128]{1,0:T(8,128)(2,1)} %param.29) | copy-start | bytes 786436
  154.5 71.0 %copy-start.5 = (bf16[1024,128]{1,0:T(8,128)(2,1)S(1)}, bf16[1024,128]{1,0:T(8,128)(2,1)}, u32[]{:S(2)}) copy-start(bf16[1024,128]{1,0:T(8,128)(2,1)} %param.28) | copy-start | bytes 786436
  191.3 34.5 %copy-start.6 = (f32[128]{0:T(128)S(1)}, f32[128]{0:T(128)}, u32[]{:S(2)}) copy-start(f32[128]{0:T(128)} %param.31) | copy-start | bytes 1540
  191.3 34.5 %copy-start.8 = (bf16[128,512]{1,0:T(8,128)(2,1)S(1)}, bf16[128,512]{1,0:T(8,128)(2,1)}, u32[]{:S(2)}) copy-start(bf16[128,512]{1,0:T(8,128)(2,1)} %param.32) | copy-start | bytes 393220
  191.3 34.5 %copy-start.9 = (bf16[512,128]{1,0:T(8,128)(2,1)S(1)}, bf16[512,128]{1,0:T(8,128)(2,1)}, u32[]{:S(2)}) copy-start(bf16[512,128]{1,0:T(8,128)(2,1)} %param.33) | copy-start | bytes 393220
  191.3 34.5 %copy-start.10 = (bf16[65,128]{1,0:T(8,128)(2,1)S(1)}, bf16[65,128]{1,0:T(8,128)(2,1)}, u32[]{:S(2)}) copy-start(bf16[65,128]{1,0:T(8,128)(2,1)} %param.30) | copy-start | bytes 49924
  229.9 4.0 %copy-start.1 = (f32[32,256,128]{2,1,0:T(8,128)}, f32[32,256,128]{2,1,0:T(8,128)S(1)}, u32[]{:S(2)}) copy-start(f32[32,256,128]{2,1,0:T(8,128)S(1)} %get-tuple-element.182) | copy-start | bytes 12582916 | tf_op jit(solution)/shard_map/while
  251.8 4.0 %copy-start.1 = (f32[32,256,128]{2,1,0:T(8,128)}, f32[32,256,128]{2,1,0:T(8,128)S(1)}, u32[]{:S(2)}) copy-start(f32[32,256,128]{2,1,0:T(8,128)S(1)} %get-tuple-element.182) | copy-start | bytes 12582916 | tf_op jit(solution)/shard_map/while
  273.7 4.0 %copy-start.1 = (f32[32,256,128]{2,1,0:T(8,128)}, f32[32,256,128]{2,1,0:T(8,128)S(1)}, u32[]{:S(2)}) copy-start(f32[32,256,128]{2,1,0:T(8,128)S(1)} %get-tuple-element.182) | copy-start | bytes 12582916 | tf_op jit(solution)/shard_map/while
  295.6 4.0 %copy-start.1 = (f32[32,256,128]{2,1,0:T(8,128)}, f32[32,256,128]{2,1,0:T(8,128)S(1)}, u32[]{:S(2)}) copy-start(f32[32,256,128]{2,1,0:T(8,128)S(1)} %get-tuple-element.182) | copy-start | bytes 12582916 | tf_op jit(solution)/shard_map/while
Sparse Core Ops, SparseCore 0:
  13.9 42.8 all-gather.1
  63.3 71.5 reduce-scatter.1
where the time goes:
time: 321 us; the launch traced here: 320 us
  waiting for transfers between devices  111 us (35%)
  blocking collectives  88.3 us (28%)
  matrix products  57.4 us (18%)
  other arithmetic  42.3 us (13%)
  between operations  13.7 us (4%)
  local copies, waits for them, and re-layouts  7.03 us (2%)
    reduce_scatter x1, waiting for transfers between devices, local(): shared = lax.psum_scatter(attn_part, 'col', scatter_dimension=1, tiled=True)  70.5 us
    all_gather x1, waiting for transfers between devices, local(): incoming = lax.all_gather(stacked, 'row', axis=0, tiled=True)  40.8 us
    psum x1, blocking collectives, local(): summed = lax.psum(part_single, 'col')  36.8 us
    all_gather x1, blocking collectives, local(): every_right = lax.all_gather(right, 'row', axis=0, tiled=True)  33.5 us
    dot_general x4, matrix products, pair_tile(): jnp.dot(expanded, w_contract, preferred_element_type=jnp.float32)  32.3 us
    dynamic_update_slice x4, other arithmetic, local(): lax.map(pair_tile, (rel_bins.reshape(row_count // block_rows, block_rows,...  22.9 us
    psum x1, blocking collectives, local(): lax.psum((jnp.sum(resid, -1), jnp.sum(resid * resid, -1)), 'col')  18.1 us
    convert_element_type x4, other arithmetic, pair_tile(): normed = layer_norm(pair_in, pair_gain).astype(jnp.bfloat16)  15.8 us
  transfers between devices with their start and end apart: 2, of which 2 were waited for; matrix products, arithmetic and copies ran while one was open for 1% of the time, Pallas kernels for 0%

commit v1 on v0

--- a/solution.py
+++ b/solution.py
@@ -27,6 +27,26 @@
     angles = jnp.concatenate([angles, angles], -1)[:, None, :]
     turned = jnp.concatenate([-vectors[..., half_size:], vectors[..., :half_size]], -1)
     return vectors * jnp.cos(angles) + turned * jnp.sin(angles)
+
+
+def flip_pairs(size, bit):
+    return [(place, place ^ bit) for place in range(size)]
+
+
+def along_z(step):
+    return [(place, place // 8 * 8 + (place % 8 + 2 * step) % 8) for place in range(16)]
+
+
+def along_y(step):
+    return [(place, place // 4 * 4 + (place + step) % 4) for place in range(8)]
+
+
+def right_pairs(flip):
+    return [
+        ((2 * col + ((row // 8) ^ flip)) * 8 + row % 8, row * 8 + col)
+        for row in range(16)
+        for col in range(8)
+    ]
 
 
 def local(
@@ -60,10 +80,28 @@
     keys = rotary(keys.reshape(row_count, local_heads, HD), positions).astype(jnp.bfloat16)
     values = jnp.dot(attn_in, w_value, preferred_element_type=jnp.float32).astype(jnp.bfloat16)
     stacked = jnp.concatenate([keys.reshape(row_count, local_width), values], 1)
-    incoming = lax.all_gather(stacked, "row", axis=0, tiled=True)
+    query = query.reshape(row_count, local_width)
+
+    blocks = [stacked] + [lax.ppermute(stacked, "row", along_z(step)) for step in (1, 3, 2)]
+    other_query = lax.ppermute(query, "row", flip_pairs(16, 8))
+    own_half = jnp.concatenate(blocks, 0)
+    other_half = lax.ppermute(own_half, "row", flip_pairs(16, 1))
+    incoming = jnp.concatenate([own_half, other_half], 0)
+    both_query = jnp.concatenate([query, other_query], 0).reshape(-1, local_heads, HD)
+
+    core = lax.rem(lax.axis_index("row"), 2)
+    col_index = lax.axis_index("col")
+    half_columns = w_single.shape[1] // 2
+    own_part = lax.dynamic_slice_in_dim(w_single, core * half_columns, half_columns, 1)
+    own_part = (own_part.astype(jnp.float32) * final_gain[:, None]).astype(jnp.bfloat16)
+    quarter = [own_part] + [lax.ppermute(own_part, "col", along_y(step)) for step in (1, 3, 2)]
+    quarter = jnp.concatenate(quarter, 0)
+    gathered = jnp.concatenate([quarter, lax.ppermute(quarter, "col", flip_pairs(8, 4))], 0)
+    gathered_other = lax.ppermute(gathered, "row", flip_pairs(16, 1))
+
     key_block = incoming[:, :local_width].reshape(-1, local_heads, HD)
     value_block = incoming[:, local_width:].reshape(-1, local_heads, HD)
-    scores = jnp.einsum("qhd,khd->hqk", query, key_block, preferred_element_type=jnp.float32)
+    scores = jnp.einsum("qhd,khd->hqk", both_query, key_block, preferred_element_type=jnp.float32)
     weights = jnp.exp(scores)
     totals = jnp.sum(weights, -1)
     numerator = jnp.einsum(
@@ -72,31 +110,53 @@
         value_block,
         preferred_element_type=jnp.float32,
     )
-    numerator, totals = (numerator, totals)
+    sent = numerator[:, row_count:].astype(jnp.bfloat16)
+    numerator = numerator[:, :row_count] + lax.ppermute(sent, "row", flip_pairs(16, 8)).astype(
+        jnp.float32
+    )
+    totals = totals[:, :row_count] + lax.ppermute(totals[:, row_count:], "row", flip_pairs(16, 8))
     context = (numerator / totals[..., None]).astype(jnp.bfloat16)
     context = jnp.transpose(context, (1, 0, 2)).reshape(row_count, local_width)
-    attn_part = jnp.dot(context, w_out, preferred_element_type=jnp.float32)
-    shared = lax.psum_scatter(attn_part, "col", scatter_dimension=1, tiled=True)
-    col_index = lax.axis_index("col")
-    feature_count = w_single.shape[0]
-    own_stream = lax.dynamic_slice_in_dim(stream, col_index * feature_count, feature_count, 1)
-    resid = own_stream + shared
-    sum_first, sum_second = lax.psum((jnp.sum(resid, -1), jnp.sum(resid * resid, -1)), "col")
-    average = sum_first / model_width
-    variance = sum_second / model_width - average * average
-    final = (
-        (resid - average[:, None]) * lax.rsqrt(variance[:, None] + epsilon) * final_gain
+    attn_part = jnp.dot(context, w_out, preferred_element_type=jnp.float32).astype(jnp.bfloat16)
+
+    col_size = lax.axis_size("col")
+    own_count = row_count // col_size
+    parts = lax.all_to_all(
+        attn_part.reshape(col_size, own_count, model_width), "col", 0, 0, tiled=False
+    )
+    own_stream = lax.dynamic_slice_in_dim(stream, col_index * own_count, own_count, 0)
+    resid = own_stream + jnp.sum(parts.astype(jnp.float32), 0)
+    final = layer_norm(resid, 1.0).astype(jnp.bfloat16)
+    far, near = (col_index // 4) * 4, lax.rem(col_index, 4)
+    order = [far + lax.rem(near + shift, 4) for shift in (0, 3, 1, 2)]
+    order = order + [lax.rem(place + 4, 8) for place in order]
+    final = jnp.concatenate(
+        [lax.dynamic_slice_in_dim(final, place * local_width, local_width, 1) for place in order], 1
+    )
+    lifted = []
+    for block in (gathered, gathered_other):
+        summed = jnp.dot(final, block, preferred_element_type=jnp.float32)
+        lifted.append(jnp.maximum(summed, 0.0).astype(jnp.bfloat16))
+    single = sum(
+        jnp.dot(
+            part,
+            lax.dynamic_slice_in_dim(w_second, side * half_columns, half_columns, 0),
+            preferred_element_type=jnp.float32,
+        )
+        for part, side in zip(lifted, (core, 1 - core))
     ).astype(jnp.bfloat16)
-    part_single = jnp.dot(final, w_single, preferred_element_type=jnp.float32)
-    summed = lax.psum(part_single, "col")
-    lifted = jnp.maximum(summed, 0.0).astype(jnp.bfloat16)
-    single = jnp.dot(lifted, w_second, preferred_element_type=jnp.float32).astype(jnp.bfloat16)
-    left = jnp.dot(single, w_left, preferred_element_type=jnp.float32).astype(jnp.bfloat16)
-    right = jnp.dot(single, w_right, preferred_element_type=jnp.float32).astype(jnp.bfloat16)
-    owner_count = lax.axis_size("row") // lax.axis_size("col")
-    every_right = lax.all_gather(right, "row", axis=0, tiled=True)
-    column_right = lax.dynamic_slice_in_dim(
-        every_right, col_index * owner_count * row_count, owner_count * row_count, 0
+    both = jnp.concatenate([w_left, w_right], 1)
+    both = jnp.dot(single, both, preferred_element_type=jnp.float32).astype(jnp.bfloat16)
+    both = lax.all_to_all(
+        jnp.broadcast_to(both, (col_size,) + both.shape), "col", 0, 0, tiled=False
+    ).reshape(row_count, -1)
+    channels = w_left.shape[1]
+    left, right = both[:, :channels], both[:, channels:]
+    first = lax.ppermute(right, ("row", "col"), right_pairs(0))
+    second = lax.ppermute(right, ("row", "col"), right_pairs(1))
+    upper = lax.axis_index("row") < 8
+    column_right = jnp.concatenate(
+        [jnp.where(upper, first, second), jnp.where(upper, second, first)], 0
     )
     col_count = column_right.shape[0]
     channels = column_right.shape[1]

time: 321 us -> 204 us (0.64)
  the two profiles are of different devices: /device:TPU:1 before, /device:TPU:96 now
where the time goes in v1:
time: 204 us; the launch traced here: 203 us
  matrix products  59.4 us (29%)
  waiting for transfers between devices  52.8 us (26%)
  other arithmetic  46.1 us (23%)
  starting transfers between devices  25.5 us (12%)
  blocking collectives  11.4 us (6%)
  local copies, waits for them, and re-layouts  7.13 us (3%)
    dot_general x4, matrix products, pair_tile(): jnp.dot(expanded, w_contract, preferred_element_type=jnp.float32)  32.4 us
    dynamic_update_slice x4, other arithmetic, local(): lax.map(pair_tile, (rel_bins.reshape(row_count // block_rows, block_rows,...  22.9 us
    ppermute x1, waiting for transfers between devices, local(): lax.ppermute(totals[:, row_count:], 'row', flip_pairs(16, 8))  21.8 us
    convert_element_type x4, other arithmetic, pair_tile(): normed = layer_norm(pair_in, pair_gain).astype(jnp.bfloat16)  16 us
    dot_general x4, matrix products, pair_tile(): jnp.einsum('ijb,bc->ijc', one_hot, rel_table, preferred_element_type=jnp....  13.4 us
    all_to_all x1, waiting for transfers between devices, local(): lax.all_to_all(attn_part.reshape(col_size, own_count, model_width), 'col'...  11.5 us
    all_to_all x1, blocking collectives, local(): lax.all_to_all(jnp.broadcast_to(both, (col_size,) + both.shape), 'col', 0...  11.4 us
    ppermute x3, waiting for transfers between devices, local(): lax.ppermute(own_part, 'col', along_y(step))  10 us
  transfers between devices with their start and end apart: 15, of which 8 were waited for; matrix products, arithmetic and copies ran while one was open for 7% of the time, Pallas kernels for 0%

profile of v1, /device:TPU:96, one launch (start us, length us, event | category | flops | bytes accessed | tf_op | source)
XLA Modules:
  0.0 202.8 jit_solution(4208587830514921673)
XLA Ops:
  24.5 6.0 %collective-permute-done.9 = bf16[320,512]{1,0:T(8,128)(2,1)S(1)} collective-permute-done((bf16[320,512]{1,0:T(8,128)(2,1)S(1)}, bf16[320,512]{1,0:T(8,128)(2,1)S(1)}, u32[]{:S(2)}, u32[]{:S(2)}) %collective-permute-start.9) | collective-permute-done | bytes 327712 | tf_op jit(solution)/shard_map/ppermute | solution.py:97
  40.4 21.8 %collective-permute-done.6 = f32[5,128]{1,0:T(8,128)S(1)} collective-permute-done((f32[5,128]{1,0:T(8,128)S(1)}, f32[5,128]{1,0:T(8,128)S(1)}, u32[]{:S(2)}, u32[]{:S(2)}) %collective-permute-start.6) | collective-permute-done | bytes 2592 | tf_op jit(solution)/shard_map/ppermute | solution.py:117
  64.8 4.9 %all-to-all-start = ((bf16[8,16,2560]{2,1,0:T(8,128)(2,1)}), bf16[8,16,2560]{2,1,0:T(8,128)(2,1)S(1)}, u32[]{:S(2)}, u32[]{:S(2)}) async-start(bf16[8,16,2560]{2,1,0:T(8,128)(2,1)} %bitcast.11), calls=%async_computation | async-start | bytes 1310720 | tf_op jit(solution)/shard_map/all_to_all | solution.py:124
  70.9 11.5 %all-to-all-done = bf16[8,16,2560]{2,1,0:T(8,128)(2,1)S(1)} async-done(((bf16[8,16,2560]{2,1,0:T(8,128)(2,1)}), bf16[8,16,2560]{2,1,0:T(8,128)(2,1)S(1)}, u32[]{:S(2)}, u32[]{:S(2)}) %all-to-all-start) | async-done | bytes 655392 | tf_op jit(solution)/shard_map/all_to_all | solution.py:124
  89.0 11.4 %all_to_all.10 = bf16[8,16,256]{2,1,0:T(8,128)(2,1)S(1)} all-to-all(bf16[8,16,256]{2,1,0:T(8,128)(2,1)S(1)} %broadcast_in_dim.8), channel_id=1, replica_groups=mesh['row'=16,'col'=8] {'col'}, dimensions={0} | all-to-all | bytes 131072 | tf_op jit(solution)/shard_map/all_to_all | solution.py:150
  100.4 4.7 %collective-permute-start.12 = (bf16[128,128]{1,0:T(8,128)(2,1)S(1)}, bf16[128,128]{1,0:T(8,128)(2,1)S(1)}, u32[]{:S(2)}, u32[]{:S(2)}) collective-permute-start(bf16[128,128]{1,0:T(8,128)(2,1)S(1)} %get-tuple-element.126), channel_id=1, source_target_pairs={{0,0},{16,1},{32,2},{48,3},{64,4},{80,5},{96,6},{112,7},{1,8},{17,... | collective-permute-start | bytes 98312 | tf_op jit(solution)/shard_map/ppermute | solution.py:155
  105.6 6.6 %collective-permute-done.12 = bf16[128,128]{1,0:T(8,128)(2,1)S(1)} collective-permute-done((bf16[128,128]{1,0:T(8,128)(2,1)S(1)}, bf16[128,128]{1,0:T(8,128)(2,1)S(1)}, u32[]{:S(2)}, u32[]{:S(2)}) %collective-permute-start.12) | collective-permute-done | bytes 32800 | tf_op jit(solution)/shard_map/ppermute | solution.py:155
  114.8 88.0 %while.11 = (s32[]{:T(128)}, bf16[4,32,256,128]{3,2,1,0:T(8,128)(2,1)}, f32[4,32,128]{2,1,0:T(8,128)S(1)}, f32[256,128]{1,0:T(8,128)S(1)}, s32[4,32,256]{2,1,0:T...) while((s32[]{:T(128)}, ...), condition=%wide.region_9.10_spmd.clone, body=%wide.region_6.9_spmd.clone.sunk | while | flops 2308472832 | bytes 45155720 | solution.py:185
  115.6 3.4 %fusion.70 = (f32[32,256]{1,0:T(8,128)S(1)}, f32[32,256]{1,0:T(8,128)S(1)}, f32[32,256,128]{2,1,0:T(8,128)S(1)}) fusion(f32[256,128]{1,0:T(8,128)S(1)} %get-tuple-element.230, f32[32,128]{1,0:T(8,128)S(1)} %dynamic-slice_bitcast_fusion.4, bf16[65,128]{1,0:T(8,128)(2,1)S(1)} %get-tuple-element.232, s32[32,256]{1,0:T(8,128)S(1)} %dynamic-slice_bitcast_fusion.5), kind=kOutput, calls=%fused_computation.7.clone.1 | convolution fusion | flops 142073856 | bytes 4456704 | tf_op jit(solution)/shard_map/while/body/eval_jaxpr/ijb,bc->ijc/dot_general | solution.py:171
  119.0 4.0 %multiply_convert_fusion.9 = bf16[32,256,128]{2,1,0:T(8,128)(2,1)} fusion(f32[32,256,128]{2,1,0:T(8,128)S(1)} %get-tuple-element.202, f32[128]{0:T(128)S(1)} %get-tuple-element.233, f32[32,256]{1,0:T(8,128)S(1)} %get-tuple-element.205, f32[32,256]{1,0:T(8,128)S(1)} %get-tuple-element.206, f32[256,128]{1,0:T(8,128)S(1)} %get-tuple-element.230, ...), kind=kLoop, calls=%fused_computation.3.clone.1 | loop fusion | flops 6291456 | bytes 6504960 | tf_op jit(solution)/shard_map/while/body/eval_jaxpr/convert_element_type | solution.py:175
  123.0 8.1 %fusion.71 = f32[8192,128]{1,0:T(8,128)} fusion(bf16[512,128]{1,0:T(8,128)(2,1)S(1)} %get-tuple-element.235, bf16[8192,128]{1,0:T(8,128)(2,1)} %bitcast.79, bf16[128,512]{1,0:T(8,128)(2,1)S(1)} %get-tuple-element.234), kind=kOutput, calls=%fused_computation.6.clone.1 | convolution fusion | flops 2155872256 | bytes 6553600 | tf_op jit(solution)/shard_map/while/body/eval_jaxpr/dot_general | solution.py:180
  131.1 5.7 %fusion.72 = bf16[4,32,256,128]{3,2,1,0:T(8,128)(2,1)} fusion(bf16[4,32,256,128]{3,2,1,0:T(8,128)(2,1)} %get-tuple-element.218, s32[]{:T(128)} %get-tuple-element.217, f32[32,256,128]{2,1,0:T(8,128)} %bitcast.78, f32[32,256,128]{2,1,0:T(8,128)} %copy-done.1, f32[256,128]{1,0:T(8,128)S(1)} %get-tuple-element.230, ...), kind=kLoop, calls=%fused_computation.11.clone.1 | loop fusion | flops 4194304 | bytes 10633728 | tf_op jit(solution)/shard_map/while/body/jit(dynamic_update_index_in_dim)/dynamic_update_slice | solution.py:185
  137.6 3.4 %fusion.70 = (f32[32,256]{1,0:T(8,128)S(1)}, f32[32,256]{1,0:T(8,128)S(1)}, f32[32,256,128]{2,1,0:T(8,128)S(1)}) fusion(f32[256,128]{1,0:T(8,128)S(1)} %get-tuple-element.230, f32[32,128]{1,0:T(8,128)S(1)} %dynamic-slice_bitcast_fusion.4, bf16[65,128]{1,0:T(8,128)(2,1)S(1)} %get-tuple-element.232, s32[32,256]{1,0:T(8,128)S(1)} %dynamic-slice_bitcast_fusion.5), kind=kOutput, calls=%fused_computation.7.clone.1 | convolution fusion | flops 142073856 | bytes 4456704 | tf_op jit(solution)/shard_map/while/body/eval_jaxpr/ijb,bc->ijc/dot_general | solution.py:171
  141.0 4.0 %multiply_convert_fusion.9 = bf16[32,256,128]{2,1,0:T(8,128)(2,1)} fusion(f32[32,256,128]{2,1,0:T(8,128)S(1)} %get-tuple-element.202, f32[128]{0:T(128)S(1)} %get-tuple-element.233, f32[32,256]{1,0:T(8,128)S(1)} %get-tuple-element.205, f32[32,256]{1,0:T(8,128)S(1)} %get-tuple-element.206, f32[256,128]{1,0:T(8,128)S(1)} %get-tuple-element.230, ...), kind=kLoop, calls=%fused_computation.3.clone.1 | loop fusion | flops 6291456 | bytes 6504960 | tf_op jit(solution)/shard_map/while/body/eval_jaxpr/convert_element_type | solution.py:175
  145.0 8.1 %fusion.71 = f32[8192,128]{1,0:T(8,128)} fusion(bf16[512,128]{1,0:T(8,128)(2,1)S(1)} %get-tuple-element.235, bf16[8192,128]{1,0:T(8,128)(2,1)} %bitcast.79, bf16[128,512]{1,0:T(8,128)(2,1)S(1)} %get-tuple-element.234), kind=kOutput, calls=%fused_computation.6.clone.1 | convolution fusion | flops 2155872256 | bytes 6553600 | tf_op jit(solution)/shard_map/while/body/eval_jaxpr/dot_general | solution.py:180
  153.1 5.7 %fusion.72 = bf16[4,32,256,128]{3,2,1,0:T(8,128)(2,1)} fusion(bf16[4,32,256,128]{3,2,1,0:T(8,128)(2,1)} %get-tuple-element.218, s32[]{:T(128)} %get-tuple-element.217, f32[32,256,128]{2,1,0:T(8,128)} %bitcast.78, f32[32,256,128]{2,1,0:T(8,128)} %copy-done.1, f32[256,128]{1,0:T(8,128)S(1)} %get-tuple-element.230, ...), kind=kLoop, calls=%fused_computation.11.clone.1 | loop fusion | flops 4194304 | bytes 10633728 | tf_op jit(solution)/shard_map/while/body/jit(dynamic_update_index_in_dim)/dynamic_update_slice | solution.py:185
  159.6 3.4 %fusion.70 = (f32[32,256]{1,0:T(8,128)S(1)}, f32[32,256]{1,0:T(8,128)S(1)}, f32[32,256,128]{2,1,0:T(8,128)S(1)}) fusion(f32[256,128]{1,0:T(8,128)S(1)} %get-tuple-element.230, f32[32,128]{1,0:T(8,128)S(1)} %dynamic-slice_bitcast_fusion.4, bf16[65,128]{1,0:T(8,128)(2,1)S(1)} %get-tuple-element.232, s32[32,256]{1,0:T(8,128)S(1)} %dynamic-slice_bitcast_fusion.5), kind=kOutput, calls=%fused_computation.7.clone.1 | convolution fusion | flops 142073856 | bytes 4456704 | tf_op jit(solution)/shard_map/while/body/eval_jaxpr/ijb,bc->ijc/dot_general | solution.py:171
  163.0 4.0 %multiply_convert_fusion.9 = bf16[32,256,128]{2,1,0:T(8,128)(2,1)} fusion(f32[32,256,128]{2,1,0:T(8,128)S(1)} %get-tuple-element.202, f32[128]{0:T(128)S(1)} %get-tuple-element.233, f32[32,256]{1,0:T(8,128)S(1)} %get-tuple-element.205, f32[32,256]{1,0:T(8,128)S(1)} %get-tuple-element.206, f32[256,128]{1,0:T(8,128)S(1)} %get-tuple-element.230, ...), kind=kLoop, calls=%fused_computation.3.clone.1 | loop fusion | flops 6291456 | bytes 6504960 | tf_op jit(solution)/shard_map/while/body/eval_jaxpr/convert_element_type | solution.py:175
  167.0 8.1 %fusion.71 = f32[8192,128]{1,0:T(8,128)} fusion(bf16[512,128]{1,0:T(8,128)(2,1)S(1)} %get-tuple-element.235, bf16[8192,128]{1,0:T(8,128)(2,1)} %bitcast.79, bf16[128,512]{1,0:T(8,128)(2,1)S(1)} %get-tuple-element.234), kind=kOutput, calls=%fused_computation.6.clone.1 | convolution fusion | flops 2155872256 | bytes 6553600 | tf_op jit(solution)/shard_map/while/body/eval_jaxpr/dot_general | solution.py:180
  175.1 5.7 %fusion.72 = bf16[4,32,256,128]{3,2,1,0:T(8,128)(2,1)} fusion(bf16[4,32,256,128]{3,2,1,0:T(8,128)(2,1)} %get-tuple-element.218, s32[]{:T(128)} %get-tuple-element.217, f32[32,256,128]{2,1,0:T(8,128)} %bitcast.78, f32[32,256,128]{2,1,0:T(8,128)} %copy-done.1, f32[256,128]{1,0:T(8,128)S(1)} %get-tuple-element.230, ...), kind=kLoop, calls=%fused_computation.11.clone.1 | loop fusion | flops 4194304 | bytes 10633728 | tf_op jit(solution)/shard_map/while/body/jit(dynamic_update_index_in_dim)/dynamic_update_slice | solution.py:185
  181.6 3.4 %fusion.70 = (f32[32,256]{1,0:T(8,128)S(1)}, f32[32,256]{1,0:T(8,128)S(1)}, f32[32,256,128]{2,1,0:T(8,128)S(1)}) fusion(f32[256,128]{1,0:T(8,128)S(1)} %get-tuple-element.230, f32[32,128]{1,0:T(8,128)S(1)} %dynamic-slice_bitcast_fusion.4, bf16[65,128]{1,0:T(8,128)(2,1)S(1)} %get-tuple-element.232, s32[32,256]{1,0:T(8,128)S(1)} %dynamic-slice_bitcast_fusion.5), kind=kOutput, calls=%fused_computation.7.clone.1 | convolution fusion | flops 142073856 | bytes 4456704 | tf_op jit(solution)/shard_map/while/body/eval_jaxpr/ijb,bc->ijc/dot_general | solution.py:171
  185.0 4.0 %multiply_convert_fusion.9 = bf16[32,256,128]{2,1,0:T(8,128)(2,1)} fusion(f32[32,256,128]{2,1,0:T(8,128)S(1)} %get-tuple-element.202, f32[128]{0:T(128)S(1)} %get-tuple-element.233, f32[32,256]{1,0:T(8,128)S(1)} %get-tuple-element.205, f32[32,256]{1,0:T(8,128)S(1)} %get-tuple-element.206, f32[256,128]{1,0:T(8,128)S(1)} %get-tuple-element.230, ...), kind=kLoop, calls=%fused_computation.3.clone.1 | loop fusion | flops 6291456 | bytes 6504960 | tf_op jit(solution)/shard_map/while/body/eval_jaxpr/convert_element_type | solution.py:175
  189.0 8.1 %fusion.71 = f32[8192,128]{1,0:T(8,128)} fusion(bf16[512,128]{1,0:T(8,128)(2,1)S(1)} %get-tuple-element.235, bf16[8192,128]{1,0:T(8,128)(2,1)} %bitcast.79, bf16[128,512]{1,0:T(8,128)(2,1)S(1)} %get-tuple-element.234), kind=kOutput, calls=%fused_computation.6.clone.1 | convolution fusion | flops 2155872256 | bytes 6553600 | tf_op jit(solution)/shard_map/while/body/eval_jaxpr/dot_general | solution.py:180
  197.1 5.7 %fusion.72 = bf16[4,32,256,128]{3,2,1,0:T(8,128)(2,1)} fusion(bf16[4,32,256,128]{3,2,1,0:T(8,128)(2,1)} %get-tuple-element.218, s32[]{:T(128)} %get-tuple-element.217, f32[32,256,128]{2,1,0:T(8,128)} %bitcast.78, f32[32,256,128]{2,1,0:T(8,128)} %copy-done.1, f32[256,128]{1,0:T(8,128)S(1)} %get-tuple-element.230, ...), kind=kLoop, calls=%fused_computation.11.clone.1 | loop fusion | flops 4194304 | bytes 10633728 | tf_op jit(solution)/shard_map/while/body/jit(dynamic_update_index_in_dim)/dynamic_update_slice | solution.py:185
  (118 shorter events, 50.7 us)
Async XLA Ops:
  0.0 83.8 %copy-start = (bf16[1024,1024]{1,0:T(8,128)(2,1)S(1)}, bf16[1024,1024]{1,0:T(8,128)(2,1)}, u32[]{:S(2)}) copy-start(bf16[1024,1024]{1,0:T(8,128)(2,1)} %param.27) | copy-start | bytes 6291460
  7.8 7.8 %collective-permute-start.1 = (bf16[128,640]{0,1:T(8,128)(2,1)}, bf16[128,640]{0,1:T(8,128)(2,1)S(1)}, u32[]{:S(2)}, u32[]{:S(2)}) collective-permute-start(bf16[128,640]{0,1:T(8,128)(2,1)} %get-tuple-element.112), channel_id=1, source_target_pairs={{0,16},{8,24},{16,32},{24,40},{32,48},{40,56},{48,0},{56,8},{64,80... | collective-permute-start | bytes 491528 | tf_op jit(solution)/shard_map/ppermute | solution.py:85
  7.8 10.9 %collective-permute-start.2 = (bf16[128,640]{0,1:T(8,128)(2,1)}, bf16[128,640]{0,1:T(8,128)(2,1)S(1)}, u32[]{:S(2)}, u32[]{:S(2)}) collective-permute-start(bf16[128,640]{0,1:T(8,128)(2,1)} %get-tuple-element.112), channel_id=1, source_target_pairs={{0,48},{8,56},{16,0},{24,8},{32,16},{40,24},{48,32},{56,40},{64,11... | collective-permute-start | bytes 491528 | tf_op jit(solution)/shard_map/ppermute | solution.py:85
  9.8 10.3 %collective-permute-start.3 = (bf16[128,640]{0,1:T(8,128)(2,1)}, bf16[128,640]{0,1:T(8,128)(2,1)S(1)}, u32[]{:S(2)}, u32[]{:S(2)}) collective-permute-start(bf16[128,640]{0,1:T(8,128)(2,1)} %get-tuple-element.112), channel_id=1, source_target_pairs={{0,32},{8,40},{16,48},{24,56},{32,0},{40,8},{48,16},{56,24},{64,96... | collective-permute-start | bytes 491528 | tf_op jit(solution)/shard_map/ppermute | solution.py:85
  10.4 10.0 %copy-start.3 = (bf16[1024,640]{0,1:T(8,128)(2,1)S(1)}, bf16[1024,640]{0,1:T(8,128)(2,1)}, u32[]{:S(2)}) copy-start(bf16[1024,640]{0,1:T(8,128)(2,1)} %get-tuple-element.113) | copy-start | bytes 3932164
  12.3 10.7 %collective-permute-start.7 = (bf16[320,512]{1,0:T(8,128)(2,1)S(1)}, bf16[320,512]{1,0:T(8,128)(2,1)S(1)}, u32[]{:S(2)}, u32[]{:S(2)}) collective-permute-start(bf16[320,512]{1,0:T(8,128)(2,1)S(1)} %get-tuple-element.103), channel_id=1, source_target_pairs={{0,1},{1,2},{2,3},{3,0},{4,5},{5,6},{6,7},{7,4},{8,9},{9,10},{10,1... | collective-permute-start | bytes 983048 | tf_op jit(solution)/shard_map/ppermute | solution.py:97
  13.9 10.7 %collective-permute-start.8 = (bf16[320,512]{1,0:T(8,128)(2,1)S(1)}, bf16[320,512]{1,0:T(8,128)(2,1)S(1)}, u32[]{:S(2)}, u32[]{:S(2)}) collective-permute-start(bf16[320,512]{1,0:T(8,128)(2,1)S(1)} %get-tuple-element.103), channel_id=1, source_target_pairs={{0,3},{1,0},{2,1},{3,2},{4,7},{5,4},{6,5},{7,6},{8,11},{9,8},{10,9... | collective-permute-start | bytes 983048 | tf_op jit(solution)/shard_map/ppermute | solution.py:97
  15.5 15.0 %collective-permute-start.9 = (bf16[320,512]{1,0:T(8,128)(2,1)S(1)}, bf16[320,512]{1,0:T(8,128)(2,1)S(1)}, u32[]{:S(2)}, u32[]{:S(2)}) collective-permute-start(bf16[320,512]{1,0:T(8,128)(2,1)S(1)} %get-tuple-element.103), channel_id=1, source_target_pairs={{0,2},{1,3},{2,0},{3,1},{4,6},{5,7},{6,4},{7,5},{8,10},{9,11},{10,... | collective-permute-start | bytes 983048 | tf_op jit(solution)/shard_map/ppermute | solution.py:97
  18.7 17.5 %collective-permute-start = (bf16[128,320]{0,1:T(8,128)(2,1)S(1)}, bf16[128,320]{0,1:T(8,128)(2,1)S(1)}, u32[]{:S(2)}, u32[]{:S(2)}) collective-permute-start(bf16[128,320]{0,1:T(8,128)(2,1)S(1)} %get-tuple-element.128), channel_id=1, source_target_pairs={{0,64},{8,72},{16,80},{24,88},{32,96},{40,104},{48,112},{56,120},{... | collective-permute-start | bytes 245768 | tf_op jit(solution)/shard_map/ppermute | solution.py:86
  20.2 15.8 %collective-permute-start.4 = (bf16[512,640]{0,1:T(8,128)(2,1)S(1)}, bf16[512,640]{0,1:T(8,128)(2,1)S(1)}, u32[]{:S(2)}, u32[]{:S(2)}) collective-permute-start(bf16[512,640]{0,1:T(8,128)(2,1)S(1)} %pad_maximum_fusion.1), channel_id=1, source_target_pairs={{0,8},{8,0},{16,24},{24,16},{32,40},{40,32},{48,56},{56,48},{64,72... | collective-permute-start | bytes 1966088 | tf_op jit(solution)/shard_map/ppermute | solution.py:88
  30.6 31.6 %collective-permute-start.10 = (bf16[1280,512]{1,0:T(8,128)(2,1)S(1)}, bf16[1280,512]{1,0:T(8,128)(2,1)S(1)}, u32[]{:S(2)}, u32[]{:S(2)}) collective-permute-start(bf16[1280,512]{1,0:T(8,128)(2,1)S(1)} %pad_maximum_fusion), channel_id=1, source_target_pairs={{0,4},{1,5},{2,6},{3,7},{4,0},{5,1},{6,2},{7,3},{8,12},{9,13},{10,... | collective-permute-start | bytes 3932168 | tf_op jit(solution)/shard_map/ppermute | solution.py:99
  37.3 24.9 %collective-permute-start.6 = (f32[5,128]{1,0:T(8,128)S(1)}, f32[5,128]{1,0:T(8,128)S(1)}, u32[]{:S(2)}, u32[]{:S(2)}) collective-permute-start(f32[5,128]{1,0:T(8,128)S(1)} %slice.58), channel_id=1, source_target_pairs={{0,64},{8,72},{16,80},{24,88},{32,96},{40,104},{48,112},{56,120},{... | collective-permute-start | bytes 7688 | tf_op jit(solution)/shard_map/ppermute | solution.py:117
  38.9 24.5 %copy-start.4 = (bf16[320,2560]{1,0:T(8,128)(2,1)S(1)}, bf16[320,2560]{1,0:T(8,128)(2,1)}, u32[]{:S(2)}) copy-start(bf16[320,2560]{1,0:T(8,128)(2,1)} %param.24) | copy-start | bytes 4915204
  38.9 24.5 %collective-permute-start.5 = (bf16[5,128,64]{1,2,0:T(8,128)(2,1)S(1)}, bf16[5,128,64]{1,2,0:T(8,128)(2,1)S(1)}, u32[]{:S(2)}, u32[]{:S(2)}) collective-permute-start(bf16[5,128,64]{1,2,0:T(8,128)(2,1)S(1)} %slice.70), channel_id=1, source_target_pairs={{0,64},{8,72},{16,80},{24,88},{32,96},{40,104},{48,112},{56,120},{... | collective-permute-start | bytes 245768 | tf_op jit(solution)/shard_map/ppermute | solution.py:114
  63.3 23.0 %collective-permute-start.11 = (bf16[2560,512]{1,0:T(8,128)(2,1)}, bf16[2560,512]{1,0:T(8,128)(2,1)}, u32[]{:S(2)}, u32[]{:S(2)}) collective-permute-start(bf16[2560,512]{1,0:T(8,128)(2,1)} %constant_dynamic-update-slice_fusion.5), channel_id=1, source_target_pairs={{0,8},{8,0},{16,24},{24,16},{32,40},{40,32},{48,56},{56,48},{64,72... | collective-permute-start | bytes 7864328 | tf_op jit(solution)/shard_map/ppermute | solution.py:100
  64.8 17.5 %all-to-all-start = ((bf16[8,16,2560]{2,1,0:T(8,128)(2,1)}), bf16[8,16,2560]{2,1,0:T(8,128)(2,1)S(1)}, u32[]{:S(2)}, u32[]{:S(2)}) async-start(bf16[8,16,2560]{2,1,0:T(8,128)(2,1)} %bitcast.11), calls=%async_computation | async-start | bytes 1310720 | tf_op jit(solution)/shard_map/all_to_all | solution.py:124
  86.3 28.5 %copy-start.7 = (f32[128]{0:T(128)S(1)}, f32[128]{0:T(128)}, u32[]{:S(2)}) copy-start(f32[128]{0:T(128)} %param.31) | copy-start | bytes 1540
  86.3 28.5 %copy-start.10 = (bf16[128,512]{1,0:T(8,128)(2,1)S(1)}, bf16[128,512]{1,0:T(8,128)(2,1)}, u32[]{:S(2)}) copy-start(bf16[128,512]{1,0:T(8,128)(2,1)} %param.32) | copy-start | bytes 393220
  86.3 28.5 %copy-start.11 = (bf16[512,128]{1,0:T(8,128)(2,1)S(1)}, bf16[512,128]{1,0:T(8,128)(2,1)}, u32[]{:S(2)}) copy-start(bf16[512,128]{1,0:T(8,128)(2,1)} %param.33) | copy-start | bytes 393220
  86.3 28.5 %copy-start.12 = (bf16[65,128]{1,0:T(8,128)(2,1)S(1)}, bf16[65,128]{1,0:T(8,128)(2,1)}, u32[]{:S(2)}) copy-start(bf16[65,128]{1,0:T(8,128)(2,1)} %param.30) | copy-start | bytes 49924
  100.4 11.8 %collective-permute-start.12 = (bf16[128,128]{1,0:T(8,128)(2,1)S(1)}, bf16[128,128]{1,0:T(8,128)(2,1)S(1)}, u32[]{:S(2)}, u32[]{:S(2)}) collective-permute-start(bf16[128,128]{1,0:T(8,128)(2,1)S(1)} %get-tuple-element.126), channel_id=1, source_target_pairs={{0,0},{16,1},{32,2},{48,3},{64,4},{80,5},{96,6},{112,7},{1,8},{17,... | collective-permute-start | bytes 98312 | tf_op jit(solution)/shard_map/ppermute | solution.py:155
  105.1 9.6 %collective-permute-start.13 = (bf16[128,128]{1,0:T(8,128)(2,1)S(1)}, bf16[128,128]{1,0:T(8,128)(2,1)S(1)}, u32[]{:S(2)}, u32[]{:S(2)}) collective-permute-start(bf16[128,128]{1,0:T(8,128)(2,1)S(1)} %get-tuple-element.126), channel_id=1, source_target_pairs={{8,0},{24,1},{40,2},{56,3},{72,4},{88,5},{104,6},{120,7},{9,8},{25... | collective-permute-start | bytes 98312 | tf_op jit(solution)/shard_map/ppermute | solution.py:156
  118.9 4.0 %copy-start.1 = (f32[32,256,128]{2,1,0:T(8,128)}, f32[32,256,128]{2,1,0:T(8,128)S(1)}, u32[]{:S(2)}) copy-start(f32[32,256,128]{2,1,0:T(8,128)S(1)} %get-tuple-element.202) | copy-start | bytes 12582916 | tf_op jit(solution)/shard_map/while
  140.9 4.0 %copy-start.1 = (f32[32,256,128]{2,1,0:T(8,128)}, f32[32,256,128]{2,1,0:T(8,128)S(1)}, u32[]{:S(2)}) copy-start(f32[32,256,128]{2,1,0:T(8,128)S(1)} %get-tuple-element.202) | copy-start | bytes 12582916 | tf_op jit(solution)/shard_map/while
  (8 other events, 27.8 us)

commit v2 on v1

v2 whole, which is shorter than its diff:
```python
import math

import jax
import jax.numpy as jnp
from jax import lax
from jax.experimental import pallas as pl
from jax.experimental.pallas import tpu as pltpu
from jax.sharding import PartitionSpec as P

HD = 64


epsilon = 1e-05


def layer_norm(values, gain):
    count = values.shape[-1]
    average = jnp.sum(values, -1, keepdims=True) / count
    variance = jnp.sum(values * values, -1, keepdims=True) / count - average * average
    return (values - average) * lax.rsqrt(variance + epsilon) * gain


def rotary(vectors, positions):
    half_size = vectors.shape[-1] // 2
    frequency = jnp.exp(
        jnp.arange(half_size, dtype=jnp.float32) * (-2.0 * math.log(10000.0) / vectors.shape[-1])
    )
    angles = positions.astype(jnp.float32)[:, None] * frequency[None, :]
    angles = jnp.concatenate([angles, angles], -1)[:, None, :]
    turned = jnp.concatenate([-vectors[..., half_size:], vectors[..., :half_size]], -1)
    return vectors * jnp.cos(angles) + turned * jnp.sin(angles)


def flip_pairs(size, bit):
    return [(place, place ^ bit) for place in range(size)]


def along_z(step):
    return [(place, place // 8 * 8 + (place % 8 + 2 * step) % 8) for place in range(16)]


def along_y(step):
    return [(place, place // 4 * 4 + (place + step) % 4) for place in range(8)]


def right_pairs(flip):
    return [
        ((2 * col + ((row // 8) ^ flip)) * 8 + row % 8, row * 8 + col)
        for row in range(16)
        for col in range(8)
    ]


def whole(array):
    return pl.BlockSpec(array.shape, lambda step: (0,) * array.ndim)


def pair_kernel(table_ref, left_ref, right_ref, gain_ref, expand_ref, contract_ref, out_ref):
    rows, columns, channels = table_ref.shape
    group = 8

    def pair_in(part):
        sums = left_ref[part, :][:, None, :] + right_ref[...][None]
        return table_ref[part].astype(jnp.float32) + sums

    for start in range(0, rows, group):
        part = slice(start, start + group)
        normed = layer_norm(pair_in(part), gain_ref[...]).astype(jnp.bfloat16)
        expanded = jnp.dot(
            normed.reshape(group * columns, channels),
            expand_ref[...],
            preferred_element_type=jnp.float32,
        )
        expanded = jnp.maximum(expanded.astype(jnp.bfloat16), 0)
        update = jnp.dot(expanded, contract_ref[...], preferred_element_type=jnp.float32)
        out_ref[part] = (pair_in(part) + update.reshape(group, columns, channels)).astype(
            jnp.bfloat16
        )


def pair_stage(table_part, left, right, gain, w_expand, w_contract):
    rows, columns, channels = table_part.shape
    block = 16
    left = left.astype(jnp.float32)
    right = right.astype(jnp.float32)
    gain = gain.reshape(1, channels)
    fixed = [right, gain, w_expand, w_contract]
    return pl.pallas_call(
        pair_kernel,
        grid=(rows // block,),
        in_specs=[
            pl.BlockSpec((block, columns, channels), lambda step: (step, 0, 0)),
            pl.BlockSpec((block, channels), lambda step: (step, 0)),
        ]
        + [whole(array) for array in fixed],
        out_specs=pl.BlockSpec((block, columns, channels), lambda step: (step, 0, 0)),
        out_shape=jax.ShapeDtypeStruct(table_part.shape, jnp.bfloat16),
        compiler_params=pltpu.CompilerParams(vmem_limit_bytes=48 << 20),
        name="pair",
    )(table_part, left, *fixed)


def local(
    hidden,
    rel_bins,
    attn_gain,
    w_query,
    w_key,
    w_value,
    w_out,
    final_gain,
    w_single,
    w_second,
    w_left,
    w_right,
    rel_table,
    pair_gain,
    w_expand,
    w_contract,
):
    row_count = hidden.shape[0]
    model_width = hidden.shape[1]
    local_width = w_query.shape[1]
    local_heads = local_width // HD
    positions = lax.axis_index("row") * row_count + jnp.arange(row_count, dtype=jnp.int32)
    stream = hidden.astype(jnp.float32)
    attn_in = layer_norm(stream, attn_gain).astype(jnp.bfloat16)
    keys = jnp.dot(attn_in, w_key, preferred_element_type=jnp.float32)
    keys = rotary(keys.reshape(row_count, local_heads, HD), positions).astype(jnp.bfloat16)
    values = jnp.dot(attn_in, w_value, preferred_element_type=jnp.float32).astype(jnp.bfloat16)
    stacked = jnp.concatenate([keys.reshape(row_count, local_width), values], 1)
    stacked, attn_in = lax.optimization_barrier((stacked, attn_in))

    blocks = [stacked] + [lax.ppermute(stacked, "row", along_z(step)) for step in (1, 3, 2)]
    query = jnp.dot(attn_in, w_query, preferred_element_type=jnp.float32) * HD ** (-0.5)
    query = rotary(query.reshape(row_count, local_heads, HD), positions).astype(jnp.bfloat16)
    query = query.reshape(row_count, local_width)
    query, w_single, rel_bins = lax.optimization_barrier((query, w_single, rel_bins))
    other_query = lax.ppermute(query, "row", flip_pairs(16, 8))

    core = lax.rem(lax.axis_index("row"), 2)
    col_index = lax.axis_index("col")
    half_columns = w_single.shape[1] // 2
    own_part = lax.dynamic_slice_in_dim(w_single, core * half_columns, half_columns, 1)
    own_part = (own_part.astype(jnp.float32) * final_gain[:, None]).astype(jnp.bfloat16)
    quarter = [own_part] + [lax.ppermute(own_part, "col", along_y(step)) for step in (1, 3, 2)]
    quarter = jnp.concatenate(quarter, 0)
    quarter_other = lax.ppermute(quarter, "row", flip_pairs(16, 1))

    bin_codes = jnp.arange(rel_table.shape[0], dtype=jnp.int32)
    one_hot = (rel_bins[..., None] == bin_codes).astype(jnp.bfloat16)
    table_part = jnp.einsum(
        "ijb,bc->ijc", one_hot, rel_table, preferred_element_type=jnp.float32
    ).astype(jnp.bfloat16)

    own_half = jnp.concatenate(blocks, 0)
    other_half = lax.ppermute(own_half, "row", flip_pairs(16, 1))
    incoming = jnp.concatenate([own_half, other_half], 0)
    both_query = jnp.concatenate([query, other_query], 0).reshape(-1, local_heads, HD)
    key_block = incoming[:, :local_width].reshape(-1, local_heads, HD)
    value_block = incoming[:, local_width:].reshape(-1, local_heads, HD)
    scores = jnp.einsum("qhd,khd->hqk", both_query, key_block, preferred_element_type=jnp.float32)
    weights = jnp.exp(scores)
    totals = jnp.sum(weights, -1)
    numerator = jnp.einsum(
        "hqk,khd->hqd",
        weights.astype(jnp.bfloat16),
        value_block,
        preferred_element_type=jnp.float32,
    )
    sent = jnp.concatenate([numerator, jnp.broadcast_to(totals[..., None], numerator.shape)], -1)
    received = lax.ppermute(sent[:, row_count:], "row", flip_pairs(16, 8))
    combined = sent[:, :row_count] + received
    context = (combined[..., :HD] / combined[..., HD:]).astype(jnp.bfloat16)
    context = jnp.transpose(context, (1, 0, 2)).reshape(row_count, local_width)
    half_width = model_width // 2
    attn_part = jnp.einsum(
        "rk,kxn->xrn",
        context,
        w_out.reshape(local_width, 2, half_width),
        preferred_element_type=jnp.float32,
    ).astype(jnp.bfloat16)

    own_count = row_count // 4
    far, near = col_index // 4, lax.rem(col_index, 4)
    parts = lax.all_to_all(
        attn_part.reshape(8, own_count, half_width), "col", 0, 0, tiled=False
    )
    own_stream = lax.dynamic_slice(
        hidden, (near * own_count, far * half_width), (own_count, half_width)
    ).astype(jnp.float32)
    resid = own_stream + jnp.sum(parts.astype(jnp.float32), 0)
    average = jnp.sum(resid, -1, keepdims=True) / half_width
    centred = resid - average
    spread = jnp.sum(centred * centred, -1, keepdims=True)
    centred = centred.astype(jnp.bfloat16)
    centred = jnp.concatenate(
        [
            lax.dynamic_slice_in_dim(centred, lax.rem(near + shift, 4) * local_width, local_width, 1)
            for shift in (0, 3, 1, 2)
        ],
        1,
    )
    ones = jnp.ones((8, half_width), jnp.bfloat16)
    centred = jnp.concatenate([centred, ones], 0)
    mine = [
        jnp.dot(centred, block, preferred_element_type=jnp.float32)
        for block in (quarter, quarter_other)
    ]
    low = core == 0
    mine = jnp.concatenate(
        [jnp.where(low, mine[0], mine[1]), jnp.where(low, mine[1], mine[0])], 1
    )
    statistics = jnp.concatenate(
        [jnp.broadcast_to(average, (own_count, 64)), jnp.broadcast_to(spread, (own_count, 64))], 1
    )
    statistics = jnp.concatenate([statistics, jnp.zeros((8, 128), jnp.float32)], 0)
    mine = jnp.concatenate([mine, statistics], 1)
    theirs = lax.ppermute(mine, "col", flip_pairs(8, 4))
    width = half_columns * 2
    average, other_average = mine[:own_count, width : width + 1], theirs[:own_count, width : width + 1]
    spread = mine[:own_count, width + 64 : width + 65] + theirs[:own_count, width + 64 : width + 65]
    apart = 0.5 * (average - other_average)
    variance = (spread + model_width * apart * apart) / model_width
    column_sums = mine[own_count : own_count + 1, :width] - theirs[own_count : own_count + 1, :width]
    summed = mine[:own_count, :width] + theirs[:own_count, :width] + apart * column_sums
    lifted = jnp.maximum(summed * lax.rsqrt(variance + epsilon), 0.0).astype(jnp.bfloat16)
    single = jnp.dot(lifted, w_second, preferred_element_type=jnp.float32).astype(jnp.bfloat16)
    both = jnp.concatenate([w_left, w_right], 1)
    both = jnp.dot(single, both, preferred_element_type=jnp.float32).astype(jnp.bfloat16)
    both = lax.all_to_all(
        jnp.broadcast_to(both, (4,) + both.shape),
        "col",
        0,
        0,
        tiled=False,
        axis_index_groups=[[0, 1, 2, 3], [4, 5, 6, 7]],
    ).reshape(row_count, -1)
    channels = w_left.shape[1]
    left, right = both[:, :channels], both[:, channels:]
    first = lax.ppermute(right, ("row", "col"), right_pairs(0))
    second = lax.ppermute(right, ("row", "col"), right_pairs(1))
    upper = lax.axis_index("row") < 8
    column_right = jnp.concatenate(
        [jnp.where(upper, first, second), jnp.where(upper, second, first)], 0
    )
    return pair_stage(table_part, left, column_right, pair_gain, w_expand, w_contract)


def solution(mesh):
    in_specs = (
        P("row", None),
        P("row", "col"),
        P(),
        P(None, "col"),
        P(None, "col"),
        P(None, "col"),
        P("col", None),
        P("col"),
        P("col", None),
        P(),
        P(),
        P(),
        P(),
        P(),
        P(),
        P(),
    )
    out_specs = P("row", "col", None)
    return jax.shard_map(local, mesh=mesh, in_specs=in_specs, out_specs=out_specs, check_vma=False)
```

time: 204 us -> 117 us (0.57)
  the two profiles are of different devices: /device:TPU:96 before, /device:TPU:1 now
where the time goes in v2:
time: 117 us; the launch traced here: 115 us
  starting transfers between devices  36.9 us (32%)
  Pallas kernels  21.9 us (19%)
  waiting for transfers between devices  17.5 us (15%)
  matrix products  14.5 us (12%)
  other arithmetic  10.3 us (9%)
  blocking collectives  10.1 us (9%)
  local copies, waits for them, and re-layouts  3.24 us (3%)
    pallas_call x1, Pallas kernels, pair_stage(): pl.pallas_call(pair_kernel, grid=(rows // block,), in_specs=[pl.BlockSpec...  21.9 us
    all_to_all x1, blocking collectives, local(): lax.all_to_all(jnp.broadcast_to(both, (4,) + both.shape), 'col', 0, 0, ti...  10.1 us
    dot_general x1, matrix products, local(): jnp.einsum('ijb,bc->ijc', one_hot, rel_table, preferred_element_type=jnp....  6.74 us
    all_to_all x1, starting transfers between devices, local(): lax.all_to_all(attn_part.reshape(8, own_count, half_width), 'col', 0, 0,...  6.66 us
    ppermute x3, starting transfers between devices, local(): lax.ppermute(stacked, 'row', along_z(step))  5.97 us
    ppermute x3, waiting for transfers between devices, local(): lax.ppermute(stacked, 'row', along_z(step))  5.87 us
    ppermute x1, starting transfers between devices, local(): first = lax.ppermute(right, ('row', 'col'), right_pairs(0))  4.64 us
    ppermute x3, starting transfers between devices, local(): lax.ppermute(own_part, 'col', along_y(step))  4.46 us
  transfers between devices with their start and end apart: 14, of which 8 were waited for; matrix products, arithmetic and copies ran while one was open for 15% of the time, Pallas kernels for 0%

profile of v2, /device:TPU:1, one launch (start us, length us, event | category | flops | bytes accessed | tf_op | source)
XLA Modules:
  0.0 114.9 jit_solution(6183387230323977890)
XLA Ops:
  0.0 1.5 %convert_reduce_fusion = (f32[128]{0:T(128)S(1)}, f32[128]{0:T(128)S(1)}) fusion(bf16[128,2560]{1,0:T(8,128)(2,1)} %param.16), kind=kLoop, calls=%fused_computation.10 | loop fusion | flops 1310464 | bytes 656384 | tf_op jit(solution)/shard_map/reduce_sum | solution.py:18
  1.7 1.5 %fusion.8 = bf16[128,2560]{1,0:T(8,128)(2,1)S(1)} fusion(bf16[128,2560]{1,0:T(8,128)(2,1)} %param.16, f32[2560]{0:T(1024)} %param.18, f32[128]{0:T(128)S(1)} %get-tuple-element.42, f32[128]{0:T(128)S(1)} %get-tuple-element.41), kind=kLoop, calls=%fused_computation.15 | loop fusion | flops 1638400 | bytes 1321984 | tf_op jit(solution)/shard_map/convert_element_type | solution.py:127
  5.4 4.5 %collective-permute-start.3 = (bf16[128,640]{0,1:T(8,128)(2,1)S(1)}, bf16[128,640]{0,1:T(8,128)(2,1)S(1)}, u32[]{:S(2)}, u32[]{:S(2)}) collective-permute-start(bf16[128,640]{0,1:T(8,128)(2,1)S(1)} %pad_maximum_fusion.4), channel_id=1, source_target_pairs={{0,32},{8,40},{16,48},{24,56},{32,0},{40,8},{48,16},{56,24},{64,96... | collective-permute-start | bytes 491528 | tf_op jit(solution)/shard_map/ppermute | solution.py:134
  11.9 1.8 %collective-permute-done.3 = bf16[128,640]{0,1:T(8,128)(2,1)S(1)} collective-permute-done((bf16[128,640]{0,1:T(8,128)(2,1)S(1)}, bf16[128,640]{0,1:T(8,128)(2,1)S(1)}, u32[]{:S(2)}, u32[]{:S(2)}) %collective-permute-start.3) | collective-permute-done | bytes 163872 | tf_op jit(solution)/shard_map/ppermute | solution.py:134
  13.8 4.0 %collective-permute-done.2 = bf16[128,640]{0,1:T(8,128)(2,1)S(1)} collective-permute-done((bf16[128,640]{0,1:T(8,128)(2,1)S(1)}, bf16[128,640]{0,1:T(8,128)(2,1)S(1)}, u32[]{:S(2)}, u32[]{:S(2)}) %collective-permute-start.2) | collective-permute-done | bytes 163872 | tf_op jit(solution)/shard_map/ppermute | solution.py:134
  17.9 1.6 %collective-permute-start.4 = (bf16[512,640]{0,1:T(8,128)(2,1)S(1)}, bf16[512,640]{0,1:T(8,128)(2,1)S(1)}, u32[]{:S(2)}, u32[]{:S(2)}) collective-permute-start(bf16[512,640]{0,1:T(8,128)(2,1)S(1)} %pad_maximum_fusion.1), channel_id=1, source_target_pairs={{0,8},{8,0},{16,24},{24,16},{32,40},{40,32},{48,56},{56,48},{64,72... | collective-permute-start | bytes 1966088 | tf_op jit(solution)/shard_map/ppermute | solution.py:157
  19.5 1.3 %collective-permute-start = (bf16[128,320]{0,1:T(8,128)(2,1)S(1)}, bf16[128,320]{0,1:T(8,128)(2,1)S(1)}, u32[]{:S(2)}, u32[]{:S(2)}) collective-permute-start(bf16[128,320]{0,1:T(8,128)(2,1)S(1)} %fusion.20), channel_id=1, source_target_pairs={{0,64},{8,72},{16,80},{24,88},{32,96},{40,104},{48,112},{56,120},{... | collective-permute-start | bytes 245768 | tf_op jit(solution)/shard_map/ppermute | solution.py:139
  20.9 2.8 %collective-permute-done = bf16[128,320]{0,1:T(8,128)(2,1)S(1)} collective-permute-done((bf16[128,320]{0,1:T(8,128)(2,1)S(1)}, bf16[128,320]{0,1:T(8,128)(2,1)S(1)}, u32[]{:S(2)}, u32[]{:S(2)}) %collective-permute-start) | collective-permute-done | bytes 81952 | tf_op jit(solution)/shard_map/ppermute | solution.py:139
  28.1 1.2 %multiply_convert_fusion = bf16[320,512]{1,0:T(8,128)(2,1)S(1)} fusion(f32[320]{0:T(512)S(1)} %copy-done.13, bf16[320,1024]{1,0:T(8,128)(2,1)} %param.24, s32[]{:T(128)S(6)} %select_n.58), kind=kLoop, calls=%fused_computation.27 | loop fusion | flops 491520 | bytes 656644 | tf_op jit(solution)/shard_map/convert_element_type | solution.py:145
  29.3 3.0 %collective-permute-start.8 = (bf16[320,512]{1,0:T(8,128)(2,1)S(1)}, bf16[320,512]{1,0:T(8,128)(2,1)}, u32[]{:S(2)}, u32[]{:S(2)}) collective-permute-start(bf16[320,512]{1,0:T(8,128)(2,1)S(1)} %multiply_convert_fusion), channel_id=1, source_target_pairs={{0,2},{1,3},{2,0},{3,1},{4,6},{5,7},{6,4},{7,5},{8,10},{9,11},{10,... | collective-permute-start | bytes 983048 | tf_op jit(solution)/shard_map/ppermute | solution.py:146
  33.7 1.8 %collective-permute-done.5 = f32[5,128,128]{1,2,0:T(8,128)S(1)} collective-permute-done((f32[5,128,128]{1,2,0:T(8,128)}, f32[5,128,128]{1,2,0:T(8,128)S(1)}, u32[]{:S(2)}, u32[]{:S(2)}) %collective-permute-start.5) | collective-permute-done | bytes 327712 | tf_op jit(solution)/shard_map/ppermute | solution.py:172
  35.7 1.4 %convolution_convert_fusion = bf16[128,2,1280]{2,0,1:T(8,128)(2,1)} fusion(bf16[128,320,1]{0,1,2:T(8,128)(2,1)S(1)} %bitcast.76, bf16[40,2,8,1280]{3,2,1,0:T(8,128)(2,1)S(1)} %bitcast.72), kind=kOutput, calls=%fused_computation.7 | convolution fusion | flops 210042880 | bytes 2375680 | tf_op jit(solution)/shard_map/rk,kxn->xrn/dot_general | solution.py:177
  37.0 6.7 %all-to-all-start = ((bf16[8,32,1280]{2,1,0:T(8,128)(2,1)}), bf16[8,32,1280]{2,1,0:T(8,128)(2,1)}, u32[]{:S(2)}, u32[]{:S(2)}) async-start(bf16[8,32,1280]{2,1,0:T(8,128)(2,1)} %bitcast.13), calls=%async_computation | async-start | bytes 1310720 | tf_op jit(solution)/shard_map/all_to_all | solution.py:186
  43.7 3.1 %collective-permute-done.7 = bf16[320,512]{1,0:T(8,128)(2,1)} collective-permute-done((bf16[320,512]{1,0:T(8,128)(2,1)S(1)}, bf16[320,512]{1,0:T(8,128)(2,1)}, u32[]{:S(2)}, u32[]{:S(2)}) %collective-permute-start.7) | collective-permute-done | bytes 327712 | tf_op jit(solution)/shard_map/ppermute | solution.py:146
  47.6 1.4 %pad_maximum_fusion = bf16[1280,512]{1,0:T(8,128)(2,1)S(1)} fusion(bf16[320,512]{1,0:T(8,128)(2,1)} %collective-permute-done.8, bf16[320,512]{1,0:T(8,128)(2,1)} %collective-permute-done.7, bf16[320,512]{1,0:T(8,128)(2,1)} %collective-permute-done.6, bf16[320,512]{1,0:T(8,128)(2,1)} %copy-done.8), kind=kLoop, calls=%fused_computation.17 | loop fusion | flops 5242880 | bytes 2621440 | tf_op jit(solution)/shard_map/concatenate | solution.py:147
  49.0 4.0 %collective-permute-start.9 = (bf16[1280,512]{1,0:T(8,128)(2,1)S(1)}, bf16[1280,512]{1,0:T(8,128)(2,1)}, u32[]{:S(2)}, u32[]{:S(2)}) collective-permute-start(bf16[1280,512]{1,0:T(8,128)(2,1)S(1)} %pad_maximum_fusion), channel_id=1, source_target_pairs={{0,8},{8,0},{16,24},{24,16},{32,40},{40,32},{48,56},{56,48},{64,72... | collective-permute-start | bytes 3932168 | tf_op jit(solution)/shard_map/ppermute | solution.py:148
  58.6 1.7 %broadcast_select_fusion = (f32[40,512]{1,0:T(8,128)S(1)}, f32[40,512]{1,0:T(8,128)S(1)}) fusion(f32[40,512]{1,0:T(8,128)S(1)} %fusion.30, pred[]{:T(512)S(6)} %eq.19, bf16[1280,512]{1,0:T(8,128)(2,1)} %collective-permute-done.9, bf16[32,1280]{1,0:T(8,128)(2,1)S(1)} %concatenate.70), kind=kOutput, calls=%fused_computation.70 | convolution fusion | flops 52469760 | bytes 1638401 | tf_op jit(solution)/shard_map/dot_general | solution.py:207
  60.3 3.9 %collective-permute-start.10 = (f32[40,1152]{1,0:T(8,128)S(1)}, f32[40,1152]{1,0:T(8,128)S(1)}, u32[]{:S(2)}, u32[]{:S(2)}) collective-permute-start(f32[40,1152]{1,0:T(8,128)S(1)} %pad_maximum_fusion.3), channel_id=1, source_target_pairs={{0,4},{1,5},{2,6},{3,7},{4,0},{5,1},{6,2},{7,3},{8,12},{9,13},{10,... | collective-permute-start | bytes 552968 | tf_op jit(solution)/shard_map/ppermute | solution.py:219
  64.3 2.9 %collective-permute-done.10 = f32[40,1152]{1,0:T(8,128)S(1)} collective-permute-done((f32[40,1152]{1,0:T(8,128)S(1)}, f32[40,1152]{1,0:T(8,128)S(1)}, u32[]{:S(2)}, u32[]{:S(2)}) %collective-permute-start.10) | collective-permute-done | bytes 184352 | tf_op jit(solution)/shard_map/ppermute | solution.py:219
  68.2 10.1 %all_to_all.10 = bf16[4,32,256]{2,1,0:T(8,128)(2,1)S(1)} all-to-all(bf16[4,32,256]{2,1,0:T(8,128)(2,1)S(1)} %broadcast_in_dim.11), channel_id=1, replica_groups={{0,1,2,3},{4,5,6,7},{8,9,10,11},{12,13,14,15},{16,17,18,19},{20,21,22,2..., dimensions={0} | all-to-all | bytes 131072 | tf_op jit(solution)/shard_map/all_to_all | solution.py:231
  78.4 3.2 %collective-permute-start.12 = (bf16[128,128]{1,0:T(8,128)(2,1)S(1)}, bf16[128,128]{1,0:T(8,128)(2,1)S(1)}, u32[]{:S(2)}, u32[]{:S(2)}) collective-permute-start(bf16[128,128]{1,0:T(8,128)(2,1)S(1)} %get-tuple-element.35), channel_id=1, source_target_pairs={{8,0},{24,1},{40,2},{56,3},{72,4},{88,5},{104,6},{120,7},{9,8},{25... | collective-permute-start | bytes 98312 | tf_op jit(solution)/shard_map/ppermute | solution.py:242
  81.5 4.6 %collective-permute-start.11 = (bf16[128,128]{1,0:T(8,128)(2,1)S(1)}, bf16[128,128]{1,0:T(8,128)(2,1)S(1)}, u32[]{:S(2)}, u32[]{:S(2)}) collective-permute-start(bf16[128,128]{1,0:T(8,128)(2,1)S(1)} %get-tuple-element.35), channel_id=1, source_target_pairs={{0,0},{16,1},{32,2},{48,3},{64,4},{80,5},{96,6},{112,7},{1,8},{17,... | collective-permute-start | bytes 98312 | tf_op jit(solution)/shard_map/ppermute | solution.py:241
  86.2 6.7 %fusion.1.table_ref = bf16[128,256,128]{2,1,0:T(8,128)(2,1)} fusion(s32[128,256]{1,0:T(8,128)S(1)} %copy-done.9, bf16[65,128]{1,0:T(8,128)(2,1)S(1)} %copy-done.12), kind=kOutput, calls=%fused_computation.2 | convolution fusion | flops 551583744 | bytes 8536320 | tf_op jit(solution)/shard_map/ijb,bc->ijc/dot_general | solution.py:152
  93.0 21.9 %pair.1 = bf16[128,256,128]{2,1,0:T(8,128)(2,1)} custom-call(bf16[128,256,128]{2,1,0:T(8,128)(2,1)} %fusion.1.table_ref, f32[128,128]{1,0:T(8,128)S(1)} %get-tuple-element.36.left_ref, f32[256,128]{1,0:T(8,128)S(1)} %maximum_convert_fusion.right_ref, f32[1,128]{1,0:T(1,128)S(1)} %bitcast.69, bf16[128,512]{1,0:T(8,128)(2,1)S(1)} %copy-done.1, ...), custom_call_target="tpu_custom_call" | custom-call | tf_op jit(solution)/shard_map/pair/pallas_call | solution.py:88
  (91 shorter events, 17.7 us)
Async XLA Ops:
  0.0 67.5 %copy-start = (bf16[1024,1024]{1,0:T(8,128)(2,1)S(1)}, bf16[1024,1024]{1,0:T(8,128)(2,1)}, u32[]{:S(2)}) copy-start(bf16[1024,1024]{1,0:T(8,128)(2,1)} %param.25) | copy-start | bytes 6291460
  5.4 8.4 %collective-permute-start.3 = (bf16[128,640]{0,1:T(8,128)(2,1)S(1)}, bf16[128,640]{0,1:T(8,128)(2,1)S(1)}, u32[]{:S(2)}, u32[]{:S(2)}) collective-permute-start(bf16[128,640]{0,1:T(8,128)(2,1)S(1)} %pad_maximum_fusion.4), channel_id=1, source_target_pairs={{0,32},{8,40},{16,48},{24,56},{32,0},{40,8},{48,16},{56,24},{64,96... | collective-permute-start | bytes 491528 | tf_op jit(solution)/shard_map/ppermute | solution.py:134
  9.9 7.9 %collective-permute-start.2 = (bf16[128,640]{0,1:T(8,128)(2,1)S(1)}, bf16[128,640]{0,1:T(8,128)(2,1)S(1)}, u32[]{:S(2)}, u32[]{:S(2)}) collective-permute-start(bf16[128,640]{0,1:T(8,128)(2,1)S(1)} %pad_maximum_fusion.4), channel_id=1, source_target_pairs={{0,48},{8,56},{16,0},{24,8},{32,16},{40,24},{48,32},{56,40},{64,11... | collective-permute-start | bytes 491528 | tf_op jit(solution)/shard_map/ppermute | solution.py:134
  10.3 7.5 %collective-permute-start.1 = (bf16[128,640]{0,1:T(8,128)(2,1)S(1)}, bf16[128,640]{0,1:T(8,128)(2,1)S(1)}, u32[]{:S(2)}, u32[]{:S(2)}) collective-permute-start(bf16[128,640]{0,1:T(8,128)(2,1)S(1)} %pad_maximum_fusion.4), channel_id=1, source_target_pairs={{0,16},{8,24},{16,32},{24,40},{32,48},{40,56},{48,0},{56,8},{64,80... | collective-permute-start | bytes 491528 | tf_op jit(solution)/shard_map/ppermute | solution.py:134
  17.9 6.0 %collective-permute-start.4 = (bf16[512,640]{0,1:T(8,128)(2,1)S(1)}, bf16[512,640]{0,1:T(8,128)(2,1)S(1)}, u32[]{:S(2)}, u32[]{:S(2)}) collective-permute-start(bf16[512,640]{0,1:T(8,128)(2,1)S(1)} %pad_maximum_fusion.1), channel_id=1, source_target_pairs={{0,8},{8,0},{16,24},{24,16},{32,40},{40,32},{48,56},{56,48},{64,72... | collective-permute-start | bytes 1966088 | tf_op jit(solution)/shard_map/ppermute | solution.py:157
  19.5 4.1 %collective-permute-start = (bf16[128,320]{0,1:T(8,128)(2,1)S(1)}, bf16[128,320]{0,1:T(8,128)(2,1)S(1)}, u32[]{:S(2)}, u32[]{:S(2)}) collective-permute-start(bf16[128,320]{0,1:T(8,128)(2,1)S(1)} %fusion.20), channel_id=1, source_target_pairs={{0,64},{8,72},{16,80},{24,88},{32,96},{40,104},{48,112},{56,120},{... | collective-permute-start | bytes 245768 | tf_op jit(solution)/shard_map/ppermute | solution.py:139
  26.8 8.8 %collective-permute-start.5 = (f32[5,128,128]{1,2,0:T(8,128)}, f32[5,128,128]{1,2,0:T(8,128)S(1)}, u32[]{:S(2)}, u32[]{:S(2)}) collective-permute-start(f32[5,128,128]{1,2,0:T(8,128)} %pad_maximum_fusion.2), channel_id=1, source_target_pairs={{0,64},{8,72},{16,80},{24,88},{32,96},{40,104},{48,112},{56,120},{... | collective-permute-start | bytes 983048 | tf_op jit(solution)/shard_map/ppermute | solution.py:172
  28.1 7.6 %copy-start.7 = (bf16[320,2560]{1,0:T(8,128)(2,1)S(1)}, bf16[320,2560]{1,0:T(8,128)(2,1)}, u32[]{:S(2)}) copy-start(bf16[320,2560]{1,0:T(8,128)(2,1)} %param.22) | copy-start | bytes 4915204
  29.3 7.8 %copy-start.8 = (bf16[320,512]{1,0:T(8,128)(2,1)}, bf16[320,512]{1,0:T(8,128)(2,1)S(1)}, u32[]{:S(2)}) copy-start(bf16[320,512]{1,0:T(8,128)(2,1)S(1)} %multiply_convert_fusion) | copy-start | bytes 983044
  29.3 14.4 %collective-permute-start.8 = (bf16[320,512]{1,0:T(8,128)(2,1)S(1)}, bf16[320,512]{1,0:T(8,128)(2,1)}, u32[]{:S(2)}, u32[]{:S(2)}) collective-permute-start(bf16[320,512]{1,0:T(8,128)(2,1)S(1)} %multiply_convert_fusion), channel_id=1, source_target_pairs={{0,2},{1,3},{2,0},{3,1},{4,6},{5,7},{6,4},{7,5},{8,10},{9,11},{10,... | collective-permute-start | bytes 983048 | tf_op jit(solution)/shard_map/ppermute | solution.py:146
  32.3 14.6 %collective-permute-start.7 = (bf16[320,512]{1,0:T(8,128)(2,1)S(1)}, bf16[320,512]{1,0:T(8,128)(2,1)}, u32[]{:S(2)}, u32[]{:S(2)}) collective-permute-start(bf16[320,512]{1,0:T(8,128)(2,1)S(1)} %multiply_convert_fusion), channel_id=1, source_target_pairs={{0,3},{1,0},{2,1},{3,2},{4,7},{5,4},{6,5},{7,6},{8,11},{9,8},{10,9... | collective-permute-start | bytes 983048 | tf_op jit(solution)/shard_map/ppermute | solution.py:146
  33.1 14.6 %collective-permute-start.6 = (bf16[320,512]{1,0:T(8,128)(2,1)S(1)}, bf16[320,512]{1,0:T(8,128)(2,1)}, u32[]{:S(2)}, u32[]{:S(2)}) collective-permute-start(bf16[320,512]{1,0:T(8,128)(2,1)S(1)} %multiply_convert_fusion), channel_id=1, source_target_pairs={{0,1},{1,2},{2,3},{3,0},{4,5},{5,6},{6,7},{7,4},{8,9},{9,10},{10,1... | collective-permute-start | bytes 983048 | tf_op jit(solution)/shard_map/ppermute | solution.py:146
  37.0 16.1 %all-to-all-start = ((bf16[8,32,1280]{2,1,0:T(8,128)(2,1)}), bf16[8,32,1280]{2,1,0:T(8,128)(2,1)}, u32[]{:S(2)}, u32[]{:S(2)}) async-start(bf16[8,32,1280]{2,1,0:T(8,128)(2,1)} %bitcast.13), calls=%async_computation | async-start | bytes 1310720 | tf_op jit(solution)/shard_map/all_to_all | solution.py:186
  49.0 9.6 %collective-permute-start.9 = (bf16[1280,512]{1,0:T(8,128)(2,1)S(1)}, bf16[1280,512]{1,0:T(8,128)(2,1)}, u32[]{:S(2)}, u32[]{:S(2)}) collective-permute-start(bf16[1280,512]{1,0:T(8,128)(2,1)S(1)} %pad_maximum_fusion), channel_id=1, source_target_pairs={{0,8},{8,0},{16,24},{24,16},{32,40},{40,32},{48,56},{56,48},{64,72... | collective-permute-start | bytes 3932168 | tf_op jit(solution)/shard_map/ppermute | solution.py:148
  58.6 8.9 %copy-start.10 = (bf16[1024,128]{1,0:T(8,128)(2,1)S(1)}, bf16[1024,128]{1,0:T(8,128)(2,1)}, u32[]{:S(2)}) copy-start(bf16[1024,128]{1,0:T(8,128)(2,1)} %param.27) | copy-start | bytes 786436
  58.6 8.9 %copy-start.11 = (bf16[1024,128]{1,0:T(8,128)(2,1)S(1)}, bf16[1024,128]{1,0:T(8,128)(2,1)}, u32[]{:S(2)}) copy-start(bf16[1024,128]{1,0:T(8,128)(2,1)} %param.26) | copy-start | bytes 786436
  60.3 6.9 %collective-permute-start.10 = (f32[40,1152]{1,0:T(8,128)S(1)}, f32[40,1152]{1,0:T(8,128)S(1)}, u32[]{:S(2)}, u32[]{:S(2)}) collective-permute-start(f32[40,1152]{1,0:T(8,128)S(1)} %pad_maximum_fusion.3), channel_id=1, source_target_pairs={{0,4},{1,5},{2,6},{3,7},{4,0},{5,1},{6,2},{7,3},{8,12},{9,13},{10,... | collective-permute-start | bytes 552968 | tf_op jit(solution)/shard_map/ppermute | solution.py:219
  67.5 18.7 %copy-start.9 = (s32[128,256]{1,0:T(8,128)S(1)}, s32[128,256]{1,0:T(8,128)}, u32[]{:S(2)}) copy-start(s32[128,256]{1,0:T(8,128)} %param.17) | copy-start | bytes 393220
  67.5 18.7 %copy-start.12 = (bf16[65,128]{1,0:T(8,128)(2,1)S(1)}, bf16[65,128]{1,0:T(8,128)(2,1)}, u32[]{:S(2)}) copy-start(bf16[65,128]{1,0:T(8,128)(2,1)} %param.28) | copy-start | bytes 49924
  78.3 14.6 %copy-start.1 = (bf16[128,512]{1,0:T(8,128)(2,1)S(1)}, bf16[128,512]{1,0:T(8,128)(2,1)}, u32[]{:S(2)}) copy-start(bf16[128,512]{1,0:T(8,128)(2,1)} %expand_ref.1) | copy-start | bytes 393220
  78.4 14.6 %copy-start.2 = (bf16[512,128]{1,0:T(8,128)(2,1)S(1)}, bf16[512,128]{1,0:T(8,128)(2,1)}, u32[]{:S(2)}) copy-start(bf16[512,128]{1,0:T(8,128)(2,1)} %contract_ref.1) | copy-start | bytes 393220
  78.4 14.6 %copy-start.3 = (f32[128]{0:T(128)S(1)}, f32[128]{0:T(128)}, u32[]{:S(2)}) copy-start(f32[128]{0:T(128)} %param.29) | copy-start | bytes 1540
  78.4 14.6 %collective-permute-start.12 = (bf16[128,128]{1,0:T(8,128)(2,1)S(1)}, bf16[128,128]{1,0:T(8,128)(2,1)S(1)}, u32[]{:S(2)}, u32[]{:S(2)}) collective-permute-start(bf16[128,128]{1,0:T(8,128)(2,1)S(1)} %get-tuple-element.35), channel_id=1, source_target_pairs={{8,0},{24,1},{40,2},{56,3},{72,4},{88,5},{104,6},{120,7},{9,8},{25... | collective-permute-start | bytes 98312 | tf_op jit(solution)/shard_map/ppermute | solution.py:242
  81.5 11.4 %collective-permute-start.11 = (bf16[128,128]{1,0:T(8,128)(2,1)S(1)}, bf16[128,128]{1,0:T(8,128)(2,1)S(1)}, u32[]{:S(2)}, u32[]{:S(2)}) collective-permute-start(bf16[128,128]{1,0:T(8,128)(2,1)S(1)} %get-tuple-element.35), channel_id=1, source_target_pairs={{0,0},{16,1},{32,2},{48,3},{64,4},{80,5},{96,6},{112,7},{1,8},{17,... | collective-permute-start | bytes 98312 | tf_op jit(solution)/shard_map/ppermute | solution.py:241
  (4 other events, 13.3 us)

commit v3 on v2

--- a/solution.py
+++ b/solution.py
@@ -98,6 +98,89 @@
         compiler_params=pltpu.CompilerParams(vmem_limit_bytes=48 << 20),
         name="pair",
     )(table_part, left, *fixed)
+
+
+def half_sums_kernel(
+    place_ref, parts_ref, stream_ref, own_ref, other_ref, mine_ref, sent_ref, blocks_ref
+):
+    near, core = place_ref[0], place_ref[2]
+    rows, features = stream_ref.shape
+    local_width = features // 4
+    half_columns = own_ref.shape[1]
+    resid = stream_ref[...].astype(jnp.float32)
+    for part in range(parts_ref.shape[0]):
+        resid += parts_ref[part].astype(jnp.float32)
+    average = jnp.sum(resid, -1, keepdims=True) / features
+    centred = resid - average
+    spread = jnp.sum(centred * centred, -1, keepdims=True)
+    centred = centred.astype(jnp.bfloat16)
+    for block in range(4):
+        blocks_ref[block, :rows, :] = centred[:, block * local_width : (block + 1) * local_width]
+        blocks_ref[block, rows:, :] = jnp.ones((16, local_width), jnp.bfloat16)
+    line = lax.broadcasted_iota(jnp.int32, (16, half_columns), 0)
+    for ref, side in ((own_ref, core), (other_ref, 1 - core)):
+        total = jnp.zeros((rows + 16, half_columns), jnp.float32)
+        for position, shift in enumerate((0, 3, 1, 2)):
+            total += jnp.dot(
+                blocks_ref[lax.rem(near + shift, 4)],
+                ref[position * local_width : (position + 1) * local_width, :],
+                preferred_element_type=jnp.float32,
+            )
+        columns = pl.ds(pl.multiple_of(side * half_columns, half_columns), half_columns)
+        mine_ref[:, columns] = total
+        sums = total[rows:]
+        high = sums.astype(jnp.bfloat16).astype(jnp.float32)
+        sums = jnp.where(line == 0, high, jnp.where(line == 1, sums - high, 0.0))
+        sent_ref[:rows, columns] = total[:rows].astype(jnp.bfloat16)
+        sent_ref[rows:, columns] = sums.astype(jnp.bfloat16)
+    lane = lax.broadcasted_iota(jnp.int32, (rows, 128), 1)
+    width = half_columns * 2
+    mine_ref[:rows, width:] = jnp.where(lane < 2, average, spread)
+    mine_ref[rows:, width:] = jnp.zeros((16, 128), jnp.float32)
+    high_average = average.astype(jnp.bfloat16).astype(jnp.float32)
+    high_spread = spread.astype(jnp.bfloat16).astype(jnp.float32)
+    terms = jnp.where(
+        lane == 0,
+        high_average,
+        jnp.where(
+            lane == 1,
+            average - high_average,
+            jnp.where(lane == 2, high_spread, spread - high_spread),
+        ),
+    )
+    sent_ref[:rows, width:] = terms.astype(jnp.bfloat16)
+    sent_ref[rows:, width:] = jnp.zeros((16, 128), jnp.bfloat16)
+
+
+def half_sums(place, parts, hidden, own, other):
+    rows, features = parts.shape[1:]
+    width = own.shape[1] * 2 + 128
+
+    def fixed(array):
+        return pl.BlockSpec(array.shape, lambda step, place: (0,) * array.ndim)
+
+    spec = pl.BlockSpec((rows + 16, width), lambda step, place: (0, 0))
+    return pl.pallas_call(
+        half_sums_kernel,
+        grid_spec=pltpu.PrefetchScalarGridSpec(
+            num_scalar_prefetch=1,
+            grid=(1,),
+            in_specs=[
+                fixed(parts),
+                pl.BlockSpec((rows, features), lambda step, place: (place[0], place[1])),
+                fixed(own),
+                fixed(other),
+            ],
+            out_specs=[spec, spec],
+            scratch_shapes=[pltpu.VMEM((4, rows + 16, features // 4), jnp.bfloat16)],
+        ),
+        out_shape=[
+            jax.ShapeDtypeStruct((rows + 16, width), jnp.float32),
+            jax.ShapeDtypeStruct((rows + 16, width), jnp.bfloat16),
+        ],
+        compiler_params=pltpu.CompilerParams(vmem_limit_bytes=24 << 20),
+        name="half_sums",
+    )(place, parts, hidden, own, other)
 
 
 def local(
@@ -168,11 +251,23 @@
         value_block,
         preferred_element_type=jnp.float32,
     )
-    sent = jnp.concatenate([numerator, jnp.broadcast_to(totals[..., None], numerator.shape)], -1)
-    received = lax.ppermute(sent[:, row_count:], "row", flip_pairs(16, 8))
-    combined = sent[:, :row_count] + received
-    context = (combined[..., :HD] / combined[..., HD:]).astype(jnp.bfloat16)
-    context = jnp.transpose(context, (1, 0, 2)).reshape(row_count, local_width)
+    sent_totals = jnp.transpose(totals[:, row_count:])
+    high = lax.reduce_precision(sent_totals, 8, 7)
+    sent = jnp.concatenate(
+        [
+            jnp.transpose(numerator[:, row_count:], (1, 0, 2)).reshape(row_count, local_width),
+            jnp.pad(high, ((0, 0), (0, 32 - local_heads))),
+            jnp.pad(sent_totals - high, ((0, 0), (0, 32 - local_heads))),
+        ],
+        1,
+    ).astype(jnp.bfloat16)
+    received = lax.ppermute(sent, "row", flip_pairs(16, 8)).astype(jnp.float32)
+    other_totals = received[:, local_width : local_width + local_heads]
+    other_totals += received[:, local_width + 32 : local_width + 32 + local_heads]
+    totals = jnp.transpose(totals[:, :row_count]) + other_totals
+    numerator = jnp.transpose(numerator[:, :row_count], (1, 0, 2))
+    numerator += received[:, :local_width].reshape(row_count, local_heads, HD)
+    context = (numerator / totals[..., None]).astype(jnp.bfloat16).reshape(row_count, local_width)
     half_width = model_width // 2
     attn_part = jnp.einsum(
         "rk,kxn->xrn",
@@ -186,43 +281,19 @@
     parts = lax.all_to_all(
         attn_part.reshape(8, own_count, half_width), "col", 0, 0, tiled=False
     )
-    own_stream = lax.dynamic_slice(
-        hidden, (near * own_count, far * half_width), (own_count, half_width)
-    ).astype(jnp.float32)
-    resid = own_stream + jnp.sum(parts.astype(jnp.float32), 0)
-    average = jnp.sum(resid, -1, keepdims=True) / half_width
-    centred = resid - average
-    spread = jnp.sum(centred * centred, -1, keepdims=True)
-    centred = centred.astype(jnp.bfloat16)
-    centred = jnp.concatenate(
-        [
-            lax.dynamic_slice_in_dim(centred, lax.rem(near + shift, 4) * local_width, local_width, 1)
-            for shift in (0, 3, 1, 2)
-        ],
-        1,
-    )
-    ones = jnp.ones((8, half_width), jnp.bfloat16)
-    centred = jnp.concatenate([centred, ones], 0)
-    mine = [
-        jnp.dot(centred, block, preferred_element_type=jnp.float32)
-        for block in (quarter, quarter_other)
-    ]
-    low = core == 0
-    mine = jnp.concatenate(
-        [jnp.where(low, mine[0], mine[1]), jnp.where(low, mine[1], mine[0])], 1
-    )
-    statistics = jnp.concatenate(
-        [jnp.broadcast_to(average, (own_count, 64)), jnp.broadcast_to(spread, (own_count, 64))], 1
-    )
-    statistics = jnp.concatenate([statistics, jnp.zeros((8, 128), jnp.float32)], 0)
-    mine = jnp.concatenate([mine, statistics], 1)
-    theirs = lax.ppermute(mine, "col", flip_pairs(8, 4))
+    parts, table_part = lax.optimization_barrier((parts, table_part))
+    place = jnp.stack([near, far, core]).astype(jnp.int32)
+    mine, sent = half_sums(place, parts, hidden, quarter, quarter_other)
+    theirs = lax.ppermute(sent, "col", flip_pairs(8, 4)).astype(jnp.float32)
     width = half_columns * 2
-    average, other_average = mine[:own_count, width : width + 1], theirs[:own_count, width : width + 1]
-    spread = mine[:own_count, width + 64 : width + 65] + theirs[:own_count, width + 64 : width + 65]
+    other_average = theirs[:own_count, width : width + 1] + theirs[:own_count, width + 1 : width + 2]
+    other_spread = theirs[:own_count, width + 2 : width + 3] + theirs[:own_count, width + 3 : width + 4]
+    average, spread = mine[:own_count, width : width + 1], mine[:own_count, width + 2 : width + 3]
     apart = 0.5 * (average - other_average)
-    variance = (spread + model_width * apart * apart) / model_width
-    column_sums = mine[own_count : own_count + 1, :width] - theirs[own_count : own_count + 1, :width]
+    variance = (spread + other_spread + model_width * apart * apart) / model_width
+    column_sums = mine[own_count : own_count + 1, :width] - (
+        theirs[own_count : own_count + 1, :width] + theirs[own_count + 1 : own_count + 2, :width]
+    )
     summed = mine[:own_count, :width] + theirs[:own_count, :width] + apart * column_sums
     lifted = jnp.maximum(summed * lax.rsqrt(variance + epsilon), 0.0).astype(jnp.bfloat16)
     single = jnp.dot(lifted, w_second, preferred_element_type=jnp.float32).astype(jnp.bfloat16)

time: 117 us -> 114 us (0.974)
  the two profiles are of different devices: /device:TPU:1 before, /device:TPU:22 now
where the time goes in v3:
time: 114 us
  starting transfers between devices  29.6 us (26%)
  waiting for transfers between devices  28.1 us (25%)
  Pallas kernels  24.9 us (22%)
  matrix products  15.9 us (14%)
  blocking collectives  8.29 us (7%)
  other arithmetic  5.9 us (5%)
    pallas_call x1, Pallas kernels, pair_stage(): pl.pallas_call(pair_kernel, grid=(rows // block,), in_specs=[pl.BlockSpec...  21.8 us
    all_to_all x1, blocking collectives, local(): lax.all_to_all(jnp.broadcast_to(both, (4,) + both.shape), 'col', 0, 0, ti...  8.29 us
    ppermute x3, waiting for transfers between devices, local(): lax.ppermute(own_part, 'col', along_y(step))  8.08 us
    dot_general x1, matrix products, local(): jnp.einsum('ijb,bc->ijc', one_hot, rel_table, preferred_element_type=jnp....  7.53 us
    all_to_all x1, starting transfers between devices, local(): lax.all_to_all(attn_part.reshape(8, own_count, half_width), 'col', 0, 0,...  7.21 us
    ppermute x3, starting transfers between devices, local(): lax.ppermute(stacked, 'row', along_z(step))  5.99 us
    ppermute x1, waiting for transfers between devices, local(): first = lax.ppermute(right, ('row', 'col'), right_pairs(0))  5.86 us
    ppermute x1, starting transfers between devices, local(): second = lax.ppermute(right, ('row', 'col'), right_pairs(1))  4.84 us
  transfers between devices with their start and end apart: 14, of which 10 were waited for; matrix products, arithmetic and copies ran while one was open for 14% of the time, Pallas kernels for 0%

profile of v3, /device:TPU:22, one launch (start us, length us, event | category | flops | bytes accessed | tf_op | source)
XLA Modules:
  0.0 113.7 jit_solution(4826850980375091444)
XLA Ops:
  0.0 1.5 %convert_reduce_fusion = (f32[128]{0:T(128)S(1)}, f32[128]{0:T(128)S(1)}) fusion(bf16[128,2560]{1,0:T(8,128)(2,1)} %stream_ref.1), kind=kLoop, calls=%fused_computation.10 | loop fusion | flops 1310464 | bytes 656384 | tf_op jit(solution)/shard_map/reduce_sum | solution.py:18
  1.7 1.6 %fusion.8 = bf16[128,2560]{1,0:T(8,128)(2,1)S(1)} fusion(bf16[128,2560]{1,0:T(8,128)(2,1)} %stream_ref.1, f32[2560]{0:T(1024)} %param.18, f32[128]{0:T(128)S(1)} %get-tuple-element.42, f32[128]{0:T(128)S(1)} %get-tuple-element.41), kind=kLoop, calls=%fused_computation.15 | loop fusion | flops 1638400 | bytes 1321984 | tf_op jit(solution)/shard_map/convert_element_type | solution.py:210
  4.7 4.0 %collective-permute-start.3 = (bf16[128,640]{0,1:T(8,128)(2,1)S(1)}, bf16[128,640]{0,1:T(8,128)(2,1)S(1)}, u32[]{:S(2)}, u32[]{:S(2)}) collective-permute-start(bf16[128,640]{0,1:T(8,128)(2,1)S(1)} %pad_maximum_fusion.2), channel_id=1, source_target_pairs={{0,32},{8,40},{16,48},{24,56},{32,0},{40,8},{48,16},{56,24},{64,96... | collective-permute-start | bytes 491528 | tf_op jit(solution)/shard_map/ppermute | solution.py:217
  9.3 1.3 %collective-permute-start.1 = (bf16[128,640]{0,1:T(8,128)(2,1)S(1)}, bf16[128,640]{0,1:T(8,128)(2,1)S(1)}, u32[]{:S(2)}, u32[]{:S(2)}) collective-permute-start(bf16[128,640]{0,1:T(8,128)(2,1)S(1)} %pad_maximum_fusion.2), channel_id=1, source_target_pairs={{0,16},{8,24},{16,32},{24,40},{32,48},{40,56},{48,0},{56,8},{64,80... | collective-permute-start | bytes 491528 | tf_op jit(solution)/shard_map/ppermute | solution.py:217
  10.7 2.0 %convolution_multiply_fusion = f32[128,320]{0,1:T(8,128)S(1)} fusion(bf16[128,2560]{1,0:T(8,128)(2,1)S(1)} %fusion.8, bf16[2560,320]{0,1:T(8,128)(2,1)} %param.19), kind=kOutput, calls=%fused_computation.18 | convolution fusion | flops 209756160 | bytes 2457600 | tf_op jit(solution)/shard_map/dot_general | solution.py:218
  13.7 3.5 %collective-permute-done.2 = bf16[128,640]{0,1:T(8,128)(2,1)S(1)} collective-permute-done((bf16[128,640]{0,1:T(8,128)(2,1)S(1)}, bf16[128,640]{0,1:T(8,128)(2,1)S(1)}, u32[]{:S(2)}, u32[]{:S(2)}) %collective-permute-start.2) | collective-permute-done | bytes 163872 | tf_op jit(solution)/shard_map/ppermute | solution.py:217
  18.5 2.4 %collective-permute-start.7 = (bf16[320,512]{1,0:T(8,128)(2,1)S(1)}, bf16[320,512]{1,0:T(8,128)(2,1)S(1)}, u32[]{:S(2)}, u32[]{:S(2)}) collective-permute-start(bf16[320,512]{1,0:T(8,128)(2,1)S(1)} %multiply_convert_fusion), channel_id=1, source_target_pairs={{0,3},{1,0},{2,1},{3,2},{4,7},{5,4},{6,5},{7,6},{8,11},{9,8},{10,9... | collective-permute-start | bytes 983048 | tf_op jit(solution)/shard_map/ppermute | solution.py:229
  21.8 3.6 %collective-permute-done = bf16[128,320]{0,1:T(8,128)(2,1)S(1)} collective-permute-done((bf16[128,320]{0,1:T(8,128)(2,1)S(1)}, bf16[128,320]{0,1:T(8,128)(2,1)S(1)}, u32[]{:S(2)}, u32[]{:S(2)}) %collective-permute-start) | collective-permute-done | bytes 81952 | tf_op jit(solution)/shard_map/ppermute | solution.py:222
  28.7 1.5 %collective-permute-done.8 = bf16[320,512]{1,0:T(8,128)(2,1)S(1)} collective-permute-done((bf16[320,512]{1,0:T(8,128)(2,1)S(1)}, bf16[320,512]{1,0:T(8,128)(2,1)S(1)}, u32[]{:S(2)}, u32[]{:S(2)}) %collective-permute-start.8) | collective-permute-done | bytes 327712 | tf_op jit(solution)/shard_map/ppermute | solution.py:229
  30.2 5.6 %collective-permute-done.7 = bf16[320,512]{1,0:T(8,128)(2,1)S(1)} collective-permute-done((bf16[320,512]{1,0:T(8,128)(2,1)S(1)}, bf16[320,512]{1,0:T(8,128)(2,1)S(1)}, u32[]{:S(2)}, u32[]{:S(2)}) %collective-permute-start.7) | collective-permute-done | bytes 327712 | tf_op jit(solution)/shard_map/ppermute | solution.py:229
  36.8 1.1 %pad_maximum_fusion.own_ref = bf16[1280,512]{1,0:T(8,128)(2,1)} fusion(bf16[320,512]{1,0:T(8,128)(2,1)S(1)} %collective-permute-done.8, bf16[320,512]{1,0:T(8,128)(2,1)S(1)} %collective-permute-done.7, bf16[320,512]{1,0:T(8,128)(2,1)S(1)} %collective-permute-done.6, bf16[320,512]{1,0:T(8,128)(2,1)S(1)} %multiply_convert_fusion), kind=kLoop, calls=%fused_computation.17 | loop fusion | flops 5242880 | bytes 2621440 | tf_op jit(solution)/shard_map/concatenate | solution.py:230
  38.1 1.4 %convolution_convert_fusion = bf16[128,2,1280]{2,0,1:T(8,128)(2,1)} fusion(bf16[128,320,1]{0,1,2:T(8,128)(2,1)S(1)} %bitcast.80, bf16[40,2,8,1280]{3,2,1,0:T(8,128)(2,1)S(1)} %bitcast.75), kind=kOutput, calls=%fused_computation.7 | convolution fusion | flops 210042880 | bytes 2375680 | tf_op jit(solution)/shard_map/rk,kxn->xrn/dot_general | solution.py:272
  39.5 7.2 %all-to-all-start = ((bf16[8,32,1280]{2,1,0:T(8,128)(2,1)}), bf16[8,32,1280]{2,1,0:T(8,128)(2,1)S(1)}, u32[]{:S(2)}, u32[]{:S(2)}) async-start(bf16[8,32,1280]{2,1,0:T(8,128)(2,1)} %bitcast.17), calls=%async_computation | async-start | bytes 1310720 | tf_op jit(solution)/shard_map/all_to_all | solution.py:281
  46.8 7.5 %fusion.1.table_ref = bf16[128,256,128]{2,1,0:T(8,128)(2,1)} fusion(s32[128,256]{1,0:T(8,128)S(1)} %copy-done.9, bf16[65,128]{1,0:T(8,128)(2,1)} %param.28), kind=kOutput, calls=%fused_computation.2 | convolution fusion | flops 551583744 | bytes 8536320 | tf_op jit(solution)/shard_map/ijb,bc->ijc/dot_general | solution.py:235
  55.3 3.1 %half_sums.1 = (f32[48,1152]{1,0:T(8,128)S(1)}, bf16[48,1152]{1,0:T(8,128)(2,1)S(1)}) custom-call(s32[3]{0:T(128)S(1)} %pad_add_fusion.place_ref, bf16[8,32,1280]{2,1,0:T(8,128)(2,1)S(1)} %all-to-all-done.parts_ref, bf16[128,2560]{1,0:T(8,128)(2,1)S(1)} %copy-done.1, bf16[1280,512]{1,0:T(8,128)(2,1)} %pad_maximum_fusion.own_ref, ...), custom_call_target="tpu_custom_call" | custom-call | tf_op jit(solution)/shard_map/half_sums/pallas_call | solution.py:163
  58.3 3.0 %collective-permute-start.10 = (bf16[48,1152]{1,0:T(8,128)(2,1)S(1)}, bf16[48,1152]{1,0:T(8,128)(2,1)S(1)}, u32[]{:S(2)}, u32[]{:S(2)}) collective-permute-start(bf16[48,1152]{1,0:T(8,128)(2,1)S(1)} %get-tuple-element.22), channel_id=1, source_target_pairs={{0,4},{1,5},{2,6},{3,7},{4,0},{5,1},{6,2},{7,3},{8,12},{9,13},{10,... | collective-permute-start | bytes 331784 | tf_op jit(solution)/shard_map/ppermute | solution.py:287
  61.4 3.5 %collective-permute-done.10 = bf16[48,1152]{1,0:T(8,128)(2,1)S(1)} collective-permute-done((bf16[48,1152]{1,0:T(8,128)(2,1)S(1)}, bf16[48,1152]{1,0:T(8,128)(2,1)S(1)}, u32[]{:S(2)}, u32[]{:S(2)}) %collective-permute-start.10) | collective-permute-done | bytes 110624 | tf_op jit(solution)/shard_map/ppermute | solution.py:287
  65.2 1.8 %fusion.11 = bf16[32,256]{1,0:T(8,128)(2,1)S(1)} fusion(bf16[1024,1024]{1,0:T(8,128)(2,1)S(1)} %copy-done, bf16[1024,128]{1,0:T(8,128)(2,1)} %param.27, bf16[1024,128]{1,0:T(8,128)(2,1)} %param.26, f32[48,1152]{1,0:T(8,128)S(1)} %convert_element_type.86, f32[48,1152]{1,0:T(8,128)} %copy-done.4, f32[32]{0:T(128)S(1)} %get-tuple-element.26, ...), kind=kOutput, calls=%fused_computation.22 | convolution fusion | flops 85172224 | bytes 2905088 | tf_op jit(solution)/shard_map/dot_general | solution.py:301
  67.1 8.3 %all_to_all.10 = bf16[4,32,256]{2,1,0:T(8,128)(2,1)S(1)} all-to-all(bf16[4,32,256]{2,1,0:T(8,128)(2,1)S(1)} %broadcast_in_dim.2), channel_id=1, replica_groups={{0,1,2,3},{4,5,6,7},{8,9,10,11},{12,13,14,15},{16,17,18,19},{20,21,22,2..., dimensions={0} | all-to-all | bytes 131072 | tf_op jit(solution)/shard_map/all_to_all | solution.py:302
  75.4 4.8 %collective-permute-start.12 = (bf16[128,128]{1,0:T(8,128)(2,1)S(1)}, bf16[128,128]{1,0:T(8,128)(2,1)S(1)}, u32[]{:S(2)}, u32[]{:S(2)}) collective-permute-start(bf16[128,128]{1,0:T(8,128)(2,1)S(1)} %get-tuple-element.35), channel_id=1, source_target_pairs={{8,0},{24,1},{40,2},{56,3},{72,4},{88,5},{104,6},{120,7},{9,8},{25... | collective-permute-start | bytes 98312 | tf_op jit(solution)/shard_map/ppermute | solution.py:313
  80.2 3.9 %collective-permute-start.11 = (bf16[128,128]{1,0:T(8,128)(2,1)S(1)}, bf16[128,128]{1,0:T(8,128)(2,1)S(1)}, u32[]{:S(2)}, u32[]{:S(2)}) collective-permute-start(bf16[128,128]{1,0:T(8,128)(2,1)S(1)} %get-tuple-element.35), channel_id=1, source_target_pairs={{0,0},{16,1},{32,2},{48,3},{64,4},{80,5},{96,6},{112,7},{1,8},{17,... | collective-permute-start | bytes 98312 | tf_op jit(solution)/shard_map/ppermute | solution.py:312
  84.1 1.8 %collective-permute-done.12 = bf16[128,128]{1,0:T(8,128)(2,1)S(1)} collective-permute-done((bf16[128,128]{1,0:T(8,128)(2,1)S(1)}, bf16[128,128]{1,0:T(8,128)(2,1)S(1)}, u32[]{:S(2)}, u32[]{:S(2)}) %collective-permute-start.12) | collective-permute-done | bytes 32800 | tf_op jit(solution)/shard_map/ppermute | solution.py:313
  85.9 5.9 %collective-permute-done.11 = bf16[128,128]{1,0:T(8,128)(2,1)S(1)} collective-permute-done((bf16[128,128]{1,0:T(8,128)(2,1)S(1)}, bf16[128,128]{1,0:T(8,128)(2,1)S(1)}, u32[]{:S(2)}, u32[]{:S(2)}) %collective-permute-start.11) | collective-permute-done | bytes 32800 | tf_op jit(solution)/shard_map/ppermute | solution.py:312
  91.8 21.8 %pair.1 = bf16[128,256,128]{2,1,0:T(8,128)(2,1)} custom-call(bf16[128,256,128]{2,1,0:T(8,128)(2,1)} %fusion.1.table_ref, f32[128,128]{1,0:T(8,128)S(1)} %get-tuple-element.36.left_ref, f32[256,128]{1,0:T(8,128)S(1)} %maximum_convert_fusion.right_ref, f32[1,128]{1,0:T(1,128)S(1)} %bitcast.72, bf16[128,512]{1,0:T(8,128)(2,1)S(1)} %copy-done.2, ...), custom_call_target="tpu_custom_call" | custom-call | tf_op jit(solution)/shard_map/pair/pallas_call | solution.py:88
  (76 shorter events, 11.0 us)
Async XLA Ops:
  0.0 65.2 %copy-start = (bf16[1024,1024]{1,0:T(8,128)(2,1)S(1)}, bf16[1024,1024]{1,0:T(8,128)(2,1)}, u32[]{:S(2)}) copy-start(bf16[1024,1024]{1,0:T(8,128)(2,1)} %param.25) | copy-start | bytes 6291460
  0.0 3.4 %copy-start.6 = (bf16[2560,320]{0,1:T(8,128)(2,1)S(1)}, bf16[2560,320]{0,1:T(8,128)(2,1)}, u32[]{:S(2)}) copy-start(bf16[2560,320]{0,1:T(8,128)(2,1)} %param.21) | copy-start | bytes 4915204
  4.7 9.0 %collective-permute-start.3 = (bf16[128,640]{0,1:T(8,128)(2,1)S(1)}, bf16[128,640]{0,1:T(8,128)(2,1)S(1)}, u32[]{:S(2)}, u32[]{:S(2)}) collective-permute-start(bf16[128,640]{0,1:T(8,128)(2,1)S(1)} %pad_maximum_fusion.2), channel_id=1, source_target_pairs={{0,32},{8,40},{16,48},{24,56},{32,0},{40,8},{48,16},{56,24},{64,96... | collective-permute-start | bytes 491528 | tf_op jit(solution)/shard_map/ppermute | solution.py:217
  8.6 8.5 %collective-permute-start.2 = (bf16[128,640]{0,1:T(8,128)(2,1)S(1)}, bf16[128,640]{0,1:T(8,128)(2,1)S(1)}, u32[]{:S(2)}, u32[]{:S(2)}) collective-permute-start(bf16[128,640]{0,1:T(8,128)(2,1)S(1)} %pad_maximum_fusion.2), channel_id=1, source_target_pairs={{0,48},{8,56},{16,0},{24,8},{32,16},{40,24},{48,32},{56,40},{64,11... | collective-permute-start | bytes 491528 | tf_op jit(solution)/shard_map/ppermute | solution.py:217
  9.3 7.8 %collective-permute-start.1 = (bf16[128,640]{0,1:T(8,128)(2,1)S(1)}, bf16[128,640]{0,1:T(8,128)(2,1)S(1)}, u32[]{:S(2)}, u32[]{:S(2)}) collective-permute-start(bf16[128,640]{0,1:T(8,128)(2,1)S(1)} %pad_maximum_fusion.2), channel_id=1, source_target_pairs={{0,16},{8,24},{16,32},{24,40},{32,48},{40,56},{48,0},{56,8},{64,80... | collective-permute-start | bytes 491528 | tf_op jit(solution)/shard_map/ppermute | solution.py:217
  12.7 4.6 %copy-start.10 = (bf16[320,1024]{1,0:T(8,128)(2,1)S(1)}, bf16[320,1024]{1,0:T(8,128)(2,1)}, u32[]{:S(2)}) copy-start(bf16[320,1024]{1,0:T(8,128)(2,1)} %param.24) | copy-start | bytes 1966084
  17.2 8.4 %collective-permute-start.4 = (bf16[512,640]{0,1:T(8,128)(2,1)S(1)}, bf16[512,640]{0,1:T(8,128)(2,1)S(1)}, u32[]{:S(2)}, u32[]{:S(2)}) collective-permute-start(bf16[512,640]{0,1:T(8,128)(2,1)S(1)} %pad_maximum_fusion.1), channel_id=1, source_target_pairs={{0,8},{8,0},{16,24},{24,16},{32,40},{40,32},{48,56},{56,48},{64,72... | collective-permute-start | bytes 1966088 | tf_op jit(solution)/shard_map/ppermute | solution.py:240
  18.1 12.1 %collective-permute-start.8 = (bf16[320,512]{1,0:T(8,128)(2,1)S(1)}, bf16[320,512]{1,0:T(8,128)(2,1)S(1)}, u32[]{:S(2)}, u32[]{:S(2)}) collective-permute-start(bf16[320,512]{1,0:T(8,128)(2,1)S(1)} %multiply_convert_fusion), channel_id=1, source_target_pairs={{0,2},{1,3},{2,0},{3,1},{4,6},{5,7},{6,4},{7,5},{8,10},{9,11},{10,... | collective-permute-start | bytes 983048 | tf_op jit(solution)/shard_map/ppermute | solution.py:229
  18.5 17.3 %collective-permute-start.7 = (bf16[320,512]{1,0:T(8,128)(2,1)S(1)}, bf16[320,512]{1,0:T(8,128)(2,1)S(1)}, u32[]{:S(2)}, u32[]{:S(2)}) collective-permute-start(bf16[320,512]{1,0:T(8,128)(2,1)S(1)} %multiply_convert_fusion), channel_id=1, source_target_pairs={{0,3},{1,0},{2,1},{3,2},{4,7},{5,4},{6,5},{7,6},{8,11},{9,8},{10,9... | collective-permute-start | bytes 983048 | tf_op jit(solution)/shard_map/ppermute | solution.py:229
  20.9 15.9 %collective-permute-start.6 = (bf16[320,512]{1,0:T(8,128)(2,1)S(1)}, bf16[320,512]{1,0:T(8,128)(2,1)S(1)}, u32[]{:S(2)}, u32[]{:S(2)}) collective-permute-start(bf16[320,512]{1,0:T(8,128)(2,1)S(1)} %multiply_convert_fusion), channel_id=1, source_target_pairs={{0,1},{1,2},{2,3},{3,0},{4,5},{5,6},{6,7},{7,4},{8,9},{9,10},{10,1... | collective-permute-start | bytes 983048 | tf_op jit(solution)/shard_map/ppermute | solution.py:229
  20.9 4.4 %collective-permute-start = (bf16[128,320]{0,1:T(8,128)(2,1)S(1)}, bf16[128,320]{0,1:T(8,128)(2,1)S(1)}, u32[]{:S(2)}, u32[]{:S(2)}) collective-permute-start(bf16[128,320]{0,1:T(8,128)(2,1)S(1)} %fusion.21), channel_id=1, source_target_pairs={{0,64},{8,72},{16,80},{24,88},{32,96},{40,104},{48,112},{56,120},{... | collective-permute-start | bytes 245768 | tf_op jit(solution)/shard_map/ppermute | solution.py:222
  27.8 10.3 %copy-start.8 = (bf16[320,2560]{1,0:T(8,128)(2,1)S(1)}, bf16[320,2560]{1,0:T(8,128)(2,1)}, u32[]{:S(2)}) copy-start(bf16[320,2560]{1,0:T(8,128)(2,1)} %param.22) | copy-start | bytes 4915204
  27.8 10.2 %collective-permute-start.5 = (bf16[128,384]{0,1:T(8,128)(2,1)S(1)}, bf16[128,384]{0,1:T(8,128)(2,1)S(1)}, u32[]{:S(2)}, u32[]{:S(2)}) collective-permute-start(bf16[128,384]{0,1:T(8,128)(2,1)S(1)} %fusion.30), channel_id=1, source_target_pairs={{0,64},{8,72},{16,80},{24,88},{32,96},{40,104},{48,112},{56,120},{... | collective-permute-start | bytes 294920 | tf_op jit(solution)/shard_map/ppermute | solution.py:264
  38.0 17.3 %collective-permute-start.9 = (bf16[1280,512]{1,0:T(8,128)(2,1)}, bf16[1280,512]{1,0:T(8,128)(2,1)}, u32[]{:S(2)}, u32[]{:S(2)}) collective-permute-start(bf16[1280,512]{1,0:T(8,128)(2,1)} %pad_maximum_fusion.own_ref), channel_id=1, source_target_pairs={{0,8},{8,0},{16,24},{24,16},{32,40},{40,32},{48,56},{56,48},{64,72... | collective-permute-start | bytes 3932168 | tf_op jit(solution)/shard_map/ppermute | solution.py:231
  38.1 8.7 %copy-start.9 = (s32[128,256]{1,0:T(8,128)S(1)}, s32[128,256]{1,0:T(8,128)}, u32[]{:S(2)}) copy-start(s32[128,256]{1,0:T(8,128)} %param.17) | copy-start | bytes 393220
  39.5 15.8 %all-to-all-start = ((bf16[8,32,1280]{2,1,0:T(8,128)(2,1)}), bf16[8,32,1280]{2,1,0:T(8,128)(2,1)S(1)}, u32[]{:S(2)}, u32[]{:S(2)}) async-start(bf16[8,32,1280]{2,1,0:T(8,128)(2,1)} %bitcast.17), calls=%async_computation | async-start | bytes 1310720 | tf_op jit(solution)/shard_map/all_to_all | solution.py:281
  46.8 8.5 %copy-start.1 = (bf16[128,2560]{1,0:T(8,128)(2,1)S(1)}, bf16[128,2560]{1,0:T(8,128)(2,1)}, u32[]{:S(2)}) copy-start(bf16[128,2560]{1,0:T(8,128)(2,1)} %stream_ref.1) | copy-start | bytes 1966084
  58.3 6.8 %copy-start.4 = (f32[48,1152]{1,0:T(8,128)}, f32[48,1152]{1,0:T(8,128)S(1)}, u32[]{:S(2)}) copy-start(f32[48,1152]{1,0:T(8,128)S(1)} %get-tuple-element.21) | copy-start | bytes 663556
  58.3 6.6 %collective-permute-start.10 = (bf16[48,1152]{1,0:T(8,128)(2,1)S(1)}, bf16[48,1152]{1,0:T(8,128)(2,1)S(1)}, u32[]{:S(2)}, u32[]{:S(2)}) collective-permute-start(bf16[48,1152]{1,0:T(8,128)(2,1)S(1)} %get-tuple-element.22), channel_id=1, source_target_pairs={{0,4},{1,5},{2,6},{3,7},{4,0},{5,1},{6,2},{7,3},{8,12},{9,13},{10,... | collective-permute-start | bytes 331784 | tf_op jit(solution)/shard_map/ppermute | solution.py:287
  65.2 26.6 %copy-start.2 = (bf16[128,512]{1,0:T(8,128)(2,1)S(1)}, bf16[128,512]{1,0:T(8,128)(2,1)}, u32[]{:S(2)}) copy-start(bf16[128,512]{1,0:T(8,128)(2,1)} %expand_ref.1) | copy-start | bytes 393220
  65.2 26.6 %copy-start.3 = (bf16[512,128]{1,0:T(8,128)(2,1)S(1)}, bf16[512,128]{1,0:T(8,128)(2,1)}, u32[]{:S(2)}) copy-start(bf16[512,128]{1,0:T(8,128)(2,1)} %contract_ref.1) | copy-start | bytes 393220
  65.2 26.6 %copy-start.5 = (f32[128]{0:T(128)S(1)}, f32[128]{0:T(128)}, u32[]{:S(2)}) copy-start(f32[128]{0:T(128)} %param.29) | copy-start | bytes 1540
  75.4 10.5 %collective-permute-start.12 = (bf16[128,128]{1,0:T(8,128)(2,1)S(1)}, bf16[128,128]{1,0:T(8,128)(2,1)S(1)}, u32[]{:S(2)}, u32[]{:S(2)}) collective-permute-start(bf16[128,128]{1,0:T(8,128)(2,1)S(1)} %get-tuple-element.35), channel_id=1, source_target_pairs={{8,0},{24,1},{40,2},{56,3},{72,4},{88,5},{104,6},{120,7},{9,8},{25... | collective-permute-start | bytes 98312 | tf_op jit(solution)/shard_map/ppermute | solution.py:313
  80.2 11.5 %collective-permute-start.11 = (bf16[128,128]{1,0:T(8,128)(2,1)S(1)}, bf16[128,128]{1,0:T(8,128)(2,1)S(1)}, u32[]{:S(2)}, u32[]{:S(2)}) collective-permute-start(bf16[128,128]{1,0:T(8,128)(2,1)S(1)} %get-tuple-element.35), channel_id=1, source_target_pairs={{0,0},{16,1},{32,2},{48,3},{64,4},{80,5},{96,6},{112,7},{1,8},{17,... | collective-permute-start | bytes 98312 | tf_op jit(solution)/shard_map/ppermute | solution.py:312
  (1 other events, 2.3 us)

commit v4 on v3

--- a/solution.py
+++ b/solution.py
@@ -35,19 +35,11 @@
     return [(place, place ^ bit) for place in range(size)]
 
 
-def along_z(step):
-    return [(place, place // 8 * 8 + (place % 8 + 2 * step) % 8) for place in range(16)]
-
-
-def along_y(step):
-    return [(place, place // 4 * 4 + (place + step) % 4) for place in range(8)]
-
-
-def right_pairs(flip):
+def right_pairs(size, other_size):
     return [
-        ((2 * col + ((row // 8) ^ flip)) * 8 + row % 8, row * 8 + col)
-        for row in range(16)
-        for col in range(8)
+        (row * other_size + col, (2 * col + row % 2) * other_size + row // 2)
+        for row in range(size)
+        for col in range(other_size)
     ]
 
 
@@ -100,6 +92,26 @@
     )(table_part, left, *fixed)
 
 
+def first_norm_kernel(hidden_ref, gain_ref, out_ref):
+    for start in range(0, hidden_ref.shape[0], 32):
+        rows = slice(start, start + 32)
+        values = hidden_ref[rows, :].astype(jnp.float32)
+        out_ref[rows, :] = layer_norm(values, gain_ref[...]).astype(jnp.bfloat16)
+
+
+def first_norm(hidden, gain):
+    gain = gain.reshape(1, -1)
+    return pl.pallas_call(
+        first_norm_kernel,
+        grid=(1,),
+        in_specs=[whole(hidden), whole(gain)],
+        out_specs=whole(hidden),
+        out_shape=jax.ShapeDtypeStruct(hidden.shape, jnp.bfloat16),
+        compiler_params=pltpu.CompilerParams(vmem_limit_bytes=8 << 20),
+        name="first_norm",
+    )(hidden, gain)
+
+
 def half_sums_kernel(
     place_ref, parts_ref, stream_ref, own_ref, other_ref, mine_ref, sent_ref, blocks_ref
 ):
@@ -120,9 +132,9 @@
     line = lax.broadcasted_iota(jnp.int32, (16, half_columns), 0)
     for ref, side in ((own_ref, core), (other_ref, 1 - core)):
         total = jnp.zeros((rows + 16, half_columns), jnp.float32)
-        for position, shift in enumerate((0, 3, 1, 2)):
+        for position, shift in enumerate((0, 1, 3, 2)):
             total += jnp.dot(
-                blocks_ref[lax.rem(near + shift, 4)],
+                blocks_ref[near ^ shift],
                 ref[position * local_width : (position + 1) * local_width, :],
                 preferred_element_type=jnp.float32,
             )
@@ -206,29 +218,29 @@
     local_width = w_query.shape[1]
     local_heads = local_width // HD
     positions = lax.axis_index("row") * row_count + jnp.arange(row_count, dtype=jnp.int32)
-    stream = hidden.astype(jnp.float32)
-    attn_in = layer_norm(stream, attn_gain).astype(jnp.bfloat16)
+    core = lax.rem(lax.axis_index("row"), 2)
+    col_index = lax.axis_index("col")
+    half_columns = w_single.shape[1] // 2
+    own_part = lax.dynamic_slice_in_dim(w_single, core * half_columns, half_columns, 1)
+    own_part = (own_part.astype(jnp.float32) * final_gain[:, None]).astype(jnp.bfloat16)
+    own_part, hidden = lax.optimization_barrier((own_part, hidden))
+    quarter = [own_part] + [lax.ppermute(own_part, "col", flip_pairs(8, bit)) for bit in (1, 3, 2)]
+    quarter = jnp.concatenate(quarter, 0)
+    quarter_other = lax.ppermute(quarter, "row", flip_pairs(16, 1))
+
+    attn_in = first_norm(hidden, attn_gain)
     keys = jnp.dot(attn_in, w_key, preferred_element_type=jnp.float32)
     keys = rotary(keys.reshape(row_count, local_heads, HD), positions).astype(jnp.bfloat16)
     values = jnp.dot(attn_in, w_value, preferred_element_type=jnp.float32).astype(jnp.bfloat16)
     stacked = jnp.concatenate([keys.reshape(row_count, local_width), values], 1)
     stacked, attn_in = lax.optimization_barrier((stacked, attn_in))
 
-    blocks = [stacked] + [lax.ppermute(stacked, "row", along_z(step)) for step in (1, 3, 2)]
+    blocks = [stacked] + [lax.ppermute(stacked, "row", flip_pairs(16, 2 * bit)) for bit in (1, 3, 2)]
     query = jnp.dot(attn_in, w_query, preferred_element_type=jnp.float32) * HD ** (-0.5)
     query = rotary(query.reshape(row_count, local_heads, HD), positions).astype(jnp.bfloat16)
     query = query.reshape(row_count, local_width)
-    query, w_single, rel_bins = lax.optimization_barrier((query, w_single, rel_bins))
+    query, rel_bins = lax.optimization_barrier((query, rel_bins))
     other_query = lax.ppermute(query, "row", flip_pairs(16, 8))
-
-    core = lax.rem(lax.axis_index("row"), 2)
-    col_index = lax.axis_index("col")
-    half_columns = w_single.shape[1] // 2
-    own_part = lax.dynamic_slice_in_dim(w_single, core * half_columns, half_columns, 1)
-    own_part = (own_part.astype(jnp.float32) * final_gain[:, None]).astype(jnp.bfloat16)
-    quarter = [own_part] + [lax.ppermute(own_part, "col", along_y(step)) for step in (1, 3, 2)]
-    quarter = jnp.concatenate(quarter, 0)
-    quarter_other = lax.ppermute(quarter, "row", flip_pairs(16, 1))
 
     bin_codes = jnp.arange(rel_table.shape[0], dtype=jnp.int32)
     one_hot = (rel_bins[..., None] == bin_codes).astype(jnp.bfloat16)
@@ -309,11 +321,12 @@
     ).reshape(row_count, -1)
     channels = w_left.shape[1]
     left, right = both[:, :channels], both[:, channels:]
-    first = lax.ppermute(right, ("row", "col"), right_pairs(0))
-    second = lax.ppermute(right, ("row", "col"), right_pairs(1))
-    upper = lax.axis_index("row") < 8
+    pairs = right_pairs(lax.axis_size("row"), lax.axis_size("col"))
+    own_right = lax.ppermute(right, ("row", "col"), pairs)
+    other_right = lax.ppermute(own_right, "row", flip_pairs(16, 1))
+    low = core == 0
     column_right = jnp.concatenate(
-        [jnp.where(upper, first, second), jnp.where(upper, second, first)], 0
+        [jnp.where(low, own_right, other_right), jnp.where(low, other_right, own_right)], 0
     )
     return pair_stage(table_part, left, column_right, pair_gain, w_expand, w_contract)
 

time: 114 us -> 107 us (0.939)
  the two profiles are of different devices: /device:TPU:22 before, /device:TPU:69 now
where the time goes in v4:
time: 107 us; the launch traced here: 106 us
  starting transfers between devices  30.8 us (29%)
  Pallas kernels  25.3 us (24%)
  waiting for transfers between devices  18.1 us (17%)
  matrix products  16 us (15%)
  blocking collectives  8.24 us (8%)
  local copies, waits for them, and re-layouts  5.24 us (5%)
  other arithmetic  2.05 us (2%)
    pallas_call x1, Pallas kernels, pair_stage(): pl.pallas_call(pair_kernel, grid=(rows // block,), in_specs=[pl.BlockSpec...  21.8 us
    all_to_all x1, blocking collectives, local(): lax.all_to_all(jnp.broadcast_to(both, (4,) + both.shape), 'col', 0, 0, ti...  8.24 us
    ppermute x1, waiting for transfers between devices, local(): own_right = lax.ppermute(right, ('row', 'col'), pairs)  7.76 us
    dot_general x1, matrix products, local(): jnp.einsum('ijb,bc->ijc', one_hot, rel_table, preferred_element_type=jnp....  7.54 us
    ppermute x1, starting transfers between devices, local(): other_right = lax.ppermute(own_right, 'row', flip_pairs(16, 1))  6.94 us
    all_to_all x1, starting transfers between devices, local(): lax.all_to_all(attn_part.reshape(8, own_count, half_width), 'col', 0, 0,...  5.85 us
    ppermute x3, waiting for transfers between devices, local(): lax.ppermute(stacked, 'row', flip_pairs(16, 2 * bit))  4.86 us
    ppermute x3, starting transfers between devices, local(): lax.ppermute(stacked, 'row', flip_pairs(16, 2 * bit))  3.93 us
  transfers between devices with their start and end apart: 14, of which 6 were waited for; matrix products, arithmetic and copies ran while one was open for 18% of the time, Pallas kernels for 0%

profile of v4, /device:TPU:69, one launch (start us, length us, event | category | flops | bytes accessed | tf_op | source)
XLA Modules:
  0.0 106.1 jit_solution(9441601980557578513)
XLA Ops:
  0.0 1.3 %multiply_convert_fusion = bf16[320,512]{1,0:T(8,128)(2,1)S(1)} fusion(f32[320]{0:T(512)} %param.23, bf16[320,1024]{1,0:T(8,128)(2,1)} %param.24, s32[]{:T(128)S(6)} %select_n.20), kind=kLoop, calls=%fused_computation.16 | loop fusion | flops 491520 | bytes 656644 | tf_op jit(solution)/shard_map/convert_element_type | solution.py:225
  1.3 3.0 %collective-permute-start.8 = (bf16[320,512]{1,0:T(8,128)(2,1)S(1)}, bf16[320,512]{1,0:T(8,128)(2,1)S(1)}, u32[]{:S(2)}, u32[]{:S(2)}) collective-permute-start(bf16[320,512]{1,0:T(8,128)(2,1)S(1)} %multiply_convert_fusion), channel_id=1, source_target_pairs={{0,2},{1,3},{2,0},{3,1},{4,6},{5,7},{6,4},{7,5},{8,10},{9,11},{10,... | collective-permute-start | bytes 983048 | tf_op jit(solution)/shard_map/ppermute | solution.py:227
  5.9 1.1 %copy-done.1 = bf16[128,2560]{1,0:T(8,128)(2,1)S(1)} copy-done((bf16[128,2560]{1,0:T(8,128)(2,1)S(1)}, bf16[128,2560]{1,0:T(8,128)(2,1)}, u32[]{:S(2)}) %copy-start.1) | copy-done | bytes 655384
  7.4 2.1 %convolution_convert_fusion.1 = bf16[128,320]{0,1:T(8,128)(2,1)S(1)} fusion(bf16[128,2560]{1,0:T(8,128)(2,1)S(1)} %first_norm.1, bf16[2560,320]{0,1:T(8,128)(2,1)} %param.21), kind=kOutput, calls=%fused_computation.11 | convolution fusion | flops 209756160 | bytes 2375680 | tf_op jit(solution)/shard_map/dot_general | solution.py:234
  10.3 2.5 %collective-permute-start.2 = (bf16[128,640]{0,1:T(8,128)(2,1)S(1)}, bf16[128,640]{0,1:T(8,128)(2,1)S(1)}, u32[]{:S(2)}, u32[]{:S(2)}) collective-permute-start(bf16[128,640]{0,1:T(8,128)(2,1)S(1)} %pad_maximum_fusion.1), channel_id=1, source_target_pairs={{0,48},{8,56},{16,32},{24,40},{32,16},{40,24},{48,0},{56,8},{64,11... | collective-permute-start | bytes 491528 | tf_op jit(solution)/shard_map/ppermute | solution.py:238
  12.8 1.3 %collective-permute-start.1 = (bf16[128,640]{0,1:T(8,128)(2,1)S(1)}, bf16[128,640]{0,1:T(8,128)(2,1)S(1)}, u32[]{:S(2)}, u32[]{:S(2)}) collective-permute-start(bf16[128,640]{0,1:T(8,128)(2,1)S(1)} %pad_maximum_fusion.1), channel_id=1, source_target_pairs={{0,16},{8,24},{16,0},{24,8},{32,48},{40,56},{48,32},{56,40},{64,80... | collective-permute-start | bytes 491528 | tf_op jit(solution)/shard_map/ppermute | solution.py:238
  16.4 4.1 %collective-permute-done.2 = bf16[128,640]{0,1:T(8,128)(2,1)S(1)} collective-permute-done((bf16[128,640]{0,1:T(8,128)(2,1)S(1)}, bf16[128,640]{0,1:T(8,128)(2,1)S(1)}, u32[]{:S(2)}, u32[]{:S(2)}) %collective-permute-start.2) | collective-permute-done | bytes 163872 | tf_op jit(solution)/shard_map/ppermute | solution.py:238
  21.5 1.4 %collective-permute-start.4 = (bf16[512,640]{0,1:T(8,128)(2,1)S(1)}, bf16[512,640]{0,1:T(8,128)(2,1)S(1)}, u32[]{:S(2)}, u32[]{:S(2)}) collective-permute-start(bf16[512,640]{0,1:T(8,128)(2,1)S(1)} %pad_maximum_fusion), channel_id=1, source_target_pairs={{0,8},{8,0},{16,24},{24,16},{32,40},{40,32},{48,56},{56,48},{64,72... | collective-permute-start | bytes 1966088 | tf_op jit(solution)/shard_map/ppermute | solution.py:252
  22.8 1.2 %collective-permute-done = bf16[128,320]{0,1:T(8,128)(2,1)S(1)} collective-permute-done((bf16[128,320]{0,1:T(8,128)(2,1)S(1)}, bf16[128,320]{0,1:T(8,128)(2,1)S(1)}, u32[]{:S(2)}, u32[]{:S(2)}) %collective-permute-start) | collective-permute-done | bytes 81952 | tf_op jit(solution)/shard_map/ppermute | solution.py:243
  26.0 1.1 exponential_reduce_fusion
  28.0 1.0 collective-permute-start.5
  29.8 3.3 %collective-permute-start.9 = (bf16[1280,512]{1,0:T(8,128)(2,1)}, bf16[1280,512]{1,0:T(8,128)(2,1)}, u32[]{:S(2)}, u32[]{:S(2)}) collective-permute-start(bf16[1280,512]{1,0:T(8,128)(2,1)} %constant_dynamic-update-slice_fusion.5.own_ref), channel_id=1, source_target_pairs={{0,8},{8,0},{16,24},{24,16},{32,40},{40,32},{48,56},{56,48},{64,72... | collective-permute-start | bytes 3932168 | tf_op jit(solution)/shard_map/ppermute | solution.py:229
  33.1 1.4 %convolution_convert_fusion = bf16[128,2,1280]{2,0,1:T(8,128)(2,1)} fusion(bf16[128,320,1]{0,1,2:T(8,128)(2,1)S(1)} %bitcast.80, bf16[40,2,8,1280]{3,2,1,0:T(8,128)(2,1)S(1)} %bitcast.75), kind=kOutput, calls=%fused_computation.7 | convolution fusion | flops 210042880 | bytes 2375680 | tf_op jit(solution)/shard_map/rk,kxn->xrn/dot_general | solution.py:284
  34.5 5.9 %all-to-all-start = ((bf16[8,32,1280]{2,1,0:T(8,128)(2,1)}), bf16[8,32,1280]{2,1,0:T(8,128)(2,1)S(1)}, u32[]{:S(2)}, u32[]{:S(2)}) async-start(bf16[8,32,1280]{2,1,0:T(8,128)(2,1)} %bitcast.17), calls=%async_computation | async-start | bytes 1310720 | tf_op jit(solution)/shard_map/all_to_all | solution.py:293
  40.5 7.5 %fusion.1.table_ref = bf16[128,256,128]{2,1,0:T(8,128)(2,1)} fusion(s32[128,256]{1,0:T(8,128)S(1)} %copy-done.10, bf16[65,128]{1,0:T(8,128)(2,1)} %param.28), kind=kOutput, calls=%fused_computation.2 | convolution fusion | flops 551583744 | bytes 8536320 | tf_op jit(solution)/shard_map/ijb,bc->ijc/dot_general | solution.py:247
  48.0 3.1 %half_sums.1 = (f32[48,1152]{1,0:T(8,128)S(1)}, bf16[48,1152]{1,0:T(8,128)(2,1)S(1)}) custom-call(s32[3]{0:T(128)S(1)} %pad_add_fusion.place_ref, bf16[8,32,1280]{2,1,0:T(8,128)(2,1)S(1)} %all-to-all-done.parts_ref, bf16[128,2560]{1,0:T(8,128)(2,1)S(1)} %copy-done.2, bf16[1280,512]{1,0:T(8,128)(2,1)} %constant_dynamic-update-slice_fusion.5.own_ref, ...), custom_call_target="tpu_custom_call" | custom-call | tf_op jit(solution)/shard_map/half_sums/pallas_call | solution.py:175
  51.1 1.8 %collective-permute-start.10 = (bf16[48,1152]{1,0:T(8,128)(2,1)S(1)}, bf16[48,1152]{1,0:T(8,128)(2,1)S(1)}, u32[]{:S(2)}, u32[]{:S(2)}) collective-permute-start(bf16[48,1152]{1,0:T(8,128)(2,1)S(1)} %get-tuple-element.24), channel_id=1, source_target_pairs={{0,4},{1,5},{2,6},{3,7},{4,0},{5,1},{6,2},{7,3},{8,12},{9,13},{10,... | collective-permute-start | bytes 331784 | tf_op jit(solution)/shard_map/ppermute | solution.py:299
  52.9 3.4 %collective-permute-done.10 = bf16[48,1152]{1,0:T(8,128)(2,1)S(1)} collective-permute-done((bf16[48,1152]{1,0:T(8,128)(2,1)S(1)}, bf16[48,1152]{1,0:T(8,128)(2,1)S(1)}, u32[]{:S(2)}, u32[]{:S(2)}) %collective-permute-start.10) | collective-permute-done | bytes 110624 | tf_op jit(solution)/shard_map/ppermute | solution.py:299
  56.6 1.8 %fusion.7 = bf16[32,256]{1,0:T(8,128)(2,1)S(1)} fusion(bf16[1024,1024]{1,0:T(8,128)(2,1)S(1)} %copy-done, bf16[1024,128]{1,0:T(8,128)(2,1)} %param.27, bf16[1024,128]{1,0:T(8,128)(2,1)} %param.26, f32[48,1152]{1,0:T(8,128)S(1)} %convert_element_type.78, f32[48,1152]{1,0:T(8,128)} %copy-done.5, f32[32]{0:T(128)S(1)} %get-tuple-element.26, ...), kind=kOutput, calls=%fused_computation.14 | convolution fusion | flops 85172224 | bytes 2905088 | tf_op jit(solution)/shard_map/dot_general | solution.py:313
  58.4 8.2 %all_to_all.10 = bf16[4,32,256]{2,1,0:T(8,128)(2,1)S(1)} all-to-all(bf16[4,32,256]{2,1,0:T(8,128)(2,1)S(1)} %broadcast_in_dim.2), channel_id=1, replica_groups={{0,1,2,3},{4,5,6,7},{8,9,10,11},{12,13,14,15},{16,17,18,19},{20,21,22,2..., dimensions={0} | all-to-all | bytes 131072 | tf_op jit(solution)/shard_map/all_to_all | solution.py:314
  66.7 1.9 %collective-permute-start.11 = (bf16[128,128]{1,0:T(8,128)(2,1)S(1)}, bf16[128,128]{1,0:T(8,128)(2,1)S(1)}, u32[]{:S(2)}, u32[]{:S(2)}) collective-permute-start(bf16[128,128]{1,0:T(8,128)(2,1)S(1)} %get-tuple-element.35), channel_id=1, source_target_pairs={{0,0},{1,16},{2,32},{3,48},{4,64},{5,80},{6,96},{7,112},{8,8},{9,2... | collective-permute-start | bytes 98312 | tf_op jit(solution)/shard_map/ppermute | solution.py:325
  68.6 7.8 %collective-permute-done.11 = bf16[128,128]{1,0:T(8,128)(2,1)S(1)} collective-permute-done((bf16[128,128]{1,0:T(8,128)(2,1)S(1)}, bf16[128,128]{1,0:T(8,128)(2,1)S(1)}, u32[]{:S(2)}, u32[]{:S(2)}) %collective-permute-start.11) | collective-permute-done | bytes 32800 | tf_op jit(solution)/shard_map/ppermute | solution.py:325
  76.4 6.9 %collective-permute-start.12 = (bf16[128,128]{1,0:T(8,128)(2,1)S(1)}, bf16[128,128]{1,0:T(8,128)(2,1)S(1)}, u32[]{:S(2)}, u32[]{:S(2)}) collective-permute-start(bf16[128,128]{1,0:T(8,128)(2,1)S(1)} %collective-permute-done.11), channel_id=1, source_target_pairs={{0,8},{8,0},{16,24},{24,16},{32,40},{40,32},{48,56},{56,48},{64,72... | collective-permute-start | bytes 98312 | tf_op jit(solution)/shard_map/ppermute | solution.py:326
  84.2 21.8 %pair.1 = bf16[128,256,128]{2,1,0:T(8,128)(2,1)} custom-call(bf16[128,256,128]{2,1,0:T(8,128)(2,1)} %fusion.1.table_ref, f32[128,128]{1,0:T(8,128)S(1)} %get-tuple-element.36.left_ref, f32[256,128]{1,0:T(8,128)S(1)} %maximum_convert_fusion.right_ref, f32[1,128]{1,0:T(1,128)S(1)} %bitcast.72, bf16[128,512]{1,0:T(8,128)(2,1)S(1)} %copy-done.3, ...), custom_call_target="tpu_custom_call" | custom-call | tf_op jit(solution)/shard_map/pair/pallas_call | solution.py:80
  (78 shorter events, 10.8 us)
Async XLA Ops:
  0.0 56.5 %copy-start = (bf16[1024,1024]{1,0:T(8,128)(2,1)S(1)}, bf16[1024,1024]{1,0:T(8,128)(2,1)}, u32[]{:S(2)}) copy-start(bf16[1024,1024]{1,0:T(8,128)(2,1)} %param.25) | copy-start | bytes 6291460
  1.3 27.7 %collective-permute-start.8 = (bf16[320,512]{1,0:T(8,128)(2,1)S(1)}, bf16[320,512]{1,0:T(8,128)(2,1)S(1)}, u32[]{:S(2)}, u32[]{:S(2)}) collective-permute-start(bf16[320,512]{1,0:T(8,128)(2,1)S(1)} %multiply_convert_fusion), channel_id=1, source_target_pairs={{0,2},{1,3},{2,0},{3,1},{4,6},{5,7},{6,4},{7,5},{8,10},{9,11},{10,... | collective-permute-start | bytes 983048 | tf_op jit(solution)/shard_map/ppermute | solution.py:227
  4.3 20.8 %collective-permute-start.7 = (bf16[320,512]{1,0:T(8,128)(2,1)S(1)}, bf16[320,512]{1,0:T(8,128)(2,1)S(1)}, u32[]{:S(2)}, u32[]{:S(2)}) collective-permute-start(bf16[320,512]{1,0:T(8,128)(2,1)S(1)} %multiply_convert_fusion), channel_id=1, source_target_pairs={{0,3},{1,2},{2,1},{3,0},{4,7},{5,6},{6,5},{7,4},{8,11},{9,10},{10,... | collective-permute-start | bytes 983048 | tf_op jit(solution)/shard_map/ppermute | solution.py:227
  7.0 2.5 %copy-start.7 = (bf16[2560,320]{0,1:T(8,128)(2,1)S(1)}, bf16[2560,320]{0,1:T(8,128)(2,1)}, u32[]{:S(2)}) copy-start(bf16[2560,320]{0,1:T(8,128)(2,1)} %param.20) | copy-start | bytes 4915204
  9.5 4.6 %copy-start.8 = (bf16[2560,320]{0,1:T(8,128)(2,1)S(1)}, bf16[2560,320]{0,1:T(8,128)(2,1)}, u32[]{:S(2)}) copy-start(bf16[2560,320]{0,1:T(8,128)(2,1)} %param.19) | copy-start | bytes 4915204
  10.2 6.1 %collective-permute-start.3 = (bf16[128,640]{0,1:T(8,128)(2,1)S(1)}, bf16[128,640]{0,1:T(8,128)(2,1)S(1)}, u32[]{:S(2)}, u32[]{:S(2)}) collective-permute-start(bf16[128,640]{0,1:T(8,128)(2,1)S(1)} %pad_maximum_fusion.1), channel_id=1, source_target_pairs={{0,32},{8,40},{16,48},{24,56},{32,0},{40,8},{48,16},{56,24},{64,96... | collective-permute-start | bytes 491528 | tf_op jit(solution)/shard_map/ppermute | solution.py:238
  10.3 10.2 %collective-permute-start.2 = (bf16[128,640]{0,1:T(8,128)(2,1)S(1)}, bf16[128,640]{0,1:T(8,128)(2,1)S(1)}, u32[]{:S(2)}, u32[]{:S(2)}) collective-permute-start(bf16[128,640]{0,1:T(8,128)(2,1)S(1)} %pad_maximum_fusion.1), channel_id=1, source_target_pairs={{0,48},{8,56},{16,32},{24,40},{32,16},{40,24},{48,0},{56,8},{64,11... | collective-permute-start | bytes 491528 | tf_op jit(solution)/shard_map/ppermute | solution.py:238
  12.8 8.6 %collective-permute-start.1 = (bf16[128,640]{0,1:T(8,128)(2,1)S(1)}, bf16[128,640]{0,1:T(8,128)(2,1)S(1)}, u32[]{:S(2)}, u32[]{:S(2)}) collective-permute-start(bf16[128,640]{0,1:T(8,128)(2,1)S(1)} %pad_maximum_fusion.1), channel_id=1, source_target_pairs={{0,16},{8,24},{16,0},{24,8},{32,48},{40,56},{48,32},{56,40},{64,80... | collective-permute-start | bytes 491528 | tf_op jit(solution)/shard_map/ppermute | solution.py:238
  16.4 7.9 %collective-permute-start.6 = (bf16[320,512]{1,0:T(8,128)(2,1)S(1)}, bf16[320,512]{1,0:T(8,128)(2,1)S(1)}, u32[]{:S(2)}, u32[]{:S(2)}) collective-permute-start(bf16[320,512]{1,0:T(8,128)(2,1)S(1)} %multiply_convert_fusion), channel_id=1, source_target_pairs={{0,1},{1,0},{2,3},{3,2},{4,5},{5,4},{6,7},{7,6},{8,9},{9,8},{10,11... | collective-permute-start | bytes 983048 | tf_op jit(solution)/shard_map/ppermute | solution.py:227
  20.5 3.6 %collective-permute-start = (bf16[128,320]{0,1:T(8,128)(2,1)S(1)}, bf16[128,320]{0,1:T(8,128)(2,1)S(1)}, u32[]{:S(2)}, u32[]{:S(2)}) collective-permute-start(bf16[128,320]{0,1:T(8,128)(2,1)S(1)} %fusion.17), channel_id=1, source_target_pairs={{0,64},{8,72},{16,80},{24,88},{32,96},{40,104},{48,112},{56,120},{... | collective-permute-start | bytes 245768 | tf_op jit(solution)/shard_map/ppermute | solution.py:243
  21.5 4.3 %collective-permute-start.4 = (bf16[512,640]{0,1:T(8,128)(2,1)S(1)}, bf16[512,640]{0,1:T(8,128)(2,1)S(1)}, u32[]{:S(2)}, u32[]{:S(2)}) collective-permute-start(bf16[512,640]{0,1:T(8,128)(2,1)S(1)} %pad_maximum_fusion), channel_id=1, source_target_pairs={{0,8},{8,0},{16,24},{24,16},{32,40},{40,32},{48,56},{56,48},{64,72... | collective-permute-start | bytes 1966088 | tf_op jit(solution)/shard_map/ppermute | solution.py:252
  28.0 5.2 %copy-start.9 = (bf16[320,2560]{1,0:T(8,128)(2,1)S(1)}, bf16[320,2560]{1,0:T(8,128)(2,1)}, u32[]{:S(2)}) copy-start(bf16[320,2560]{1,0:T(8,128)(2,1)} %param.22) | copy-start | bytes 4915204
  28.0 5.0 %collective-permute-start.5 = (bf16[128,384]{0,1:T(8,128)(2,1)S(1)}, bf16[128,384]{0,1:T(8,128)(2,1)S(1)}, u32[]{:S(2)}, u32[]{:S(2)}) collective-permute-start(bf16[128,384]{0,1:T(8,128)(2,1)S(1)} %fusion.26), channel_id=1, source_target_pairs={{0,64},{8,72},{16,80},{24,88},{32,96},{40,104},{48,112},{56,120},{... | collective-permute-start | bytes 294920 | tf_op jit(solution)/shard_map/ppermute | solution.py:276
  29.8 18.2 %collective-permute-start.9 = (bf16[1280,512]{1,0:T(8,128)(2,1)}, bf16[1280,512]{1,0:T(8,128)(2,1)}, u32[]{:S(2)}, u32[]{:S(2)}) collective-permute-start(bf16[1280,512]{1,0:T(8,128)(2,1)} %constant_dynamic-update-slice_fusion.5.own_ref), channel_id=1, source_target_pairs={{0,8},{8,0},{16,24},{24,16},{32,40},{40,32},{48,56},{56,48},{64,72... | collective-permute-start | bytes 3932168 | tf_op jit(solution)/shard_map/ppermute | solution.py:229
  33.1 7.3 %copy-start.10 = (s32[128,256]{1,0:T(8,128)S(1)}, s32[128,256]{1,0:T(8,128)}, u32[]{:S(2)}) copy-start(s32[128,256]{1,0:T(8,128)} %param.17) | copy-start | bytes 393220
  34.5 13.5 %all-to-all-start = ((bf16[8,32,1280]{2,1,0:T(8,128)(2,1)}), bf16[8,32,1280]{2,1,0:T(8,128)(2,1)S(1)}, u32[]{:S(2)}, u32[]{:S(2)}) async-start(bf16[8,32,1280]{2,1,0:T(8,128)(2,1)} %bitcast.17), calls=%async_computation | async-start | bytes 1310720 | tf_op jit(solution)/shard_map/all_to_all | solution.py:293
  40.5 7.5 %copy-start.2 = (bf16[128,2560]{1,0:T(8,128)(2,1)S(1)}, bf16[128,2560]{1,0:T(8,128)(2,1)}, u32[]{:S(2)}) copy-start(bf16[128,2560]{1,0:T(8,128)(2,1)} %stream_ref) | copy-start | bytes 1966084
  51.1 5.4 %copy-start.5 = (f32[48,1152]{1,0:T(8,128)}, f32[48,1152]{1,0:T(8,128)S(1)}, u32[]{:S(2)}) copy-start(f32[48,1152]{1,0:T(8,128)S(1)} %get-tuple-element.23) | copy-start | bytes 663556
  51.1 5.2 %collective-permute-start.10 = (bf16[48,1152]{1,0:T(8,128)(2,1)S(1)}, bf16[48,1152]{1,0:T(8,128)(2,1)S(1)}, u32[]{:S(2)}, u32[]{:S(2)}) collective-permute-start(bf16[48,1152]{1,0:T(8,128)(2,1)S(1)} %get-tuple-element.24), channel_id=1, source_target_pairs={{0,4},{1,5},{2,6},{3,7},{4,0},{5,1},{6,2},{7,3},{8,12},{9,13},{10,... | collective-permute-start | bytes 331784 | tf_op jit(solution)/shard_map/ppermute | solution.py:299
  56.5 27.7 %copy-start.3 = (bf16[128,512]{1,0:T(8,128)(2,1)S(1)}, bf16[128,512]{1,0:T(8,128)(2,1)}, u32[]{:S(2)}) copy-start(bf16[128,512]{1,0:T(8,128)(2,1)} %expand_ref.1) | copy-start | bytes 393220
  56.5 27.7 %copy-start.4 = (bf16[512,128]{1,0:T(8,128)(2,1)S(1)}, bf16[512,128]{1,0:T(8,128)(2,1)}, u32[]{:S(2)}) copy-start(bf16[512,128]{1,0:T(8,128)(2,1)} %contract_ref.1) | copy-start | bytes 393220
  56.6 27.7 %copy-start.6 = (f32[128]{0:T(128)S(1)}, f32[128]{0:T(128)}, u32[]{:S(2)}) copy-start(f32[128]{0:T(128)} %param.29) | copy-start | bytes 1540
  66.7 9.7 %collective-permute-start.11 = (bf16[128,128]{1,0:T(8,128)(2,1)S(1)}, bf16[128,128]{1,0:T(8,128)(2,1)S(1)}, u32[]{:S(2)}, u32[]{:S(2)}) collective-permute-start(bf16[128,128]{1,0:T(8,128)(2,1)S(1)} %get-tuple-element.35), channel_id=1, source_target_pairs={{0,0},{1,16},{2,32},{3,48},{4,64},{5,80},{6,96},{7,112},{8,8},{9,2... | collective-permute-start | bytes 98312 | tf_op jit(solution)/shard_map/ppermute | solution.py:325
  76.4 7.8 %collective-permute-start.12 = (bf16[128,128]{1,0:T(8,128)(2,1)S(1)}, bf16[128,128]{1,0:T(8,128)(2,1)S(1)}, u32[]{:S(2)}, u32[]{:S(2)}) collective-permute-start(bf16[128,128]{1,0:T(8,128)(2,1)S(1)} %collective-permute-done.11), channel_id=1, source_target_pairs={{0,8},{8,0},{16,24},{24,16},{32,40},{40,32},{48,56},{56,48},{64,72... | collective-permute-start | bytes 98312 | tf_op jit(solution)/shard_map/ppermute | solution.py:326
  (1 other events, 1.1 us)

commit v5 on v4

--- a/solution.py
+++ b/solution.py
@@ -37,7 +37,10 @@
 
 def right_pairs(size, other_size):
     return [
-        (row * other_size + col, (2 * col + row % 2) * other_size + row // 2)
+        (
+            (2 * col + row % 2) * other_size + row // 8 * 4 + (row // 2 + 2) % 4,
+            row * other_size + col,
+        )
         for row in range(size)
         for col in range(other_size)
     ]
@@ -87,7 +90,7 @@
         + [whole(array) for array in fixed],
         out_specs=pl.BlockSpec((block, columns, channels), lambda step: (step, 0, 0)),
         out_shape=jax.ShapeDtypeStruct(table_part.shape, jnp.bfloat16),
-        compiler_params=pltpu.CompilerParams(vmem_limit_bytes=48 << 20),
+        compiler_params=pltpu.CompilerParams(vmem_limit_bytes=24 << 20),
         name="pair",
     )(table_part, left, *fixed)
 
@@ -96,11 +99,10 @@
     for start in range(0, hidden_ref.shape[0], 32):
         rows = slice(start, start + 32)
         values = hidden_ref[rows, :].astype(jnp.float32)
-        out_ref[rows, :] = layer_norm(values, gain_ref[...]).astype(jnp.bfloat16)
+        out_ref[rows, :] = layer_norm(values, gain_ref[...][None, :]).astype(jnp.bfloat16)
 
 
 def first_norm(hidden, gain):
-    gain = gain.reshape(1, -1)
     return pl.pallas_call(
         first_norm_kernel,
         grid=(1,),
@@ -220,14 +222,6 @@
     positions = lax.axis_index("row") * row_count + jnp.arange(row_count, dtype=jnp.int32)
     core = lax.rem(lax.axis_index("row"), 2)
     col_index = lax.axis_index("col")
-    half_columns = w_single.shape[1] // 2
-    own_part = lax.dynamic_slice_in_dim(w_single, core * half_columns, half_columns, 1)
-    own_part = (own_part.astype(jnp.float32) * final_gain[:, None]).astype(jnp.bfloat16)
-    own_part, hidden = lax.optimization_barrier((own_part, hidden))
-    quarter = [own_part] + [lax.ppermute(own_part, "col", flip_pairs(8, bit)) for bit in (1, 3, 2)]
-    quarter = jnp.concatenate(quarter, 0)
-    quarter_other = lax.ppermute(quarter, "row", flip_pairs(16, 1))
-
     attn_in = first_norm(hidden, attn_gain)
     keys = jnp.dot(attn_in, w_key, preferred_element_type=jnp.float32)
     keys = rotary(keys.reshape(row_count, local_heads, HD), positions).astype(jnp.bfloat16)
@@ -250,6 +244,14 @@
 
     own_half = jnp.concatenate(blocks, 0)
     other_half = lax.ppermute(own_half, "row", flip_pairs(16, 1))
+    own_half, w_single = lax.optimization_barrier((own_half, w_single))
+    half_columns = w_single.shape[1] // 2
+    own_part = lax.dynamic_slice_in_dim(w_single, core * half_columns, half_columns, 1)
+    own_part = (own_part.astype(jnp.float32) * final_gain[:, None]).astype(jnp.bfloat16)
+    quarter = [own_part] + [lax.ppermute(own_part, "col", flip_pairs(8, bit)) for bit in (1, 3, 2)]
+    quarter = jnp.concatenate(quarter, 0)
+    quarter_other = lax.ppermute(quarter, "row", flip_pairs(16, 1))
+
     incoming = jnp.concatenate([own_half, other_half], 0)
     both_query = jnp.concatenate([query, other_query], 0).reshape(-1, local_heads, HD)
     key_block = incoming[:, :local_width].reshape(-1, local_heads, HD)

time: 107 us -> 118 us (1.10)
  the two profiles are of different devices: /device:TPU:69 before, /device:TPU:1 now
where the time goes in v5:
time: 118 us; the launch traced here: 117 us
  waiting for transfers between devices  30.1 us (26%)
  starting transfers between devices  29.3 us (25%)
  Pallas kernels  23.8 us (20%)
  matrix products  15.9 us (13%)
  blocking collectives  7.88 us (7%)
  local copies, waits for them, and re-layouts  6.86 us (6%)
  other arithmetic  2.79 us (2%)
    pallas_call x1, Pallas kernels, pair_stage(): pl.pallas_call(pair_kernel, grid=(rows // block,), in_specs=[pl.BlockSpec...  20.5 us
    ppermute x3, waiting for transfers between devices, local(): lax.ppermute(own_part, 'col', flip_pairs(8, bit))  10.9 us
    all_to_all x1, blocking collectives, local(): lax.all_to_all(jnp.broadcast_to(both, (4,) + both.shape), 'col', 0, 0, ti...  7.88 us
    dot_general x1, matrix products, local(): jnp.einsum('ijb,bc->ijc', one_hot, rel_table, preferred_element_type=jnp....  7.48 us
    unnamed x32, local copies, waits for them, and re-layouts  6.6 us
    ppermute x3, waiting for transfers between devices, local(): lax.ppermute(stacked, 'row', flip_pairs(16, 2 * bit))  6.54 us
    all_to_all x1, starting transfers between devices, local(): lax.all_to_all(attn_part.reshape(8, own_count, half_width), 'col', 0, 0,...  6.09 us
    ppermute x3, starting transfers between devices, local(): lax.ppermute(stacked, 'row', flip_pairs(16, 2 * bit))  5.24 us
  transfers between devices with their start and end apart: 14, of which 8 were waited for; matrix products, arithmetic and copies ran while one was open for 12% of the time, Pallas kernels for 0%

profile of v5, /device:TPU:1, one launch (start us, length us, event | category | flops | bytes accessed | tf_op | source)
XLA Modules:
  0.0 117.1 jit_solution(10537077374431409890)
XLA Ops:
  2.5 2.1 %convolution_convert_fusion.1 = bf16[128,320]{0,1:T(8,128)(2,1)S(1)} fusion(bf16[128,2560]{1,0:T(8,128)(2,1)S(1)} %first_norm.1, bf16[2560,320]{0,1:T(8,128)(2,1)} %param.21), kind=kOutput, calls=%fused_computation.12 | convolution fusion | flops 209756160 | bytes 2375680 | tf_op jit(solution)/shard_map/dot_general | solution.py:228
  5.3 4.5 %collective-permute-start.3 = (bf16[128,640]{0,1:T(8,128)(2,1)S(1)}, bf16[128,640]{0,1:T(8,128)(2,1)S(1)}, u32[]{:S(2)}, u32[]{:S(2)}) collective-permute-start(bf16[128,640]{0,1:T(8,128)(2,1)S(1)} %pad_maximum_fusion.1), channel_id=1, source_target_pairs={{0,32},{8,40},{16,48},{24,56},{32,0},{40,8},{48,16},{56,24},{64,96... | collective-permute-start | bytes 491528 | tf_op jit(solution)/shard_map/ppermute | solution.py:232
  11.2 6.5 %collective-permute-done.1 = bf16[128,640]{0,1:T(8,128)(2,1)S(1)} collective-permute-done((bf16[128,640]{0,1:T(8,128)(2,1)S(1)}, bf16[128,640]{0,1:T(8,128)(2,1)S(1)}, u32[]{:S(2)}, u32[]{:S(2)}) %collective-permute-start.1) | collective-permute-done | bytes 163872 | tf_op jit(solution)/shard_map/ppermute | solution.py:232
  17.9 1.6 %collective-permute-start.4 = (bf16[512,640]{0,1:T(8,128)(2,1)S(1)}, bf16[512,640]{0,1:T(8,128)(2,1)S(1)}, u32[]{:S(2)}, u32[]{:S(2)}) collective-permute-start(bf16[512,640]{0,1:T(8,128)(2,1)S(1)} %constant_dynamic-update-slice_fusion), channel_id=1, source_target_pairs={{0,8},{8,0},{16,24},{24,16},{32,40},{40,32},{48,56},{56,48},{64,72... | collective-permute-start | bytes 1966088 | tf_op jit(solution)/shard_map/ppermute | solution.py:246
  19.5 1.3 %collective-permute-start = (bf16[128,320]{0,1:T(8,128)(2,1)S(1)}, bf16[128,320]{0,1:T(8,128)(2,1)}, u32[]{:S(2)}, u32[]{:S(2)}) collective-permute-start(bf16[128,320]{0,1:T(8,128)(2,1)S(1)} %fusion.17), channel_id=1, source_target_pairs={{0,64},{8,72},{16,80},{24,88},{32,96},{40,104},{48,112},{56,120},{... | collective-permute-start | bytes 245768 | tf_op jit(solution)/shard_map/ppermute | solution.py:237
  20.8 2.9 %collective-permute-done = bf16[128,320]{0,1:T(8,128)(2,1)} collective-permute-done((bf16[128,320]{0,1:T(8,128)(2,1)S(1)}, bf16[128,320]{0,1:T(8,128)(2,1)}, u32[]{:S(2)}, u32[]{:S(2)}) %collective-permute-start) | collective-permute-done | bytes 81952 | tf_op jit(solution)/shard_map/ppermute | solution.py:237
  25.8 3.0 %collective-permute-start.8 = (bf16[320,512]{1,0:T(8,128)(2,1)S(1)}, bf16[320,512]{1,0:T(8,128)(2,1)S(1)}, u32[]{:S(2)}, u32[]{:S(2)}) collective-permute-start(bf16[320,512]{1,0:T(8,128)(2,1)S(1)} %multiply_convert_fusion), channel_id=1, source_target_pairs={{0,2},{1,3},{2,0},{3,1},{4,6},{5,7},{6,4},{7,5},{8,10},{9,11},{10,... | collective-permute-start | bytes 983048 | tf_op jit(solution)/shard_map/ppermute | solution.py:251
  31.9 1.3 %collective-permute-start.5 = (bf16[128,384]{0,1:T(8,128)(2,1)S(1)}, bf16[128,384]{0,1:T(8,128)(2,1)S(1)}, u32[]{:S(2)}, u32[]{:S(2)}) collective-permute-start(bf16[128,384]{0,1:T(8,128)(2,1)S(1)} %fusion.26), channel_id=1, source_target_pairs={{0,64},{8,72},{16,80},{24,88},{32,96},{40,104},{48,112},{56,120},{... | collective-permute-start | bytes 294920 | tf_op jit(solution)/shard_map/ppermute | solution.py:278
  33.2 2.7 %collective-permute-done.8 = bf16[320,512]{1,0:T(8,128)(2,1)S(1)} collective-permute-done((bf16[320,512]{1,0:T(8,128)(2,1)S(1)}, bf16[320,512]{1,0:T(8,128)(2,1)S(1)}, u32[]{:S(2)}, u32[]{:S(2)}) %collective-permute-start.8) | collective-permute-done | bytes 327712 | tf_op jit(solution)/shard_map/ppermute | solution.py:251
  35.9 8.2 %collective-permute-done.7 = bf16[320,512]{1,0:T(8,128)(2,1)S(1)} collective-permute-done((bf16[320,512]{1,0:T(8,128)(2,1)S(1)}, bf16[320,512]{1,0:T(8,128)(2,1)S(1)}, u32[]{:S(2)}, u32[]{:S(2)}) %collective-permute-start.7) | collective-permute-done | bytes 327712 | tf_op jit(solution)/shard_map/ppermute | solution.py:251
  45.2 1.4 %convolution_convert_fusion = bf16[128,2,1280]{2,0,1:T(8,128)(2,1)} fusion(bf16[128,320,1]{0,1,2:T(8,128)(2,1)S(1)} %bitcast.81, bf16[40,2,8,1280]{3,2,1,0:T(8,128)(2,1)S(1)} %bitcast.76), kind=kOutput, calls=%fused_computation.7 | convolution fusion | flops 210042880 | bytes 2375680 | tf_op jit(solution)/shard_map/rk,kxn->xrn/dot_general | solution.py:286
  46.6 6.1 %all-to-all-start = ((bf16[8,32,1280]{2,1,0:T(8,128)(2,1)}), bf16[8,32,1280]{2,1,0:T(8,128)(2,1)}, u32[]{:S(2)}, u32[]{:S(2)}) async-start(bf16[8,32,1280]{2,1,0:T(8,128)(2,1)} %bitcast.75), calls=%async_computation | async-start | bytes 1310720 | tf_op jit(solution)/shard_map/all_to_all | solution.py:295
  52.8 7.5 %fusion.1.table_ref = bf16[128,256,128]{2,1,0:T(8,128)(2,1)} fusion(s32[128,256]{1,0:T(8,128)S(1)} %copy-done.12, bf16[65,128]{1,0:T(8,128)(2,1)} %param.28), kind=kOutput, calls=%fused_computation.2 | convolution fusion | flops 551583744 | bytes 8536320 | tf_op jit(solution)/shard_map/ijb,bc->ijc/dot_general | solution.py:241
  60.3 3.6 %all-to-all-done.parts_ref = bf16[8,32,1280]{2,1,0:T(8,128)(2,1)} async-done(((bf16[8,32,1280]{2,1,0:T(8,128)(2,1)}), bf16[8,32,1280]{2,1,0:T(8,128)(2,1)}, u32[]{:S(2)}, u32[]{:S(2)}) %all-to-all-start) | async-done | bytes 655392 | tf_op jit(solution)/shard_map/all_to_all | solution.py:295
  65.0 2.9 %half_sums.1 = (f32[48,1152]{1,0:T(8,128)S(1)}, bf16[48,1152]{1,0:T(8,128)(2,1)S(1)}) custom-call(s32[3]{0:T(128)S(1)} %pad_add_fusion.place_ref, bf16[8,32,1280]{2,1,0:T(8,128)(2,1)} %all-to-all-done.parts_ref, bf16[128,2560]{1,0:T(8,128)(2,1)S(1)} %copy-done.3, bf16[1280,512]{1,0:T(8,128)(2,1)S(1)} %pad_maximum_fusion.own_ref, ...), custom_call_target="tpu_custom_call" | custom-call | tf_op jit(solution)/shard_map/half_sums/pallas_call | solution.py:177
  67.9 2.5 %collective-permute-start.10 = (bf16[48,1152]{1,0:T(8,128)(2,1)S(1)}, bf16[48,1152]{1,0:T(8,128)(2,1)S(1)}, u32[]{:S(2)}, u32[]{:S(2)}) collective-permute-start(bf16[48,1152]{1,0:T(8,128)(2,1)S(1)} %get-tuple-element.24), channel_id=1, source_target_pairs={{0,4},{1,5},{2,6},{3,7},{4,0},{5,1},{6,2},{7,3},{8,12},{9,13},{10,... | collective-permute-start | bytes 331784 | tf_op jit(solution)/shard_map/ppermute | solution.py:301
  70.4 2.7 %collective-permute-done.10 = bf16[48,1152]{1,0:T(8,128)(2,1)S(1)} collective-permute-done((bf16[48,1152]{1,0:T(8,128)(2,1)S(1)}, bf16[48,1152]{1,0:T(8,128)(2,1)S(1)}, u32[]{:S(2)}, u32[]{:S(2)}) %collective-permute-start.10) | collective-permute-done | bytes 110624 | tf_op jit(solution)/shard_map/ppermute | solution.py:301
  73.3 1.8 %fusion.7 = bf16[32,256]{1,0:T(8,128)(2,1)S(1)} fusion(bf16[1024,1024]{1,0:T(8,128)(2,1)S(1)} %copy-done, bf16[1024,128]{1,0:T(8,128)(2,1)} %param.27, bf16[1024,128]{1,0:T(8,128)(2,1)} %param.26, f32[48,1152]{1,0:T(8,128)S(1)} %convert_element_type.78, f32[48,1152]{1,0:T(8,128)} %copy-done.6, f32[32]{0:T(128)S(1)} %get-tuple-element.26, ...), kind=kOutput, calls=%fused_computation.15 | convolution fusion | flops 85172224 | bytes 2905088 | tf_op jit(solution)/shard_map/dot_general | solution.py:315
  75.2 7.9 %all_to_all.10 = bf16[4,32,256]{2,1,0:T(8,128)(2,1)S(1)} all-to-all(bf16[4,32,256]{2,1,0:T(8,128)(2,1)S(1)} %broadcast_in_dim.2), channel_id=1, replica_groups={{0,1,2,3},{4,5,6,7},{8,9,10,11},{12,13,14,15},{16,17,18,19},{20,21,22,2..., dimensions={0} | all-to-all | bytes 131072 | tf_op jit(solution)/shard_map/all_to_all | solution.py:316
  83.1 1.8 %collective-permute-start.11 = (bf16[128,128]{1,0:T(8,128)(2,1)S(1)}, bf16[128,128]{1,0:T(8,128)(2,1)S(1)}, u32[]{:S(2)}, u32[]{:S(2)}) collective-permute-start(bf16[128,128]{1,0:T(8,128)(2,1)S(1)} %get-tuple-element.35), channel_id=1, source_target_pairs={{2,0},{18,1},{34,2},{50,3},{66,4},{82,5},{98,6},{114,7},{10,8},{26... | collective-permute-start | bytes 98312 | tf_op jit(solution)/shard_map/ppermute | solution.py:327
  84.8 2.6 %collective-permute-done.11 = bf16[128,128]{1,0:T(8,128)(2,1)S(1)} collective-permute-done((bf16[128,128]{1,0:T(8,128)(2,1)S(1)}, bf16[128,128]{1,0:T(8,128)(2,1)S(1)}, u32[]{:S(2)}, u32[]{:S(2)}) %collective-permute-start.11) | collective-permute-done | bytes 32800 | tf_op jit(solution)/shard_map/ppermute | solution.py:327
  87.4 4.9 %collective-permute-start.12 = (bf16[128,128]{1,0:T(8,128)(2,1)S(1)}, bf16[128,128]{1,0:T(8,128)(2,1)S(1)}, u32[]{:S(2)}, u32[]{:S(2)}) collective-permute-start(bf16[128,128]{1,0:T(8,128)(2,1)S(1)} %collective-permute-done.11), channel_id=1, source_target_pairs={{0,8},{8,0},{16,24},{24,16},{32,40},{40,32},{48,56},{56,48},{64,72... | collective-permute-start | bytes 98312 | tf_op jit(solution)/shard_map/ppermute | solution.py:328
  93.2 3.4 %copy-done.1 = bf16[128,256,128]{2,1,0:T(8,128)(2,1)S(1)} copy-done((bf16[128,256,128]{2,1,0:T(8,128)(2,1)S(1)}, bf16[128,256,128]{2,1,0:T(8,128)(2,1)}, u32[]{:S(2)}) %copy-start.1) | copy-done | bytes 8388632
  96.6 20.5 %pair.1 = bf16[128,256,128]{2,1,0:T(8,128)(2,1)} custom-call(bf16[128,256,128]{2,1,0:T(8,128)(2,1)S(1)} %copy-done.1, f32[128,128]{1,0:T(8,128)S(1)} %get-tuple-element.36.left_ref, f32[256,128]{1,0:T(8,128)S(1)} %maximum_convert_fusion.right_ref, f32[1,128]{1,0:T(1,128)S(1)} %bitcast.72, bf16[128,512]{1,0:T(8,128)(2,1)S(1)} %copy-done.4, ...), custom_call_target="tpu_custom_call" | custom-call | tf_op jit(solution)/shard_map/pair/pallas_call | solution.py:83
  (80 shorter events, 13.1 us)
Async XLA Ops:
  0.0 73.3 %copy-start = (bf16[1024,1024]{1,0:T(8,128)(2,1)S(1)}, bf16[1024,1024]{1,0:T(8,128)(2,1)}, u32[]{:S(2)}) copy-start(bf16[1024,1024]{1,0:T(8,128)(2,1)} %param.25) | copy-start | bytes 6291460
  4.6 5.9 %copy-start.10 = (bf16[2560,320]{0,1:T(8,128)(2,1)S(1)}, bf16[2560,320]{0,1:T(8,128)(2,1)}, u32[]{:S(2)}) copy-start(bf16[2560,320]{0,1:T(8,128)(2,1)} %param.19) | copy-start | bytes 4915204
  5.3 12.5 %collective-permute-start.3 = (bf16[128,640]{0,1:T(8,128)(2,1)S(1)}, bf16[128,640]{0,1:T(8,128)(2,1)S(1)}, u32[]{:S(2)}, u32[]{:S(2)}) collective-permute-start(bf16[128,640]{0,1:T(8,128)(2,1)S(1)} %pad_maximum_fusion.1), channel_id=1, source_target_pairs={{0,32},{8,40},{16,48},{24,56},{32,0},{40,8},{48,16},{56,24},{64,96... | collective-permute-start | bytes 491528 | tf_op jit(solution)/shard_map/ppermute | solution.py:232
  9.8 8.0 %collective-permute-start.2 = (bf16[128,640]{0,1:T(8,128)(2,1)S(1)}, bf16[128,640]{0,1:T(8,128)(2,1)S(1)}, u32[]{:S(2)}, u32[]{:S(2)}) collective-permute-start(bf16[128,640]{0,1:T(8,128)(2,1)S(1)} %pad_maximum_fusion.1), channel_id=1, source_target_pairs={{0,48},{8,56},{16,32},{24,40},{32,16},{40,24},{48,0},{56,8},{64,11... | collective-permute-start | bytes 491528 | tf_op jit(solution)/shard_map/ppermute | solution.py:232
  10.2 7.5 %collective-permute-start.1 = (bf16[128,640]{0,1:T(8,128)(2,1)S(1)}, bf16[128,640]{0,1:T(8,128)(2,1)S(1)}, u32[]{:S(2)}, u32[]{:S(2)}) collective-permute-start(bf16[128,640]{0,1:T(8,128)(2,1)S(1)} %pad_maximum_fusion.1), channel_id=1, source_target_pairs={{0,16},{8,24},{16,0},{24,8},{32,48},{40,56},{48,32},{56,40},{64,80... | collective-permute-start | bytes 491528 | tf_op jit(solution)/shard_map/ppermute | solution.py:232
  11.1 13.6 %copy-start.13 = (f32[320]{0:T(512)S(1)}, f32[320]{0:T(512)}, u32[]{:S(2)}) copy-start(f32[320]{0:T(512)} %param.23) | copy-start | bytes 3844
  17.9 11.8 %collective-permute-start.4 = (bf16[512,640]{0,1:T(8,128)(2,1)S(1)}, bf16[512,640]{0,1:T(8,128)(2,1)S(1)}, u32[]{:S(2)}, u32[]{:S(2)}) collective-permute-start(bf16[512,640]{0,1:T(8,128)(2,1)S(1)} %constant_dynamic-update-slice_fusion), channel_id=1, source_target_pairs={{0,8},{8,0},{16,24},{24,16},{32,40},{40,32},{48,56},{56,48},{64,72... | collective-permute-start | bytes 1966088 | tf_op jit(solution)/shard_map/ppermute | solution.py:246
  19.5 4.2 %collective-permute-start = (bf16[128,320]{0,1:T(8,128)(2,1)S(1)}, bf16[128,320]{0,1:T(8,128)(2,1)}, u32[]{:S(2)}, u32[]{:S(2)}) collective-permute-start(bf16[128,320]{0,1:T(8,128)(2,1)S(1)} %fusion.17), channel_id=1, source_target_pairs={{0,64},{8,72},{16,80},{24,88},{32,96},{40,104},{48,112},{56,120},{... | collective-permute-start | bytes 245768 | tf_op jit(solution)/shard_map/ppermute | solution.py:237
  25.8 10.1 %collective-permute-start.8 = (bf16[320,512]{1,0:T(8,128)(2,1)S(1)}, bf16[320,512]{1,0:T(8,128)(2,1)S(1)}, u32[]{:S(2)}, u32[]{:S(2)}) collective-permute-start(bf16[320,512]{1,0:T(8,128)(2,1)S(1)} %multiply_convert_fusion), channel_id=1, source_target_pairs={{0,2},{1,3},{2,0},{3,1},{4,6},{5,7},{6,4},{7,5},{8,10},{9,11},{10,... | collective-permute-start | bytes 983048 | tf_op jit(solution)/shard_map/ppermute | solution.py:251
  28.8 15.2 %collective-permute-start.7 = (bf16[320,512]{1,0:T(8,128)(2,1)S(1)}, bf16[320,512]{1,0:T(8,128)(2,1)S(1)}, u32[]{:S(2)}, u32[]{:S(2)}) collective-permute-start(bf16[320,512]{1,0:T(8,128)(2,1)S(1)} %multiply_convert_fusion), channel_id=1, source_target_pairs={{0,3},{1,2},{2,1},{3,0},{4,7},{5,6},{6,5},{7,4},{8,11},{9,10},{10,... | collective-permute-start | bytes 983048 | tf_op jit(solution)/shard_map/ppermute | solution.py:251
  29.6 14.5 %collective-permute-start.6 = (bf16[320,512]{1,0:T(8,128)(2,1)S(1)}, bf16[320,512]{1,0:T(8,128)(2,1)S(1)}, u32[]{:S(2)}, u32[]{:S(2)}) collective-permute-start(bf16[320,512]{1,0:T(8,128)(2,1)S(1)} %multiply_convert_fusion), channel_id=1, source_target_pairs={{0,1},{1,0},{2,3},{3,2},{4,5},{5,4},{6,7},{7,6},{8,9},{9,8},{10,11... | collective-permute-start | bytes 983048 | tf_op jit(solution)/shard_map/ppermute | solution.py:251
  31.9 13.3 %copy-start.11 = (bf16[320,2560]{1,0:T(8,128)(2,1)S(1)}, bf16[320,2560]{1,0:T(8,128)(2,1)}, u32[]{:S(2)}) copy-start(bf16[320,2560]{1,0:T(8,128)(2,1)} %param.22) | copy-start | bytes 4915204
  31.9 13.2 %collective-permute-start.5 = (bf16[128,384]{0,1:T(8,128)(2,1)S(1)}, bf16[128,384]{0,1:T(8,128)(2,1)S(1)}, u32[]{:S(2)}, u32[]{:S(2)}) collective-permute-start(bf16[128,384]{0,1:T(8,128)(2,1)S(1)} %fusion.26), channel_id=1, source_target_pairs={{0,64},{8,72},{16,80},{24,88},{32,96},{40,104},{48,112},{56,120},{... | collective-permute-start | bytes 294920 | tf_op jit(solution)/shard_map/ppermute | solution.py:278
  44.1 19.7 %collective-permute-start.9 = (bf16[1280,512]{1,0:T(8,128)(2,1)S(1)}, bf16[1280,512]{1,0:T(8,128)(2,1)}, u32[]{:S(2)}, u32[]{:S(2)}) collective-permute-start(bf16[1280,512]{1,0:T(8,128)(2,1)S(1)} %pad_maximum_fusion.own_ref), channel_id=1, source_target_pairs={{0,8},{8,0},{16,24},{24,16},{32,40},{40,32},{48,56},{56,48},{64,72... | collective-permute-start | bytes 3932168 | tf_op jit(solution)/shard_map/ppermute | solution.py:253
  45.2 7.6 %copy-start.12 = (s32[128,256]{1,0:T(8,128)S(1)}, s32[128,256]{1,0:T(8,128)}, u32[]{:S(2)}) copy-start(s32[128,256]{1,0:T(8,128)} %param.17) | copy-start | bytes 393220
  46.6 17.3 %all-to-all-start = ((bf16[8,32,1280]{2,1,0:T(8,128)(2,1)}), bf16[8,32,1280]{2,1,0:T(8,128)(2,1)}, u32[]{:S(2)}, u32[]{:S(2)}) async-start(bf16[8,32,1280]{2,1,0:T(8,128)(2,1)} %bitcast.75), calls=%async_computation | async-start | bytes 1310720 | tf_op jit(solution)/shard_map/all_to_all | solution.py:295
  67.8 5.4 %copy-start.6 = (f32[48,1152]{1,0:T(8,128)}, f32[48,1152]{1,0:T(8,128)S(1)}, u32[]{:S(2)}) copy-start(f32[48,1152]{1,0:T(8,128)S(1)} %get-tuple-element.23) | copy-start | bytes 663556
  67.9 5.2 %collective-permute-start.10 = (bf16[48,1152]{1,0:T(8,128)(2,1)S(1)}, bf16[48,1152]{1,0:T(8,128)(2,1)S(1)}, u32[]{:S(2)}, u32[]{:S(2)}) collective-permute-start(bf16[48,1152]{1,0:T(8,128)(2,1)S(1)} %get-tuple-element.24), channel_id=1, source_target_pairs={{0,4},{1,5},{2,6},{3,7},{4,0},{5,1},{6,2},{7,3},{8,12},{9,13},{10,... | collective-permute-start | bytes 331784 | tf_op jit(solution)/shard_map/ppermute | solution.py:301
  73.3 19.9 %copy-start.4 = (bf16[128,512]{1,0:T(8,128)(2,1)S(1)}, bf16[128,512]{1,0:T(8,128)(2,1)}, u32[]{:S(2)}) copy-start(bf16[128,512]{1,0:T(8,128)(2,1)} %expand_ref.1) | copy-start | bytes 393220
  73.3 19.9 %copy-start.5 = (bf16[512,128]{1,0:T(8,128)(2,1)S(1)}, bf16[512,128]{1,0:T(8,128)(2,1)}, u32[]{:S(2)}) copy-start(bf16[512,128]{1,0:T(8,128)(2,1)} %contract_ref.1) | copy-start | bytes 393220
  73.3 19.9 %copy-start.8 = (f32[128]{0:T(128)S(1)}, f32[128]{0:T(128)}, u32[]{:S(2)}) copy-start(f32[128]{0:T(128)} %param.29) | copy-start | bytes 1540
  83.1 4.4 %collective-permute-start.11 = (bf16[128,128]{1,0:T(8,128)(2,1)S(1)}, bf16[128,128]{1,0:T(8,128)(2,1)S(1)}, u32[]{:S(2)}, u32[]{:S(2)}) collective-permute-start(bf16[128,128]{1,0:T(8,128)(2,1)S(1)} %get-tuple-element.35), channel_id=1, source_target_pairs={{2,0},{18,1},{34,2},{50,3},{66,4},{82,5},{98,6},{114,7},{10,8},{26... | collective-permute-start | bytes 98312 | tf_op jit(solution)/shard_map/ppermute | solution.py:327
  87.4 5.7 %collective-permute-start.12 = (bf16[128,128]{1,0:T(8,128)(2,1)S(1)}, bf16[128,128]{1,0:T(8,128)(2,1)S(1)}, u32[]{:S(2)}, u32[]{:S(2)}) collective-permute-start(bf16[128,128]{1,0:T(8,128)(2,1)S(1)} %collective-permute-done.11), channel_id=1, source_target_pairs={{0,8},{8,0},{16,24},{24,16},{32,40},{40,32},{48,56},{56,48},{64,72... | collective-permute-start | bytes 98312 | tf_op jit(solution)/shard_map/ppermute | solution.py:328
  93.2 3.4 %copy-start.1 = (bf16[128,256,128]{2,1,0:T(8,128)(2,1)S(1)}, bf16[128,256,128]{2,1,0:T(8,128)(2,1)}, u32[]{:S(2)}) copy-start(bf16[128,256,128]{2,1,0:T(8,128)(2,1)} %fusion.1.table_ref) | copy-start | bytes 25165828
  (4 other events, 5.5 us)

commit v6 on v4

--- a/solution.py
+++ b/solution.py
@@ -37,7 +37,10 @@
 
 def right_pairs(size, other_size):
     return [
-        (row * other_size + col, (2 * col + row % 2) * other_size + row // 2)
+        (
+            (2 * col + row % 2) * other_size + row // 8 * 4 + (row // 2 + 2) % 4,
+            row * other_size + col,
+        )
         for row in range(size)
         for col in range(other_size)
     ]
@@ -96,11 +99,10 @@
     for start in range(0, hidden_ref.shape[0], 32):
         rows = slice(start, start + 32)
         values = hidden_ref[rows, :].astype(jnp.float32)
-        out_ref[rows, :] = layer_norm(values, gain_ref[...]).astype(jnp.bfloat16)
+        out_ref[rows, :] = layer_norm(values, gain_ref[...][None, :]).astype(jnp.bfloat16)
 
 
 def first_norm(hidden, gain):
-    gain = gain.reshape(1, -1)
     return pl.pallas_call(
         first_norm_kernel,
         grid=(1,),

time: 107 us -> 103 us (0.963)
  the two profiles are of different devices: /device:TPU:69 before, /device:TPU:1 now
where the time goes in v6:
time: 103 us; the launch traced here: 102 us
  starting transfers between devices  32.4 us (31%)
  Pallas kernels  25.3 us (25%)
  matrix products  16.1 us (16%)
  waiting for transfers between devices  14 us (14%)
  blocking collectives  6.87 us (7%)
  local copies, waits for them, and re-layouts  5.23 us (5%)
  other arithmetic  2.05 us (2%)
    pallas_call x1, Pallas kernels, pair_stage(): pl.pallas_call(pair_kernel, grid=(rows // block,), in_specs=[pl.BlockSpec...  21.8 us
    dot_general x1, matrix products, local(): jnp.einsum('ijb,bc->ijc', one_hot, rel_table, preferred_element_type=jnp....  7.63 us
    ppermute x1, starting transfers between devices, local(): other_right = lax.ppermute(own_right, 'row', flip_pairs(16, 1))  7.28 us
    all_to_all x1, blocking collectives, local(): lax.all_to_all(jnp.broadcast_to(both, (4,) + both.shape), 'col', 0, 0, ti...  6.87 us
    ppermute x3, waiting for transfers between devices, local(): lax.ppermute(stacked, 'row', flip_pairs(16, 2 * bit))  5.62 us
    all_to_all x1, starting transfers between devices, local(): lax.all_to_all(attn_part.reshape(8, own_count, half_width), 'col', 0, 0,...  5.33 us
    ppermute x3, starting transfers between devices, local(): lax.ppermute(own_part, 'col', flip_pairs(8, bit))  4.6 us
    ppermute x3, starting transfers between devices, local(): lax.ppermute(stacked, 'row', flip_pairs(16, 2 * bit))  4.41 us
  transfers between devices with their start and end apart: 14, of which 7 were waited for; matrix products, arithmetic and copies ran while one was open for 18% of the time, Pallas kernels for 0%

profile of v6, /device:TPU:1, one launch (start us, length us, event | category | flops | bytes accessed | tf_op | source)
XLA Modules:
  0.0 102.4 jit_solution(11044403524919017848)
XLA Ops:
  0.0 1.3 %multiply_convert_fusion = bf16[320,512]{1,0:T(8,128)(2,1)S(1)} fusion(f32[320]{0:T(512)} %param.23, bf16[320,1024]{1,0:T(8,128)(2,1)} %param.24, s32[]{:T(128)S(6)} %select_n.20), kind=kLoop, calls=%fused_computation.16 | loop fusion | flops 491520 | bytes 656644 | tf_op jit(solution)/shard_map/convert_element_type | solution.py:227
  1.3 3.8 %collective-permute-start.8 = (bf16[320,512]{1,0:T(8,128)(2,1)S(1)}, bf16[320,512]{1,0:T(8,128)(2,1)S(1)}, u32[]{:S(2)}, u32[]{:S(2)}) collective-permute-start(bf16[320,512]{1,0:T(8,128)(2,1)S(1)} %multiply_convert_fusion), channel_id=1, source_target_pairs={{0,2},{1,3},{2,0},{3,1},{4,6},{5,7},{6,4},{7,5},{8,10},{9,11},{10,... | collective-permute-start | bytes 983048 | tf_op jit(solution)/shard_map/ppermute | solution.py:229
  6.1 1.1 %copy-done.1 = bf16[128,2560]{1,0:T(8,128)(2,1)S(1)} copy-done((bf16[128,2560]{1,0:T(8,128)(2,1)S(1)}, bf16[128,2560]{1,0:T(8,128)(2,1)}, u32[]{:S(2)}) %copy-start.1) | copy-done | bytes 655384
  8.2 2.1 %convolution_convert_fusion.1 = bf16[128,320]{0,1:T(8,128)(2,1)S(1)} fusion(bf16[128,2560]{1,0:T(8,128)(2,1)S(1)} %first_norm.1, bf16[2560,320]{0,1:T(8,128)(2,1)} %param.21), kind=kOutput, calls=%fused_computation.11 | convolution fusion | flops 209756160 | bytes 2375680 | tf_op jit(solution)/shard_map/dot_general | solution.py:236
  11.1 3.7 %collective-permute-start.3 = (bf16[128,640]{0,1:T(8,128)(2,1)S(1)}, bf16[128,640]{0,1:T(8,128)(2,1)S(1)}, u32[]{:S(2)}, u32[]{:S(2)}) collective-permute-start(bf16[128,640]{0,1:T(8,128)(2,1)S(1)} %pad_maximum_fusion.1), channel_id=1, source_target_pairs={{0,32},{8,40},{16,48},{24,56},{32,0},{40,8},{48,16},{56,24},{64,96... | collective-permute-start | bytes 491528 | tf_op jit(solution)/shard_map/ppermute | solution.py:240
  16.9 1.1 %collective-permute-done.3 = bf16[128,640]{0,1:T(8,128)(2,1)S(1)} collective-permute-done((bf16[128,640]{0,1:T(8,128)(2,1)S(1)}, bf16[128,640]{0,1:T(8,128)(2,1)S(1)}, u32[]{:S(2)}, u32[]{:S(2)}) %collective-permute-start.3) | collective-permute-done | bytes 163872 | tf_op jit(solution)/shard_map/ppermute | solution.py:240
  18.0 4.5 %collective-permute-done.2 = bf16[128,640]{0,1:T(8,128)(2,1)S(1)} collective-permute-done((bf16[128,640]{0,1:T(8,128)(2,1)S(1)}, bf16[128,640]{0,1:T(8,128)(2,1)S(1)}, u32[]{:S(2)}, u32[]{:S(2)}) %collective-permute-start.2) | collective-permute-done | bytes 163872 | tf_op jit(solution)/shard_map/ppermute | solution.py:240
  22.5 1.2 %collective-permute-start = (bf16[128,320]{0,1:T(8,128)(2,1)S(1)}, bf16[128,320]{0,1:T(8,128)(2,1)S(1)}, u32[]{:S(2)}, u32[]{:S(2)}) collective-permute-start(bf16[128,320]{0,1:T(8,128)(2,1)S(1)} %fusion.17), channel_id=1, source_target_pairs={{0,64},{8,72},{16,80},{24,88},{32,96},{40,104},{48,112},{56,120},{... | collective-permute-start | bytes 245768 | tf_op jit(solution)/shard_map/ppermute | solution.py:245
  23.8 1.2 %collective-permute-start.4 = (bf16[512,640]{0,1:T(8,128)(2,1)S(1)}, bf16[512,640]{0,1:T(8,128)(2,1)S(1)}, u32[]{:S(2)}, u32[]{:S(2)}) collective-permute-start(bf16[512,640]{0,1:T(8,128)(2,1)S(1)} %pad_maximum_fusion), channel_id=1, source_target_pairs={{0,8},{8,0},{16,24},{24,16},{32,40},{40,32},{48,56},{56,48},{64,72... | collective-permute-start | bytes 1966088 | tf_op jit(solution)/shard_map/ppermute | solution.py:254
  25.0 1.1 %collective-permute-done = bf16[128,320]{0,1:T(8,128)(2,1)S(1)} collective-permute-done((bf16[128,320]{0,1:T(8,128)(2,1)S(1)}, bf16[128,320]{0,1:T(8,128)(2,1)S(1)}, u32[]{:S(2)}, u32[]{:S(2)}) %collective-permute-start) | collective-permute-done | bytes 81952 | tf_op jit(solution)/shard_map/ppermute | solution.py:245
  30.1 1.3 %collective-permute-start.5 = (bf16[128,384]{0,1:T(8,128)(2,1)S(1)}, bf16[128,384]{0,1:T(8,128)(2,1)S(1)}, u32[]{:S(2)}, u32[]{:S(2)}) collective-permute-start(bf16[128,384]{0,1:T(8,128)(2,1)S(1)} %fusion.26), channel_id=1, source_target_pairs={{0,64},{8,72},{16,80},{24,88},{32,96},{40,104},{48,112},{56,120},{... | collective-permute-start | bytes 294920 | tf_op jit(solution)/shard_map/ppermute | solution.py:278
  32.1 2.1 %collective-permute-start.9 = (bf16[1280,512]{1,0:T(8,128)(2,1)}, bf16[1280,512]{1,0:T(8,128)(2,1)}, u32[]{:S(2)}, u32[]{:S(2)}) collective-permute-start(bf16[1280,512]{1,0:T(8,128)(2,1)} %constant_dynamic-update-slice_fusion.5.own_ref), channel_id=1, source_target_pairs={{0,8},{8,0},{16,24},{24,16},{32,40},{40,32},{48,56},{56,48},{64,72... | collective-permute-start | bytes 3932168 | tf_op jit(solution)/shard_map/ppermute | solution.py:231
  34.3 1.4 %convolution_convert_fusion = bf16[128,2,1280]{2,0,1:T(8,128)(2,1)} fusion(bf16[128,320,1]{0,1,2:T(8,128)(2,1)S(1)} %bitcast.80, bf16[40,2,8,1280]{3,2,1,0:T(8,128)(2,1)S(1)} %bitcast.75), kind=kOutput, calls=%fused_computation.7 | convolution fusion | flops 210042880 | bytes 2375680 | tf_op jit(solution)/shard_map/rk,kxn->xrn/dot_general | solution.py:286
  35.7 5.3 %all-to-all-start = ((bf16[8,32,1280]{2,1,0:T(8,128)(2,1)}), bf16[8,32,1280]{2,1,0:T(8,128)(2,1)S(1)}, u32[]{:S(2)}, u32[]{:S(2)}) async-start(bf16[8,32,1280]{2,1,0:T(8,128)(2,1)} %bitcast.17), calls=%async_computation | async-start | bytes 1310720 | tf_op jit(solution)/shard_map/all_to_all | solution.py:295
  41.1 7.6 %fusion.1.table_ref = bf16[128,256,128]{2,1,0:T(8,128)(2,1)} fusion(s32[128,256]{1,0:T(8,128)S(1)} %copy-done.11, bf16[65,128]{1,0:T(8,128)(2,1)} %param.28), kind=kOutput, calls=%fused_computation.2 | convolution fusion | flops 551583744 | bytes 8536320 | tf_op jit(solution)/shard_map/ijb,bc->ijc/dot_general | solution.py:249
  48.8 1.7 %all-to-all-done.parts_ref = bf16[8,32,1280]{2,1,0:T(8,128)(2,1)S(1)} async-done(((bf16[8,32,1280]{2,1,0:T(8,128)(2,1)}), bf16[8,32,1280]{2,1,0:T(8,128)(2,1)S(1)}, u32[]{:S(2)}, u32[]{:S(2)}) %all-to-all-start) | async-done | bytes 655392 | tf_op jit(solution)/shard_map/all_to_all | solution.py:295
  50.4 3.1 %half_sums.1 = (f32[48,1152]{1,0:T(8,128)S(1)}, bf16[48,1152]{1,0:T(8,128)(2,1)S(1)}) custom-call(s32[3]{0:T(128)S(1)} %pad_add_fusion.place_ref, bf16[8,32,1280]{2,1,0:T(8,128)(2,1)S(1)} %all-to-all-done.parts_ref, bf16[128,2560]{1,0:T(8,128)(2,1)S(1)} %copy-done.2, bf16[1280,512]{1,0:T(8,128)(2,1)} %constant_dynamic-update-slice_fusion.5.own_ref, ...), custom_call_target="tpu_custom_call" | custom-call | tf_op jit(solution)/shard_map/half_sums/pallas_call | solution.py:177
  53.5 1.4 %collective-permute-start.10 = (bf16[48,1152]{1,0:T(8,128)(2,1)S(1)}, bf16[48,1152]{1,0:T(8,128)(2,1)S(1)}, u32[]{:S(2)}, u32[]{:S(2)}) collective-permute-start(bf16[48,1152]{1,0:T(8,128)(2,1)S(1)} %get-tuple-element.24), channel_id=1, source_target_pairs={{0,4},{1,5},{2,6},{3,7},{4,0},{5,1},{6,2},{7,3},{8,12},{9,13},{10,... | collective-permute-start | bytes 331784 | tf_op jit(solution)/shard_map/ppermute | solution.py:301
  54.9 3.8 %collective-permute-done.10 = bf16[48,1152]{1,0:T(8,128)(2,1)S(1)} collective-permute-done((bf16[48,1152]{1,0:T(8,128)(2,1)S(1)}, bf16[48,1152]{1,0:T(8,128)(2,1)S(1)}, u32[]{:S(2)}, u32[]{:S(2)}) %collective-permute-start.10) | collective-permute-done | bytes 110624 | tf_op jit(solution)/shard_map/ppermute | solution.py:301
  59.0 1.8 %fusion.7 = bf16[32,256]{1,0:T(8,128)(2,1)S(1)} fusion(bf16[1024,1024]{1,0:T(8,128)(2,1)S(1)} %copy-done, bf16[1024,128]{1,0:T(8,128)(2,1)} %param.27, bf16[1024,128]{1,0:T(8,128)(2,1)} %param.26, f32[48,1152]{1,0:T(8,128)S(1)} %convert_element_type.78, f32[48,1152]{1,0:T(8,128)} %copy-done.5, f32[32]{0:T(128)S(1)} %get-tuple-element.26, ...), kind=kOutput, calls=%fused_computation.14 | convolution fusion | flops 85172224 | bytes 2905088 | tf_op jit(solution)/shard_map/dot_general | solution.py:315
  60.8 6.9 %all_to_all.10 = bf16[4,32,256]{2,1,0:T(8,128)(2,1)S(1)} all-to-all(bf16[4,32,256]{2,1,0:T(8,128)(2,1)S(1)} %broadcast_in_dim.2), channel_id=1, replica_groups={{0,1,2,3},{4,5,6,7},{8,9,10,11},{12,13,14,15},{16,17,18,19},{20,21,22,2..., dimensions={0} | all-to-all | bytes 131072 | tf_op jit(solution)/shard_map/all_to_all | solution.py:316
  67.7 3.6 %collective-permute-start.11 = (bf16[128,128]{1,0:T(8,128)(2,1)S(1)}, bf16[128,128]{1,0:T(8,128)(2,1)S(1)}, u32[]{:S(2)}, u32[]{:S(2)}) collective-permute-start(bf16[128,128]{1,0:T(8,128)(2,1)S(1)} %get-tuple-element.35), channel_id=1, source_target_pairs={{2,0},{18,1},{34,2},{50,3},{66,4},{82,5},{98,6},{114,7},{10,8},{26... | collective-permute-start | bytes 98312 | tf_op jit(solution)/shard_map/ppermute | solution.py:327
  72.3 7.3 %collective-permute-start.12 = (bf16[128,128]{1,0:T(8,128)(2,1)S(1)}, bf16[128,128]{1,0:T(8,128)(2,1)S(1)}, u32[]{:S(2)}, u32[]{:S(2)}) collective-permute-start(bf16[128,128]{1,0:T(8,128)(2,1)S(1)} %collective-permute-done.11), channel_id=1, source_target_pairs={{0,8},{8,0},{16,24},{24,16},{32,40},{40,32},{48,56},{56,48},{64,72... | collective-permute-start | bytes 98312 | tf_op jit(solution)/shard_map/ppermute | solution.py:328
  80.6 21.8 %pair.1 = bf16[128,256,128]{2,1,0:T(8,128)(2,1)} custom-call(bf16[128,256,128]{2,1,0:T(8,128)(2,1)} %fusion.1.table_ref, f32[128,128]{1,0:T(8,128)S(1)} %get-tuple-element.36.left_ref, f32[256,128]{1,0:T(8,128)S(1)} %maximum_convert_fusion.right_ref, f32[1,128]{1,0:T(1,128)S(1)} %bitcast.72, bf16[128,512]{1,0:T(8,128)(2,1)S(1)} %copy-done.3, ...), custom_call_target="tpu_custom_call" | custom-call | tf_op jit(solution)/shard_map/pair/pallas_call | solution.py:83
  (79 shorter events, 11.9 us)
Async XLA Ops:
  0.0 58.9 %copy-start = (bf16[1024,1024]{1,0:T(8,128)(2,1)S(1)}, bf16[1024,1024]{1,0:T(8,128)(2,1)}, u32[]{:S(2)}) copy-start(bf16[1024,1024]{1,0:T(8,128)(2,1)} %param.25) | copy-start | bytes 6291460
  1.3 30.1 %collective-permute-start.8 = (bf16[320,512]{1,0:T(8,128)(2,1)S(1)}, bf16[320,512]{1,0:T(8,128)(2,1)S(1)}, u32[]{:S(2)}, u32[]{:S(2)}) collective-permute-start(bf16[320,512]{1,0:T(8,128)(2,1)S(1)} %multiply_convert_fusion), channel_id=1, source_target_pairs={{0,2},{1,3},{2,0},{3,1},{4,6},{5,7},{6,4},{7,5},{8,10},{9,11},{10,... | collective-permute-start | bytes 983048 | tf_op jit(solution)/shard_map/ppermute | solution.py:229
  5.1 22.0 %collective-permute-start.7 = (bf16[320,512]{1,0:T(8,128)(2,1)S(1)}, bf16[320,512]{1,0:T(8,128)(2,1)S(1)}, u32[]{:S(2)}, u32[]{:S(2)}) collective-permute-start(bf16[320,512]{1,0:T(8,128)(2,1)S(1)} %multiply_convert_fusion), channel_id=1, source_target_pairs={{0,3},{1,2},{2,1},{3,0},{4,7},{5,6},{6,5},{7,4},{8,11},{9,10},{10,... | collective-permute-start | bytes 983048 | tf_op jit(solution)/shard_map/ppermute | solution.py:229
  7.8 2.5 %copy-start.8 = (bf16[2560,320]{0,1:T(8,128)(2,1)S(1)}, bf16[2560,320]{0,1:T(8,128)(2,1)}, u32[]{:S(2)}) copy-start(bf16[2560,320]{0,1:T(8,128)(2,1)} %param.20) | copy-start | bytes 4915204
  10.4 5.1 %copy-start.9 = (bf16[2560,320]{0,1:T(8,128)(2,1)S(1)}, bf16[2560,320]{0,1:T(8,128)(2,1)}, u32[]{:S(2)}) copy-start(bf16[2560,320]{0,1:T(8,128)(2,1)} %param.19) | copy-start | bytes 4915204
  11.1 7.0 %collective-permute-start.3 = (bf16[128,640]{0,1:T(8,128)(2,1)S(1)}, bf16[128,640]{0,1:T(8,128)(2,1)S(1)}, u32[]{:S(2)}, u32[]{:S(2)}) collective-permute-start(bf16[128,640]{0,1:T(8,128)(2,1)S(1)} %pad_maximum_fusion.1), channel_id=1, source_target_pairs={{0,32},{8,40},{16,48},{24,56},{32,0},{40,8},{48,16},{56,24},{64,96... | collective-permute-start | bytes 491528 | tf_op jit(solution)/shard_map/ppermute | solution.py:240
  14.7 7.8 %collective-permute-start.2 = (bf16[128,640]{0,1:T(8,128)(2,1)S(1)}, bf16[128,640]{0,1:T(8,128)(2,1)S(1)}, u32[]{:S(2)}, u32[]{:S(2)}) collective-permute-start(bf16[128,640]{0,1:T(8,128)(2,1)S(1)} %pad_maximum_fusion.1), channel_id=1, source_target_pairs={{0,48},{8,56},{16,32},{24,40},{32,16},{40,24},{48,0},{56,8},{64,11... | collective-permute-start | bytes 491528 | tf_op jit(solution)/shard_map/ppermute | solution.py:240
  15.2 8.6 %collective-permute-start.1 = (bf16[128,640]{0,1:T(8,128)(2,1)S(1)}, bf16[128,640]{0,1:T(8,128)(2,1)S(1)}, u32[]{:S(2)}, u32[]{:S(2)}) collective-permute-start(bf16[128,640]{0,1:T(8,128)(2,1)S(1)} %pad_maximum_fusion.1), channel_id=1, source_target_pairs={{0,16},{8,24},{16,0},{24,8},{32,48},{40,56},{48,32},{56,40},{64,80... | collective-permute-start | bytes 491528 | tf_op jit(solution)/shard_map/ppermute | solution.py:240
  18.0 8.3 %collective-permute-start.6 = (bf16[320,512]{1,0:T(8,128)(2,1)S(1)}, bf16[320,512]{1,0:T(8,128)(2,1)S(1)}, u32[]{:S(2)}, u32[]{:S(2)}) collective-permute-start(bf16[320,512]{1,0:T(8,128)(2,1)S(1)} %multiply_convert_fusion), channel_id=1, source_target_pairs={{0,1},{1,0},{2,3},{3,2},{4,5},{5,4},{6,7},{7,6},{8,9},{9,8},{10,11... | collective-permute-start | bytes 983048 | tf_op jit(solution)/shard_map/ppermute | solution.py:229
  22.5 3.6 %collective-permute-start = (bf16[128,320]{0,1:T(8,128)(2,1)S(1)}, bf16[128,320]{0,1:T(8,128)(2,1)S(1)}, u32[]{:S(2)}, u32[]{:S(2)}) collective-permute-start(bf16[128,320]{0,1:T(8,128)(2,1)S(1)} %fusion.17), channel_id=1, source_target_pairs={{0,64},{8,72},{16,80},{24,88},{32,96},{40,104},{48,112},{56,120},{... | collective-permute-start | bytes 245768 | tf_op jit(solution)/shard_map/ppermute | solution.py:245
  23.8 4.0 %collective-permute-start.4 = (bf16[512,640]{0,1:T(8,128)(2,1)S(1)}, bf16[512,640]{0,1:T(8,128)(2,1)S(1)}, u32[]{:S(2)}, u32[]{:S(2)}) collective-permute-start(bf16[512,640]{0,1:T(8,128)(2,1)S(1)} %pad_maximum_fusion), channel_id=1, source_target_pairs={{0,8},{8,0},{16,24},{24,16},{32,40},{40,32},{48,56},{56,48},{64,72... | collective-permute-start | bytes 1966088 | tf_op jit(solution)/shard_map/ppermute | solution.py:254
  30.0 4.3 %copy-start.10 = (bf16[320,2560]{1,0:T(8,128)(2,1)S(1)}, bf16[320,2560]{1,0:T(8,128)(2,1)}, u32[]{:S(2)}) copy-start(bf16[320,2560]{1,0:T(8,128)(2,1)} %param.22) | copy-start | bytes 4915204
  30.1 4.1 %collective-permute-start.5 = (bf16[128,384]{0,1:T(8,128)(2,1)S(1)}, bf16[128,384]{0,1:T(8,128)(2,1)S(1)}, u32[]{:S(2)}, u32[]{:S(2)}) collective-permute-start(bf16[128,384]{0,1:T(8,128)(2,1)S(1)} %fusion.26), channel_id=1, source_target_pairs={{0,64},{8,72},{16,80},{24,88},{32,96},{40,104},{48,112},{56,120},{... | collective-permute-start | bytes 294920 | tf_op jit(solution)/shard_map/ppermute | solution.py:278
  32.1 18.3 %collective-permute-start.9 = (bf16[1280,512]{1,0:T(8,128)(2,1)}, bf16[1280,512]{1,0:T(8,128)(2,1)}, u32[]{:S(2)}, u32[]{:S(2)}) collective-permute-start(bf16[1280,512]{1,0:T(8,128)(2,1)} %constant_dynamic-update-slice_fusion.5.own_ref), channel_id=1, source_target_pairs={{0,8},{8,0},{16,24},{24,16},{32,40},{40,32},{48,56},{56,48},{64,72... | collective-permute-start | bytes 3932168 | tf_op jit(solution)/shard_map/ppermute | solution.py:231
  34.3 6.8 %copy-start.11 = (s32[128,256]{1,0:T(8,128)S(1)}, s32[128,256]{1,0:T(8,128)}, u32[]{:S(2)}) copy-start(s32[128,256]{1,0:T(8,128)} %param.17) | copy-start | bytes 393220
  35.7 14.7 %all-to-all-start = ((bf16[8,32,1280]{2,1,0:T(8,128)(2,1)}), bf16[8,32,1280]{2,1,0:T(8,128)(2,1)S(1)}, u32[]{:S(2)}, u32[]{:S(2)}) async-start(bf16[8,32,1280]{2,1,0:T(8,128)(2,1)} %bitcast.17), calls=%async_computation | async-start | bytes 1310720 | tf_op jit(solution)/shard_map/all_to_all | solution.py:295
  41.1 9.3 %copy-start.2 = (bf16[128,2560]{1,0:T(8,128)(2,1)S(1)}, bf16[128,2560]{1,0:T(8,128)(2,1)}, u32[]{:S(2)}) copy-start(bf16[128,2560]{1,0:T(8,128)(2,1)} %stream_ref) | copy-start | bytes 1966084
  53.5 5.4 %copy-start.5 = (f32[48,1152]{1,0:T(8,128)}, f32[48,1152]{1,0:T(8,128)S(1)}, u32[]{:S(2)}) copy-start(f32[48,1152]{1,0:T(8,128)S(1)} %get-tuple-element.23) | copy-start | bytes 663556
  53.5 5.2 %collective-permute-start.10 = (bf16[48,1152]{1,0:T(8,128)(2,1)S(1)}, bf16[48,1152]{1,0:T(8,128)(2,1)S(1)}, u32[]{:S(2)}, u32[]{:S(2)}) collective-permute-start(bf16[48,1152]{1,0:T(8,128)(2,1)S(1)} %get-tuple-element.24), channel_id=1, source_target_pairs={{0,4},{1,5},{2,6},{3,7},{4,0},{5,1},{6,2},{7,3},{8,12},{9,13},{10,... | collective-permute-start | bytes 331784 | tf_op jit(solution)/shard_map/ppermute | solution.py:301
  58.9 21.6 %copy-start.3 = (bf16[128,512]{1,0:T(8,128)(2,1)S(1)}, bf16[128,512]{1,0:T(8,128)(2,1)}, u32[]{:S(2)}) copy-start(bf16[128,512]{1,0:T(8,128)(2,1)} %expand_ref.1) | copy-start | bytes 393220
  58.9 21.6 %copy-start.4 = (bf16[512,128]{1,0:T(8,128)(2,1)S(1)}, bf16[512,128]{1,0:T(8,128)(2,1)}, u32[]{:S(2)}) copy-start(bf16[512,128]{1,0:T(8,128)(2,1)} %contract_ref.1) | copy-start | bytes 393220
  59.0 21.6 %copy-start.7 = (f32[128]{0:T(128)S(1)}, f32[128]{0:T(128)}, u32[]{:S(2)}) copy-start(f32[128]{0:T(128)} %param.29) | copy-start | bytes 1540
  67.7 4.6 %collective-permute-start.11 = (bf16[128,128]{1,0:T(8,128)(2,1)S(1)}, bf16[128,128]{1,0:T(8,128)(2,1)S(1)}, u32[]{:S(2)}, u32[]{:S(2)}) collective-permute-start(bf16[128,128]{1,0:T(8,128)(2,1)S(1)} %get-tuple-element.35), channel_id=1, source_target_pairs={{2,0},{18,1},{34,2},{50,3},{66,4},{82,5},{98,6},{114,7},{10,8},{26... | collective-permute-start | bytes 98312 | tf_op jit(solution)/shard_map/ppermute | solution.py:327
  72.3 8.1 %collective-permute-start.12 = (bf16[128,128]{1,0:T(8,128)(2,1)S(1)}, bf16[128,128]{1,0:T(8,128)(2,1)S(1)}, u32[]{:S(2)}, u32[]{:S(2)}) collective-permute-start(bf16[128,128]{1,0:T(8,128)(2,1)S(1)} %collective-permute-done.11), channel_id=1, source_target_pairs={{0,8},{8,0},{16,24},{24,16},{32,40},{40,32},{48,56},{56,48},{64,72... | collective-permute-start | bytes 98312 | tf_op jit(solution)/shard_map/ppermute | solution.py:328
  (2 other events, 1.8 us)

commit v7 on v6

--- a/solution.py
+++ b/solution.py
@@ -52,7 +52,7 @@
 
 def pair_kernel(table_ref, left_ref, right_ref, gain_ref, expand_ref, contract_ref, out_ref):
     rows, columns, channels = table_ref.shape
-    group = 8
+    group = 16
 
     def pair_in(part):
         sums = left_ref[part, :][:, None, :] + right_ref[...][None]
@@ -75,7 +75,7 @@
 
 def pair_stage(table_part, left, right, gain, w_expand, w_contract):
     rows, columns, channels = table_part.shape
-    block = 16
+    block = 32
     left = left.astype(jnp.float32)
     right = right.astype(jnp.float32)
     gain = gain.reshape(1, channels)
@@ -225,7 +225,7 @@
     half_columns = w_single.shape[1] // 2
     own_part = lax.dynamic_slice_in_dim(w_single, core * half_columns, half_columns, 1)
     own_part = (own_part.astype(jnp.float32) * final_gain[:, None]).astype(jnp.bfloat16)
-    own_part, hidden = lax.optimization_barrier((own_part, hidden))
+    own_part, attn_gain = lax.optimization_barrier((own_part, attn_gain))
     quarter = [own_part] + [lax.ppermute(own_part, "col", flip_pairs(8, bit)) for bit in (1, 3, 2)]
     quarter = jnp.concatenate(quarter, 0)
     quarter_other = lax.ppermute(quarter, "row", flip_pairs(16, 1))

time: 103 us -> 103 us (level)
  no operation moved by 1% of the time
where the time goes in v7:
time: 103 us; the launch traced here: 102 us
  starting transfers between devices  32.4 us (31%)
  Pallas kernels  25.1 us (24%)
  matrix products  16.1 us (16%)
  waiting for transfers between devices  14 us (14%)
  blocking collectives  6.87 us (7%)
  local copies, waits for them, and re-layouts  5.23 us (5%)
  other arithmetic  2.05 us (2%)
    pallas_call x1, Pallas kernels, pair_stage(): pl.pallas_call(pair_kernel, grid=(rows // block,), in_specs=[pl.BlockSpec...  21.6 us
    dot_general x1, matrix products, local(): jnp.einsum('ijb,bc->ijc', one_hot, rel_table, preferred_element_type=jnp....  7.63 us
    ppermute x1, starting transfers between devices, local(): other_right = lax.ppermute(own_right, 'row', flip_pairs(16, 1))  7.28 us
    all_to_all x1, blocking collectives, local(): lax.all_to_all(jnp.broadcast_to(both, (4,) + both.shape), 'col', 0, 0, ti...  6.87 us
    ppermute x3, waiting for transfers between devices, local(): lax.ppermute(stacked, 'row', flip_pairs(16, 2 * bit))  5.62 us
    all_to_all x1, starting transfers between devices, local(): lax.all_to_all(attn_part.reshape(8, own_count, half_width), 'col', 0, 0,...  5.33 us
    ppermute x3, starting transfers between devices, local(): lax.ppermute(own_part, 'col', flip_pairs(8, bit))  4.6 us
    ppermute x3, starting transfers between devices, local(): lax.ppermute(stacked, 'row', flip_pairs(16, 2 * bit))  4.41 us
  transfers between devices with their start and end apart: 14, of which 7 were waited for; matrix products, arithmetic and copies ran while one was open for 18% of the time, Pallas kernels for 0%

profile of v7, /device:TPU:1, one launch (start us, length us, event | category | flops | bytes accessed | tf_op | source)
XLA Modules:
  0.0 102.2 jit_solution(1129210018565244915)
XLA Ops:
  0.0 1.3 %multiply_convert_fusion = bf16[320,512]{1,0:T(8,128)(2,1)S(1)} fusion(f32[320]{0:T(512)} %param.23, bf16[320,1024]{1,0:T(8,128)(2,1)} %param.24, s32[]{:T(128)S(6)} %select_n.20), kind=kLoop, calls=%fused_computation.16 | loop fusion | flops 491520 | bytes 656644 | tf_op jit(solution)/shard_map/convert_element_type | solution.py:227
  1.3 3.8 %collective-permute-start.8 = (bf16[320,512]{1,0:T(8,128)(2,1)S(1)}, bf16[320,512]{1,0:T(8,128)(2,1)S(1)}, u32[]{:S(2)}, u32[]{:S(2)}) collective-permute-start(bf16[320,512]{1,0:T(8,128)(2,1)S(1)} %multiply_convert_fusion), channel_id=1, source_target_pairs={{0,2},{1,3},{2,0},{3,1},{4,6},{5,7},{6,4},{7,5},{8,10},{9,11},{10,... | collective-permute-start | bytes 983048 | tf_op jit(solution)/shard_map/ppermute | solution.py:229
  6.1 1.1 %copy-done.1 = bf16[128,2560]{1,0:T(8,128)(2,1)S(1)} copy-done((bf16[128,2560]{1,0:T(8,128)(2,1)S(1)}, bf16[128,2560]{1,0:T(8,128)(2,1)}, u32[]{:S(2)}) %copy-start.1) | copy-done | bytes 655384
  8.2 2.1 %convolution_convert_fusion.1 = bf16[128,320]{0,1:T(8,128)(2,1)S(1)} fusion(bf16[128,2560]{1,0:T(8,128)(2,1)S(1)} %first_norm.1, bf16[2560,320]{0,1:T(8,128)(2,1)} %param.21), kind=kOutput, calls=%fused_computation.11 | convolution fusion | flops 209756160 | bytes 2375680 | tf_op jit(solution)/shard_map/dot_general | solution.py:236
  11.1 3.7 %collective-permute-start.3 = (bf16[128,640]{0,1:T(8,128)(2,1)S(1)}, bf16[128,640]{0,1:T(8,128)(2,1)S(1)}, u32[]{:S(2)}, u32[]{:S(2)}) collective-permute-start(bf16[128,640]{0,1:T(8,128)(2,1)S(1)} %pad_maximum_fusion.1), channel_id=1, source_target_pairs={{0,32},{8,40},{16,48},{24,56},{32,0},{40,8},{48,16},{56,24},{64,96... | collective-permute-start | bytes 491528 | tf_op jit(solution)/shard_map/ppermute | solution.py:240
  16.9 1.1 %collective-permute-done.3 = bf16[128,640]{0,1:T(8,128)(2,1)S(1)} collective-permute-done((bf16[128,640]{0,1:T(8,128)(2,1)S(1)}, bf16[128,640]{0,1:T(8,128)(2,1)S(1)}, u32[]{:S(2)}, u32[]{:S(2)}) %collective-permute-start.3) | collective-permute-done | bytes 163872 | tf_op jit(solution)/shard_map/ppermute | solution.py:240
  18.0 4.5 %collective-permute-done.2 = bf16[128,640]{0,1:T(8,128)(2,1)S(1)} collective-permute-done((bf16[128,640]{0,1:T(8,128)(2,1)S(1)}, bf16[128,640]{0,1:T(8,128)(2,1)S(1)}, u32[]{:S(2)}, u32[]{:S(2)}) %collective-permute-start.2) | collective-permute-done | bytes 163872 | tf_op jit(solution)/shard_map/ppermute | solution.py:240
  22.5 1.2 %collective-permute-start = (bf16[128,320]{0,1:T(8,128)(2,1)S(1)}, bf16[128,320]{0,1:T(8,128)(2,1)S(1)}, u32[]{:S(2)}, u32[]{:S(2)}) collective-permute-start(bf16[128,320]{0,1:T(8,128)(2,1)S(1)} %fusion.17), channel_id=1, source_target_pairs={{0,64},{8,72},{16,80},{24,88},{32,96},{40,104},{48,112},{56,120},{... | collective-permute-start | bytes 245768 | tf_op jit(solution)/shard_map/ppermute | solution.py:245
  23.8 1.2 %collective-permute-start.4 = (bf16[512,640]{0,1:T(8,128)(2,1)S(1)}, bf16[512,640]{0,1:T(8,128)(2,1)S(1)}, u32[]{:S(2)}, u32[]{:S(2)}) collective-permute-start(bf16[512,640]{0,1:T(8,128)(2,1)S(1)} %pad_maximum_fusion), channel_id=1, source_target_pairs={{0,8},{8,0},{16,24},{24,16},{32,40},{40,32},{48,56},{56,48},{64,72... | collective-permute-start | bytes 1966088 | tf_op jit(solution)/shard_map/ppermute | solution.py:254
  25.0 1.1 %collective-permute-done = bf16[128,320]{0,1:T(8,128)(2,1)S(1)} collective-permute-done((bf16[128,320]{0,1:T(8,128)(2,1)S(1)}, bf16[128,320]{0,1:T(8,128)(2,1)S(1)}, u32[]{:S(2)}, u32[]{:S(2)}) %collective-permute-start) | collective-permute-done | bytes 81952 | tf_op jit(solution)/shard_map/ppermute | solution.py:245
  30.1 1.3 %collective-permute-start.5 = (bf16[128,384]{0,1:T(8,128)(2,1)S(1)}, bf16[128,384]{0,1:T(8,128)(2,1)S(1)}, u32[]{:S(2)}, u32[]{:S(2)}) collective-permute-start(bf16[128,384]{0,1:T(8,128)(2,1)S(1)} %fusion.26), channel_id=1, source_target_pairs={{0,64},{8,72},{16,80},{24,88},{32,96},{40,104},{48,112},{56,120},{... | collective-permute-start | bytes 294920 | tf_op jit(solution)/shard_map/ppermute | solution.py:278
  32.1 2.1 %collective-permute-start.9 = (bf16[1280,512]{1,0:T(8,128)(2,1)}, bf16[1280,512]{1,0:T(8,128)(2,1)}, u32[]{:S(2)}, u32[]{:S(2)}) collective-permute-start(bf16[1280,512]{1,0:T(8,128)(2,1)} %constant_dynamic-update-slice_fusion.5.own_ref), channel_id=1, source_target_pairs={{0,8},{8,0},{16,24},{24,16},{32,40},{40,32},{48,56},{56,48},{64,72... | collective-permute-start | bytes 3932168 | tf_op jit(solution)/shard_map/ppermute | solution.py:231
  34.3 1.4 %convolution_convert_fusion = bf16[128,2,1280]{2,0,1:T(8,128)(2,1)} fusion(bf16[128,320,1]{0,1,2:T(8,128)(2,1)S(1)} %bitcast.80, bf16[40,2,8,1280]{3,2,1,0:T(8,128)(2,1)S(1)} %bitcast.75), kind=kOutput, calls=%fused_computation.7 | convolution fusion | flops 210042880 | bytes 2375680 | tf_op jit(solution)/shard_map/rk,kxn->xrn/dot_general | solution.py:286
  35.7 5.3 %all-to-all-start = ((bf16[8,32,1280]{2,1,0:T(8,128)(2,1)}), bf16[8,32,1280]{2,1,0:T(8,128)(2,1)S(1)}, u32[]{:S(2)}, u32[]{:S(2)}) async-start(bf16[8,32,1280]{2,1,0:T(8,128)(2,1)} %bitcast.17), calls=%async_computation | async-start | bytes 1310720 | tf_op jit(solution)/shard_map/all_to_all | solution.py:295
  41.1 7.6 %fusion.1.table_ref = bf16[128,256,128]{2,1,0:T(8,128)(2,1)} fusion(s32[128,256]{1,0:T(8,128)S(1)} %copy-done.11, bf16[65,128]{1,0:T(8,128)(2,1)} %param.28), kind=kOutput, calls=%fused_computation.2 | convolution fusion | flops 551583744 | bytes 8536320 | tf_op jit(solution)/shard_map/ijb,bc->ijc/dot_general | solution.py:249
  48.8 1.7 %all-to-all-done.parts_ref = bf16[8,32,1280]{2,1,0:T(8,128)(2,1)S(1)} async-done(((bf16[8,32,1280]{2,1,0:T(8,128)(2,1)}), bf16[8,32,1280]{2,1,0:T(8,128)(2,1)S(1)}, u32[]{:S(2)}, u32[]{:S(2)}) %all-to-all-start) | async-done | bytes 655392 | tf_op jit(solution)/shard_map/all_to_all | solution.py:295
  50.4 3.1 %half_sums.1 = (f32[48,1152]{1,0:T(8,128)S(1)}, bf16[48,1152]{1,0:T(8,128)(2,1)S(1)}) custom-call(s32[3]{0:T(128)S(1)} %pad_add_fusion.place_ref, bf16[8,32,1280]{2,1,0:T(8,128)(2,1)S(1)} %all-to-all-done.parts_ref, bf16[128,2560]{1,0:T(8,128)(2,1)S(1)} %copy-done.2, bf16[1280,512]{1,0:T(8,128)(2,1)} %constant_dynamic-update-slice_fusion.5.own_ref, ...), custom_call_target="tpu_custom_call" | custom-call | tf_op jit(solution)/shard_map/half_sums/pallas_call | solution.py:177
  53.5 1.4 %collective-permute-start.10 = (bf16[48,1152]{1,0:T(8,128)(2,1)S(1)}, bf16[48,1152]{1,0:T(8,128)(2,1)S(1)}, u32[]{:S(2)}, u32[]{:S(2)}) collective-permute-start(bf16[48,1152]{1,0:T(8,128)(2,1)S(1)} %get-tuple-element.24), channel_id=1, source_target_pairs={{0,4},{1,5},{2,6},{3,7},{4,0},{5,1},{6,2},{7,3},{8,12},{9,13},{10,... | collective-permute-start | bytes 331784 | tf_op jit(solution)/shard_map/ppermute | solution.py:301
  54.9 3.8 %collective-permute-done.10 = bf16[48,1152]{1,0:T(8,128)(2,1)S(1)} collective-permute-done((bf16[48,1152]{1,0:T(8,128)(2,1)S(1)}, bf16[48,1152]{1,0:T(8,128)(2,1)S(1)}, u32[]{:S(2)}, u32[]{:S(2)}) %collective-permute-start.10) | collective-permute-done | bytes 110624 | tf_op jit(solution)/shard_map/ppermute | solution.py:301
  59.0 1.8 %fusion.7 = bf16[32,256]{1,0:T(8,128)(2,1)S(1)} fusion(bf16[1024,1024]{1,0:T(8,128)(2,1)S(1)} %copy-done, bf16[1024,128]{1,0:T(8,128)(2,1)} %param.27, bf16[1024,128]{1,0:T(8,128)(2,1)} %param.26, f32[48,1152]{1,0:T(8,128)S(1)} %convert_element_type.78, f32[48,1152]{1,0:T(8,128)} %copy-done.5, f32[32]{0:T(128)S(1)} %get-tuple-element.26, ...), kind=kOutput, calls=%fused_computation.14 | convolution fusion | flops 85172224 | bytes 2905088 | tf_op jit(solution)/shard_map/dot_general | solution.py:315
  60.8 6.9 %all_to_all.10 = bf16[4,32,256]{2,1,0:T(8,128)(2,1)S(1)} all-to-all(bf16[4,32,256]{2,1,0:T(8,128)(2,1)S(1)} %broadcast_in_dim.2), channel_id=1, replica_groups={{0,1,2,3},{4,5,6,7},{8,9,10,11},{12,13,14,15},{16,17,18,19},{20,21,22,2..., dimensions={0} | all-to-all | bytes 131072 | tf_op jit(solution)/shard_map/all_to_all | solution.py:316
  67.7 3.6 %collective-permute-start.11 = (bf16[128,128]{1,0:T(8,128)(2,1)S(1)}, bf16[128,128]{1,0:T(8,128)(2,1)S(1)}, u32[]{:S(2)}, u32[]{:S(2)}) collective-permute-start(bf16[128,128]{1,0:T(8,128)(2,1)S(1)} %get-tuple-element.35), channel_id=1, source_target_pairs={{2,0},{18,1},{34,2},{50,3},{66,4},{82,5},{98,6},{114,7},{10,8},{26... | collective-permute-start | bytes 98312 | tf_op jit(solution)/shard_map/ppermute | solution.py:327
  72.3 7.3 %collective-permute-start.12 = (bf16[128,128]{1,0:T(8,128)(2,1)S(1)}, bf16[128,128]{1,0:T(8,128)(2,1)S(1)}, u32[]{:S(2)}, u32[]{:S(2)}) collective-permute-start(bf16[128,128]{1,0:T(8,128)(2,1)S(1)} %collective-permute-done.11), channel_id=1, source_target_pairs={{0,8},{8,0},{16,24},{24,16},{32,40},{40,32},{48,56},{56,48},{64,72... | collective-permute-start | bytes 98312 | tf_op jit(solution)/shard_map/ppermute | solution.py:328
  80.6 21.6 %pair.1 = bf16[128,256,128]{2,1,0:T(8,128)(2,1)} custom-call(bf16[128,256,128]{2,1,0:T(8,128)(2,1)} %fusion.1.table_ref, f32[128,128]{1,0:T(8,128)S(1)} %get-tuple-element.36.left_ref, f32[256,128]{1,0:T(8,128)S(1)} %maximum_convert_fusion.right_ref, f32[1,128]{1,0:T(1,128)S(1)} %bitcast.72, bf16[128,512]{1,0:T(8,128)(2,1)S(1)} %copy-done.3, ...), custom_call_target="tpu_custom_call" | custom-call | tf_op jit(solution)/shard_map/pair/pallas_call | solution.py:83
  (79 shorter events, 11.9 us)
Async XLA Ops:
  0.0 58.9 %copy-start = (bf16[1024,1024]{1,0:T(8,128)(2,1)S(1)}, bf16[1024,1024]{1,0:T(8,128)(2,1)}, u32[]{:S(2)}) copy-start(bf16[1024,1024]{1,0:T(8,128)(2,1)} %param.25) | copy-start | bytes 6291460
  1.3 30.1 %collective-permute-start.8 = (bf16[320,512]{1,0:T(8,128)(2,1)S(1)}, bf16[320,512]{1,0:T(8,128)(2,1)S(1)}, u32[]{:S(2)}, u32[]{:S(2)}) collective-permute-start(bf16[320,512]{1,0:T(8,128)(2,1)S(1)} %multiply_convert_fusion), channel_id=1, source_target_pairs={{0,2},{1,3},{2,0},{3,1},{4,6},{5,7},{6,4},{7,5},{8,10},{9,11},{10,... | collective-permute-start | bytes 983048 | tf_op jit(solution)/shard_map/ppermute | solution.py:229
  5.1 22.0 %collective-permute-start.7 = (bf16[320,512]{1,0:T(8,128)(2,1)S(1)}, bf16[320,512]{1,0:T(8,128)(2,1)S(1)}, u32[]{:S(2)}, u32[]{:S(2)}) collective-permute-start(bf16[320,512]{1,0:T(8,128)(2,1)S(1)} %multiply_convert_fusion), channel_id=1, source_target_pairs={{0,3},{1,2},{2,1},{3,0},{4,7},{5,6},{6,5},{7,4},{8,11},{9,10},{10,... | collective-permute-start | bytes 983048 | tf_op jit(solution)/shard_map/ppermute | solution.py:229
  7.8 2.5 %copy-start.8 = (bf16[2560,320]{0,1:T(8,128)(2,1)S(1)}, bf16[2560,320]{0,1:T(8,128)(2,1)}, u32[]{:S(2)}) copy-start(bf16[2560,320]{0,1:T(8,128)(2,1)} %param.20) | copy-start | bytes 4915204
  10.4 5.1 %copy-start.9 = (bf16[2560,320]{0,1:T(8,128)(2,1)S(1)}, bf16[2560,320]{0,1:T(8,128)(2,1)}, u32[]{:S(2)}) copy-start(bf16[2560,320]{0,1:T(8,128)(2,1)} %param.19) | copy-start | bytes 4915204
  11.1 7.0 %collective-permute-start.3 = (bf16[128,640]{0,1:T(8,128)(2,1)S(1)}, bf16[128,640]{0,1:T(8,128)(2,1)S(1)}, u32[]{:S(2)}, u32[]{:S(2)}) collective-permute-start(bf16[128,640]{0,1:T(8,128)(2,1)S(1)} %pad_maximum_fusion.1), channel_id=1, source_target_pairs={{0,32},{8,40},{16,48},{24,56},{32,0},{40,8},{48,16},{56,24},{64,96... | collective-permute-start | bytes 491528 | tf_op jit(solution)/shard_map/ppermute | solution.py:240
  14.7 7.8 %collective-permute-start.2 = (bf16[128,640]{0,1:T(8,128)(2,1)S(1)}, bf16[128,640]{0,1:T(8,128)(2,1)S(1)}, u32[]{:S(2)}, u32[]{:S(2)}) collective-permute-start(bf16[128,640]{0,1:T(8,128)(2,1)S(1)} %pad_maximum_fusion.1), channel_id=1, source_target_pairs={{0,48},{8,56},{16,32},{24,40},{32,16},{40,24},{48,0},{56,8},{64,11... | collective-permute-start | bytes 491528 | tf_op jit(solution)/shard_map/ppermute | solution.py:240
  15.2 8.6 %collective-permute-start.1 = (bf16[128,640]{0,1:T(8,128)(2,1)S(1)}, bf16[128,640]{0,1:T(8,128)(2,1)S(1)}, u32[]{:S(2)}, u32[]{:S(2)}) collective-permute-start(bf16[128,640]{0,1:T(8,128)(2,1)S(1)} %pad_maximum_fusion.1), channel_id=1, source_target_pairs={{0,16},{8,24},{16,0},{24,8},{32,48},{40,56},{48,32},{56,40},{64,80... | collective-permute-start | bytes 491528 | tf_op jit(solution)/shard_map/ppermute | solution.py:240
  18.0 8.3 %collective-permute-start.6 = (bf16[320,512]{1,0:T(8,128)(2,1)S(1)}, bf16[320,512]{1,0:T(8,128)(2,1)S(1)}, u32[]{:S(2)}, u32[]{:S(2)}) collective-permute-start(bf16[320,512]{1,0:T(8,128)(2,1)S(1)} %multiply_convert_fusion), channel_id=1, source_target_pairs={{0,1},{1,0},{2,3},{3,2},{4,5},{5,4},{6,7},{7,6},{8,9},{9,8},{10,11... | collective-permute-start | bytes 983048 | tf_op jit(solution)/shard_map/ppermute | solution.py:229
  22.5 3.6 %collective-permute-start = (bf16[128,320]{0,1:T(8,128)(2,1)S(1)}, bf16[128,320]{0,1:T(8,128)(2,1)S(1)}, u32[]{:S(2)}, u32[]{:S(2)}) collective-permute-start(bf16[128,320]{0,1:T(8,128)(2,1)S(1)} %fusion.17), channel_id=1, source_target_pairs={{0,64},{8,72},{16,80},{24,88},{32,96},{40,104},{48,112},{56,120},{... | collective-permute-start | bytes 245768 | tf_op jit(solution)/shard_map/ppermute | solution.py:245
  23.8 4.0 %collective-permute-start.4 = (bf16[512,640]{0,1:T(8,128)(2,1)S(1)}, bf16[512,640]{0,1:T(8,128)(2,1)S(1)}, u32[]{:S(2)}, u32[]{:S(2)}) collective-permute-start(bf16[512,640]{0,1:T(8,128)(2,1)S(1)} %pad_maximum_fusion), channel_id=1, source_target_pairs={{0,8},{8,0},{16,24},{24,16},{32,40},{40,32},{48,56},{56,48},{64,72... | collective-permute-start | bytes 1966088 | tf_op jit(solution)/shard_map/ppermute | solution.py:254
  30.0 4.3 %copy-start.10 = (bf16[320,2560]{1,0:T(8,128)(2,1)S(1)}, bf16[320,2560]{1,0:T(8,128)(2,1)}, u32[]{:S(2)}) copy-start(bf16[320,2560]{1,0:T(8,128)(2,1)} %param.22) | copy-start | bytes 4915204
  30.1 4.1 %collective-permute-start.5 = (bf16[128,384]{0,1:T(8,128)(2,1)S(1)}, bf16[128,384]{0,1:T(8,128)(2,1)S(1)}, u32[]{:S(2)}, u32[]{:S(2)}) collective-permute-start(bf16[128,384]{0,1:T(8,128)(2,1)S(1)} %fusion.26), channel_id=1, source_target_pairs={{0,64},{8,72},{16,80},{24,88},{32,96},{40,104},{48,112},{56,120},{... | collective-permute-start | bytes 294920 | tf_op jit(solution)/shard_map/ppermute | solution.py:278
  32.1 18.3 %collective-permute-start.9 = (bf16[1280,512]{1,0:T(8,128)(2,1)}, bf16[1280,512]{1,0:T(8,128)(2,1)}, u32[]{:S(2)}, u32[]{:S(2)}) collective-permute-start(bf16[1280,512]{1,0:T(8,128)(2,1)} %constant_dynamic-update-slice_fusion.5.own_ref), channel_id=1, source_target_pairs={{0,8},{8,0},{16,24},{24,16},{32,40},{40,32},{48,56},{56,48},{64,72... | collective-permute-start | bytes 3932168 | tf_op jit(solution)/shard_map/ppermute | solution.py:231
  34.3 6.8 %copy-start.11 = (s32[128,256]{1,0:T(8,128)S(1)}, s32[128,256]{1,0:T(8,128)}, u32[]{:S(2)}) copy-start(s32[128,256]{1,0:T(8,128)} %param.17) | copy-start | bytes 393220
  35.7 14.7 %all-to-all-start = ((bf16[8,32,1280]{2,1,0:T(8,128)(2,1)}), bf16[8,32,1280]{2,1,0:T(8,128)(2,1)S(1)}, u32[]{:S(2)}, u32[]{:S(2)}) async-start(bf16[8,32,1280]{2,1,0:T(8,128)(2,1)} %bitcast.17), calls=%async_computation | async-start | bytes 1310720 | tf_op jit(solution)/shard_map/all_to_all | solution.py:295
  41.1 9.3 %copy-start.2 = (bf16[128,2560]{1,0:T(8,128)(2,1)S(1)}, bf16[128,2560]{1,0:T(8,128)(2,1)}, u32[]{:S(2)}) copy-start(bf16[128,2560]{1,0:T(8,128)(2,1)} %stream_ref.1) | copy-start | bytes 1966084
  53.5 5.4 %copy-start.5 = (f32[48,1152]{1,0:T(8,128)}, f32[48,1152]{1,0:T(8,128)S(1)}, u32[]{:S(2)}) copy-start(f32[48,1152]{1,0:T(8,128)S(1)} %get-tuple-element.23) | copy-start | bytes 663556
  53.5 5.2 %collective-permute-start.10 = (bf16[48,1152]{1,0:T(8,128)(2,1)S(1)}, bf16[48,1152]{1,0:T(8,128)(2,1)S(1)}, u32[]{:S(2)}, u32[]{:S(2)}) collective-permute-start(bf16[48,1152]{1,0:T(8,128)(2,1)S(1)} %get-tuple-element.24), channel_id=1, source_target_pairs={{0,4},{1,5},{2,6},{3,7},{4,0},{5,1},{6,2},{7,3},{8,12},{9,13},{10,... | collective-permute-start | bytes 331784 | tf_op jit(solution)/shard_map/ppermute | solution.py:301
  58.9 21.6 %copy-start.3 = (bf16[128,512]{1,0:T(8,128)(2,1)S(1)}, bf16[128,512]{1,0:T(8,128)(2,1)}, u32[]{:S(2)}) copy-start(bf16[128,512]{1,0:T(8,128)(2,1)} %expand_ref.1) | copy-start | bytes 393220
  58.9 21.6 %copy-start.4 = (bf16[512,128]{1,0:T(8,128)(2,1)S(1)}, bf16[512,128]{1,0:T(8,128)(2,1)}, u32[]{:S(2)}) copy-start(bf16[512,128]{1,0:T(8,128)(2,1)} %contract_ref.1) | copy-start | bytes 393220
  59.0 21.6 %copy-start.7 = (f32[128]{0:T(128)S(1)}, f32[128]{0:T(128)}, u32[]{:S(2)}) copy-start(f32[128]{0:T(128)} %param.29) | copy-start | bytes 1540
  67.7 4.6 %collective-permute-start.11 = (bf16[128,128]{1,0:T(8,128)(2,1)S(1)}, bf16[128,128]{1,0:T(8,128)(2,1)S(1)}, u32[]{:S(2)}, u32[]{:S(2)}) collective-permute-start(bf16[128,128]{1,0:T(8,128)(2,1)S(1)} %get-tuple-element.35), channel_id=1, source_target_pairs={{2,0},{18,1},{34,2},{50,3},{66,4},{82,5},{98,6},{114,7},{10,8},{26... | collective-permute-start | bytes 98312 | tf_op jit(solution)/shard_map/ppermute | solution.py:327
  72.3 8.1 %collective-permute-start.12 = (bf16[128,128]{1,0:T(8,128)(2,1)S(1)}, bf16[128,128]{1,0:T(8,128)(2,1)S(1)}, u32[]{:S(2)}, u32[]{:S(2)}) collective-permute-start(bf16[128,128]{1,0:T(8,128)(2,1)S(1)} %collective-permute-done.11), channel_id=1, source_target_pairs={{0,8},{8,0},{16,24},{24,16},{32,40},{40,32},{48,56},{56,48},{64,72... | collective-permute-start | bytes 98312 | tf_op jit(solution)/shard_map/ppermute | solution.py:328
  (2 other events, 1.8 us)
